TPU v7x, 32 devices: a whole 2x2x4 slice. The times are simulated.
32 devices in a mesh: dp: 4 (over x, core), ctx: 8 (over z, y).
Axes of the slice: x: 2, y: 2, z: 4, core: 2. Of those that a mesh axis runs over, the one named last changes fastest.
Arguments:
- feats: bfloat16 [4, 3, 1024, 4096], P('dp', None, 'ctx'), may hold values from -6 to 6
- grad_y: bfloat16 [4, 1024, 4096], P('dp', 'ctx'), may hold values from -6 to 6
- short_w: float32 [7, 3, 4096], replicated, may hold values from -2 to 2
- long_h: float32 [1024, 4096], P(None, 'ctx'), may hold values from -2 to 2
- block_order: int32 [16], replicated, may hold values from 0 to 15, as said below
Outputs:
- mixed: bfloat16 [4, 1024, 4096], P('dp', 'ctx')
- feats_grad: bfloat16 [4, 3, 1024, 4096], P('dp', None, 'ctx')
- short_grad: float32 [7, 3, 4096], P(None, None, 'ctx')
- filter_grad: float32 [1024, 4096], P(None, 'ctx')
Inputs may be any that keep to these rules, and one draw needn't show every extreme that they name: Stored blocks 2 i and 2 i + 1 (those of index i of ctx) hold sequence blocks i and 15 - i, in an order drawn for each i; block_order is a permutation.
All inputs are finite; a program needn't handle non-finite values.
Results may differ from a plain program's by a relative error of at most 0.0085.
Values may be sent and summed in bfloat16 or wider, within the bound.
No kernel may reach another device: no remote copies, remote signals or barrier semaphores. Data moves between devices by JAX's collectives and lax.ppermute only.
A program may use at most 192 MiB of HBM per device.

v0:
```python
import jax
import jax.numpy as jnp
from jax import lax
from jax.sharding import PartitionSpec as P

HIGH = lax.Precision.HIGHEST


def dft_tables(frames):
    half_rows = frames // 2
    total_len = frames * 128
    freq_rows = jnp.arange(frames, dtype=jnp.int32)[:, None]
    time_rows = jnp.arange(half_rows, dtype=jnp.int32)[None, :]
    lane_ids = jnp.arange(128, dtype=jnp.int32)
    angle_outer = 2.0 * jnp.pi / frames * (freq_rows * time_rows % frames).astype(jnp.float32)
    angle_twist = (
        2.0 * jnp.pi / total_len * (freq_rows * lane_ids[None, :] % total_len).astype(jnp.float32)
    )
    angle_inner = (
        2.0 * jnp.pi / 128.0 * (lane_ids[:, None] * lane_ids[None, :] % 128).astype(jnp.float32)
    )
    outer_tab = (jnp.cos(angle_outer), -jnp.sin(angle_outer))
    twist_tab = (jnp.cos(angle_twist)[:, :, None], -jnp.sin(angle_twist)[:, :, None])
    inner_tab = (jnp.cos(angle_inner), -jnp.sin(angle_inner))
    return (outer_tab, twist_tab, inner_tab)


def along_lanes(left, table):
    return jnp.einsum(
        "cbh,bd->cdh", left, table, precision=HIGH, preferred_element_type=jnp.float32
    )


def against_lanes(left, table):
    return jnp.einsum(
        "cdh,bd->cbh", left, table, precision=HIGH, preferred_element_type=jnp.float32
    )


def spectrum(signal, tables):
    outer_tab, twist_tab, inner_tab = tables
    frames, half_rows = outer_tab[0].shape
    channels = signal.shape[1]
    folded = signal.reshape(half_rows, 128 * channels)
    part_re = jnp.dot(
        outer_tab[0], folded, precision=HIGH, preferred_element_type=jnp.float32
    ).reshape(frames, 128, channels)
    part_im = jnp.dot(
        outer_tab[1], folded, precision=HIGH, preferred_element_type=jnp.float32
    ).reshape(frames, 128, channels)
    turned_re = part_re * twist_tab[0] - part_im * twist_tab[1]
    turned_im = part_re * twist_tab[1] + part_im * twist_tab[0]
    out_re = along_lanes(turned_re, inner_tab[0]) - along_lanes(turned_im, inner_tab[1])
    out_im = along_lanes(turned_re, inner_tab[1]) + along_lanes(turned_im, inner_tab[0])
    return (out_re, out_im)


def inverse(spec_re, spec_im, tables):
    outer_tab, twist_tab, inner_tab = tables
    frames, half_rows = outer_tab[0].shape
    channels = spec_re.shape[2]
    rows_re = against_lanes(spec_re, inner_tab[0]) + against_lanes(spec_im, inner_tab[1])
    rows_im = against_lanes(spec_im, inner_tab[0]) - against_lanes(spec_re, inner_tab[1])
    turned_re = rows_re * twist_tab[0] + rows_im * twist_tab[1]
    turned_im = rows_im * twist_tab[0] - rows_re * twist_tab[1]
    folded = jnp.dot(
        outer_tab[0].T,
        turned_re.reshape(frames, 128 * channels),
        precision=HIGH,
        preferred_element_type=jnp.float32,
    )
    folded = folded + jnp.dot(
        outer_tab[1].T,
        turned_im.reshape(frames, 128 * channels),
        precision=HIGH,
        preferred_element_type=jnp.float32,
    )
    return (folded / (frames * 128.0)).reshape(half_rows * 128, channels)


def product(left_re, left_im, right_re, right_im):
    return (left_re * right_re - left_im * right_im, left_re * right_im + left_im * right_re)


def product_conj(left_re, left_im, right_re, right_im):
    return (left_re * right_re + left_im * right_im, left_im * right_re - left_re * right_im)


def reorder(values, table, block_count, axis):
    shape_full = values.shape
    row_total = shape_full[axis]
    grouped = values.reshape(
        shape_full[:axis] + (block_count, row_total // block_count) + shape_full[axis + 1 :]
    )
    return jnp.take(grouped, table, axis=axis).reshape(shape_full)


def featurize(padded, weights, rows):
    tap_count = weights.shape[0]
    total = jnp.zeros((padded.shape[0], rows, padded.shape[2]), jnp.float32)
    for offset in range(tap_count):
        begin = tap_count - 1 - offset
        total = total + weights[offset] * padded[:, begin : begin + rows].astype(jnp.float32)
    return total


def spread_back(extended, weights, rows):
    tap_count = weights.shape[0]
    total = jnp.zeros((extended.shape[0], rows, extended.shape[2]), jnp.float32)
    for offset in range(tap_count):
        total = total + weights[offset] * extended[:, offset : offset + rows]
    return total


def weight_terms(grads, padded, rows, tap_count):
    terms = []
    for offset in range(tap_count):
        begin = tap_count - 1 - offset
        terms.append(jnp.sum(grads * padded[:, begin : begin + rows].astype(jnp.float32), axis=1))
    return jnp.stack(terms, 0)


def on_device(feats, grad_y, short_w, long_h, block_order):
    block_count = block_order.shape[0]
    ctx_count = lax.axis_size("ctx")
    my_index = lax.axis_index("ctx")
    local_rows = feats.shape[2]
    model_width = feats.shape[3]
    channels = model_width // ctx_count
    seq_rows = local_rows * ctx_count
    tap_count = short_w.shape[0]
    rim_rows = tap_count - 1
    numbers = jnp.arange(block_count, dtype=jnp.int32)
    source = jnp.sum(
        numbers[None, :] * (block_order[None, :] == numbers[:, None]).astype(jnp.int32), axis=1
    )
    tables = dft_tables(2 * seq_rows // 128)
    weights_here = lax.dynamic_slice_in_dim(short_w, my_index * channels, channels, 2)[
        :, :, None, :
    ]
    cotangent = grad_y.reshape(1, 1, local_rows, model_width)
    raw_all, cot_all = (
        lax.all_to_all(feats, "ctx", split_axis=3, concat_axis=2, tiled=True),
        lax.all_to_all(cotangent, "ctx", split_axis=3, concat_axis=2, tiled=True),
    )
    raw_seq = reorder(raw_all[0], source, block_count, 1)
    padded_x = jnp.concatenate([jnp.zeros((3, rim_rows, channels), jnp.bfloat16), raw_seq], 1)
    featured = featurize(padded_x, weights_here, seq_rows).astype(jnp.bfloat16)
    query = featured[0]
    key_part = featured[1].astype(jnp.float32)
    value_part = featured[2].astype(jnp.float32)
    gated = (key_part * value_part).astype(jnp.bfloat16)
    grad_seq = reorder(cot_all[0], source, block_count, 1)[0].astype(jnp.float32)
    quarter = channels // lax.axis_size("dp")
    mine = lax.dynamic_slice_in_dim(long_h, lax.axis_index("dp") * quarter, quarter, 1)
    piece_re, piece_im = spectrum(mine, tables)
    filter_re, filter_im = (
        lax.all_gather(piece_re, "dp", axis=2, tiled=True),
        lax.all_gather(piece_im, "dp", axis=2, tiled=True),
    )
    gated_re, gated_im = spectrum(gated.astype(jnp.float32), tables)
    conv_re, conv_im = product(gated_re, gated_im, filter_re, filter_im)
    conv_out = inverse(conv_re, conv_im, tables)
    query_f = query.astype(jnp.float32)
    mixed_seq = (query_f * conv_out).astype(jnp.bfloat16)
    grad_query = (grad_seq * conv_out).astype(jnp.bfloat16)
    grad_conv = grad_seq * query_f
    back_re, back_im = spectrum(grad_conv, tables)
    through_re, through_im = product_conj(back_re, back_im, filter_re, filter_im)
    grad_gated = inverse(through_re, through_im, tables).astype(jnp.bfloat16)
    cross_re, cross_im = product_conj(back_re, back_im, gated_re, gated_im)
    filter_part = inverse(cross_re, cross_im, tables)
    mixed_back = reorder(mixed_seq, block_order, block_count, 0)[None, None]
    gate_grad = grad_gated.astype(jnp.float32)
    grad_feat = jnp.stack(
        [grad_query.astype(jnp.float32), gate_grad * value_part, gate_grad * key_part], 0
    )
    extended = jnp.concatenate([grad_feat, jnp.zeros((3, rim_rows, channels), jnp.float32)], 1)
    grad_x = spread_back(extended, weights_here, seq_rows).astype(jnp.bfloat16)
    short_part = weight_terms(grad_feat, padded_x, seq_rows, tap_count)
    grads_back = reorder(grad_x, block_order, block_count, 1)[None]
    mixed_out, grad_out = (
        lax.all_to_all(mixed_back, "ctx", split_axis=2, concat_axis=3, tiled=True),
        lax.all_to_all(grads_back, "ctx", split_axis=2, concat_axis=3, tiled=True),
    )
    filter_sum, short_sum = lax.psum((filter_part, short_part), "dp")
    return (mixed_out.reshape(1, local_rows, model_width), grad_out, short_sum, filter_sum)


def solution(mesh):
    placed = (P("dp", None, "ctx", None), P("dp", "ctx", None), P(), P(None, "ctx"), P())
    return jax.shard_map(
        on_device,
        mesh=mesh,
        in_specs=placed,
        out_specs=(
            P("dp", "ctx", None),
            P("dp", None, "ctx", None),
            P(None, None, "ctx"),
            P(None, "ctx"),
        ),
        check_vma=False,
    )
```

profile of v0, /device:TPU:0, one launch (start us, length us, event | category | flops | bytes accessed | tf_op | source)
XLA Modules:
  0.0 635.1 jit_solution(8026584114502599254)
XLA Ops:
  20.0 23.4 %reduce.1 = bf16[4096,128]{1,0:T(8,128)(2,1)S(1)} reduce(bf16[4096,1,1,128]{3,2,1,0:T(2,128)(2,1)} %bitcast.349, bf16[]{:T(256)} %broadcast.374), dimensions={1,2}, to_apply=%bitcast.287.reduce_sub_computation | reduce | bytes 2097154
  44.5 7.3 %all-to-all-start.2 = ((bf16[8,2,32768]{2,1,0:T(2,128)(2,1)}), bf16[8,2,32768]{2,1,0:T(2,128)(2,1)S(1)}, u32[]{:S(2)}, u32[]{:S(2)}) async-start(bf16[8,2,32768]{2,1,0:T(2,128)(2,1)} %reshape.391), calls=%async_computation.2 | async-start | bytes 2097152 | tf_op jit(solution)/shard_map/all_to_all | solution.py:144
  51.8 7.2 %copy.263 = bf16[1,3,128,4096]{2,1,0,3:T(4,128)(2,1)} copy(bf16[1,3,128,4096]{3,2,1,0:T(8,128)(2,1)} %param.7) | data formatting | bytes 6291456 | tf_op args[0]
  59.0 18.6 %all-to-all-done.2 = bf16[8,2,32768]{2,1,0:T(2,128)(2,1)S(1)} async-done(((bf16[8,2,32768]{2,1,0:T(2,128)(2,1)}), bf16[8,2,32768]{2,1,0:T(2,128)(2,1)S(1)}, u32[]{:S(2)}, u32[]{:S(2)}) %all-to-all-start.2) | async-done | bytes 1048608 | tf_op jit(solution)/shard_map/all_to_all | solution.py:144
  92.6 82.0 %all-to-all-done = bf16[1,3,128,4096]{2,1,0,3:T(4,128)(2,1)} async-done(((bf16[1,3,128,4096]{2,1,0,3:T(4,128)(2,1)}), bf16[1,3,128,4096]{2,1,0,3:T(4,128)(2,1)}, u32[]{:S(2)}, u32[]{:S(2)}) %all-to-all-start) | async-done | bytes 3145760 | tf_op jit(solution)/shard_map/all_to_all | solution.py:143
  192.1 5.7 fusion.11
  223.2 22.7 %multiply_subtract_fusion = (f32[16,128,512]{2,0,1:T(8,128)S(1)}, f32[16,128,512]{2,0,1:T(8,128)S(1)}, f32[16,128,512]{2,0,1:T(8,128)S(1)}, f32[16,128,512]{2,0,1:T(8,128)S(1)}) fusion(f32[16,128,512]{2,0,1:T(8,128)} %fusion.151, f32[16,128]{0,1:T(8,128)S(1)} %get-tuple-element.81, f32[16,128]{0,1:T(8,128)S(1)} %get-tuple-element.82, ...), kind=kOutput, calls=%fused_computation.90 | convolution fusion | flops 113248128 | bytes 31473664 | tf_op jit(solution)/shard_map/dot_general | solution.py:48
  245.9 6.1 fusion.47
  252.0 6.3 fusion.45
  258.4 6.1 fusion.39
  264.5 7.4 %fusion.37 = f32[128,16,512]{2,0,1:T(8,128)} fusion(f32[16,128,512]{2,0,1:T(8,128)S(1)} %get-tuple-element.46), kind=kOutput, calls=%fused_computation.93 | convolution fusion | flops 1610842112 | bytes 8388608 | tf_op jit(solution)/shard_map/cbh,bd->cdh/dot_general | solution.py:29
  271.9 7.7 %fusion.53 = f32[128,16,512]{2,0,1:T(8,128)} fusion(f32[128,16,512]{2,0,1:T(8,128)S(1)} %fusion.47, f32[16,128,512]{2,0,1:T(8,128)S(1)} %get-tuple-element.70), kind=kOutput, calls=%fused_computation.114 | convolution fusion | flops 1611890688 | bytes 12582912 | tf_op jit(solution)/shard_map/cbh,bd->cdh/dot_general | solution.py:29
  279.6 7.4 %fusion.56 = f32[128,16,512]{2,0,1:T(8,128)} fusion(f32[128,16,512]{2,0,1:T(8,128)S(1)} %fusion.45, f32[16,128,512]{2,0,1:T(8,128)S(1)} %get-tuple-element.70), kind=kOutput, calls=%fused_computation.115 | convolution fusion | flops 1611907072 | bytes 12582912 | tf_op jit(solution)/shard_map/cbh,bd->cdh/dot_general | solution.py:29
  287.0 7.4 %fusion.59 = f32[128,16,512]{2,0,1:T(8,128)} fusion(f32[128,16,512]{2,0,1:T(8,128)S(1)} %fusion.39, f32[16,128,512]{2,0,1:T(8,128)S(1)} %get-tuple-element.45), kind=kOutput, calls=%fused_computation.116 | convolution fusion | flops 1611890688 | bytes 12582912 | tf_op jit(solution)/shard_map/cbh,bd->cdh/dot_general | solution.py:29
  294.4 19.7 %fusion.29 = (f32[16,128,512]{2,1,0:T(8,128)}, f32[16,128,512]{2,1,0:T(8,128)}, f32[16,128,512]{2,1,0:T(8,128)}, f32[16,128,512]{2,1,0:T(8,128)}, f32[16,128,512]{2,1,0:T(8,128)}, /*index=5*/f32[16,128,512]{2,1,0:T(8,128)}) fusion(f32[128,16,512]{2,0,1:T(8,128)} %fusion.59, f32[128,16,512]{2,0,1:T(8,128)} %fusion.56, f32[128,16,512]{2,0,1:T(8,128)} %fusion.53, ...), kind=kOutput, calls=%fused_computation.63 | convolution fusion | flops 1630781440 | bytes 54525952 | tf_op jit(solution)/shard_map/cbh,bd->cdh/dot_general | solution.py:29
  314.1 6.3 fusion.113
  329.0 5.7 fusion.91
  334.7 6.1 fusion.117
  340.8 5.6 fusion.93
  346.4 5.6 fusion.115
  352.1 5.6 fusion.95
  357.7 5.6 fusion.121
  363.3 5.7 fusion.97
  369.0 5.6 fusion.119
  374.6 5.7 fusion.99
  380.3 51.4 %fusion.22 = (f32[128,2,8,512]{3,2,1,0:T(8,128)}, f32[128,2,8,512]{3,2,1,0:T(8,128)}, f32[128,2,8,512]{3,2,1,0:T(8,128)}, f32[128,2,8,512]{3,2,1,0:T(8,128)}, f3...) fusion(f32[16,128]{0,1:T(8,128)S(1)} %get-tuple-element.81, f32[16,128]{0,1:T(8,128)S(1)} %get-tuple-element.82, ...), kind=kLoop, calls=%fused_computation.46 | loop fusion | flops 25165824 | bytes 75513856
  468.7 9.0 %reduce.2 = bf16[1024,512]{1,0:T(8,128)(2,1)} reduce(bf16[1024,1,1,512]{3,2,1,0:T(2,128)(2,1)} %bitcast.350, bf16[]{:T(256)} %broadcast.374), dimensions={1,2}, to_apply=%bitcast.323.reduce_sub_computation | reduce | bytes 2097154
  487.8 7.3 %fusion.17 = (f32[3,512]{1,0:T(4,128)S(1)}, f32[3,512]{1,0:T(4,128)S(1)}, f32[3,512]{1,0:T(4,128)S(1)}, f32[3,512]{1,0:T(4,128)S(1)}, f32[3,512]{1,0:T(4,128)S(1...) fusion(bf16[3,1024,512]{2,1,0:T(8,128)(2,1)S(1)} %bitcast.326, f32[1,1024,512]{2,1,0:T(8,128)} %get-tuple-element.55, ...), kind=kLoop, calls=%fused_computation.36 | loop fusion | flops 31448064 | bytes 15765504 | tf_op jit(solution)/shard_map/reduce_sum | solution.py:119
  495.1 6.2 add_convert_fusion
  512.8 5.9 all-to-all-start.3
  539.1 12.9 %psum.14 = f32[7,3,512]{2,1,0:T(4,128)S(1)} all-reduce(f32[7,3,512]{2,1,0:T(4,128)S(1)} %constant_dynamic-update-slice_fusion), channel_id=1, replica_groups=mesh['dp'=4,'ctx'=8] {'dp'}, use_global_device_ids=true, to_apply=%region_8.10 | all-reduce | flops 10752 | bytes 86016 | tf_op jit(solution)/shard_map/psum | solution.py:186
  559.2 51.8 %all-to-all-done.3 = bf16[1,3,1024,512]{3,1,0,2:T(4,128)(2,1)} async-done(((bf16[1,3,1024,512]{3,1,0,2:T(4,128)(2,1)}), bf16[1,3,1024,512]{3,1,0,2:T(4,128)(2,1)}, u32[]{:S(2)}, u32[]{:S(2)}) %all-to-all-start.3) | async-done | bytes 3145760 | tf_op jit(solution)/shard_map/all_to_all | solution.py:184
  (171 shorter events, 183.2 us)
Async XLA Ops:
  7.2 287.3 %all-gather.3.cloned.1.call-start = ((), (), s32[]{:S(2)}) async-start(), calls=%async_computation.4 | async-start | bytes 5242880 | tf_op jit(solution)/shard_map/all_gather | solution.py:158
  11.5 4.1 copy-start.24
  44.5 33.1 %all-to-all-start.2 = ((bf16[8,2,32768]{2,1,0:T(2,128)(2,1)}), bf16[8,2,32768]{2,1,0:T(2,128)(2,1)S(1)}, u32[]{:S(2)}, u32[]{:S(2)}) async-start(bf16[8,2,32768]{2,1,0:T(2,128)(2,1)} %reshape.391), calls=%async_computation.2 | async-start | bytes 2097152 | tf_op jit(solution)/shard_map/all_to_all | solution.py:144
  77.6 97.1 %all-to-all-start = ((bf16[1,3,128,4096]{2,1,0,3:T(4,128)(2,1)}), bf16[1,3,128,4096]{2,1,0,3:T(4,128)(2,1)}, u32[]{:S(2)}, u32[]{:S(2)}) async-start(bf16[1,3,128,4096]{2,1,0,3:T(4,128)(2,1)} %copy.263), calls=%async_computation | async-start | bytes 8388608 | tf_op jit(solution)/shard_map/all_to_all | solution.py:143
  82.2 5.7 copy-start.29
  82.2 212.2 %all-gather.5.cloned.1.call-start = ((), (), s32[]{:S(2)}) async-start(), calls=%async_computation.5 | async-start | bytes 5242880 | tf_op jit(solution)/shard_map/all_gather | solution.py:159
  88.2 99.6 %copy-start.25 = (pred[16]{0:T(512)(128)(4,1)}, pred[16]{0:T(512)(128)(4,1)S(1)}, u32[]{:S(2)}) copy-start(pred[16]{0:T(512)(128)(4,1)S(1)} %get-tuple-element.73) | copy-start | bytes 52
  199.8 6.0 copy-start.13
  201.8 3.9 copy-start.12
  209.8 4.7 copy-start.22
  209.8 8.2 %copy-start.18 = (f32[8,65536]{1,0:T(8,128)S(1)}, f32[8,65536]{1,0:T(8,128)}, u32[]{:S(2)}) copy-start(f32[8,65536]{1,0:T(8,128)} %convert_multiply_fusion.15) | copy-start | bytes 6291460
  245.9 41.1 %copy-start.2 = (f32[16,128,512]{2,0,1:T(8,128)}, f32[16,128,512]{2,0,1:T(8,128)S(1)}, u32[]{:S(2)}) copy-start(f32[16,128,512]{2,0,1:T(8,128)S(1)} %get-tuple-element.45) | copy-start | bytes 12582916
  314.1 6.3 copy-start.8
  320.5 4.3 copy-start.7
  329.0 5.7 copy-start.6
  340.8 5.6 copy-start.5
  352.1 5.6 copy-start.4
  363.3 5.7 copy-start.3
  434.4 2.2 copy-start.21
  455.2 5.0 copy-start.14
  455.2 5.0 copy-start.23
  480.4 32.4 %all-to-all-start.1 = ((bf16[8,2,32768]{2,1,0:T(2,128)(2,1)}), bf16[8,2,32768]{2,1,0:T(2,128)(2,1)}, u32[]{:S(2)}, u32[]{:S(2)}) async-start(bf16[8,2,32768]{2,1,0:T(2,128)(2,1)} %reshape.389), calls=%async_computation.1 | async-start | bytes 2097152 | tf_op jit(solution)/shard_map/all_to_all | solution.py:183
  484.6 2.5 copy-start.10
  484.6 3.2 copy-start.15
  501.3 4.3 copy-start.28
  512.8 98.3 %all-to-all-start.3 = ((bf16[1,3,1024,512]{3,1,0,2:T(4,128)(2,1)}), bf16[1,3,1024,512]{3,1,0,2:T(4,128)(2,1)}, u32[]{:S(2)}, u32[]{:S(2)}) async-start(bf16[1,3,1024,512]{3,1,0,2:T(4,128)(2,1)} %copy.309), calls=%async_computation.3 | async-start | bytes 8388608 | tf_op jit(solution)/shard_map/all_to_all | solution.py:184
  518.7 106.5 %all-reduce.4.cloned.1.call-start = ((), (), s32[]{:S(2)}) async-start(), calls=%async_computation.6 | async-start | bytes 4194304 | tf_op jit(solution)/shard_map/psum | solution.py:186
  520.6 3.4 copy-start.19
  530.3 3.4 copy-start.26
  533.6 2.2 copy-start.16
  533.6 2.8 copy-start.17
  620.3 7.9 %copy-start.1 = (f32[1024,512]{1,0:T(8,128)S(1)}, f32[1024,512]{1,0:T(8,128)}, u32[]{:S(2)}) copy-start(f32[1024,512]{1,0:T(8,128)} %param.10) | copy-start | bytes 6291460
  (5 other events, 7.6 us)
Sparse Core Ops, SparseCore 0:
  15.7 37.7 all-gather.2
  86.7 36.2 all-gather.4
  533.8 53.7 all-reduce.3
where the time goes:
time: 645 us; the launch traced here: 635 us
  matrix products  196 us (30%)
  waiting for transfers between devices  152 us (24%)
  other arithmetic  128 us (20%)
  local copies, waits for them, and re-layouts  108 us (17%)
  starting transfers between devices  22.6 us (4%)
  between operations  14.8 us (2%)
  blocking collectives  12.9 us (2%)
    unnamed x3, other arithmetic  83.8 us
    all_to_all x1, waiting for transfers between devices, on_device(): lax.all_to_all(feats, 'ctx', split_axis=3, concat_axis=2, tiled=True)  82 us
    dot_general x12, matrix products, along_lanes(): jnp.einsum('cbh,bd->cdh', left, table, precision=HIGH, preferred_element_...  76.2 us
    dot_general x12, matrix products, against_lanes(): jnp.einsum('cdh,bd->cbh', left, table, precision=HIGH, preferred_element_...  66.1 us
    all_to_all x1, waiting for transfers between devices, on_device(): lax.all_to_all(grads_back, 'ctx', split_axis=2, concat_axis=3, tiled=True)  51.8 us
    unnamed x82, local copies, waits for them, and re-layouts  34.3 us
    dot_general x3, matrix products, spectrum(): jnp.dot(outer_tab[1], folded, precision=HIGH, preferred_element_type=jnp....  28.9 us
    all_to_all x1, waiting for transfers between devices, on_device(): lax.all_to_all(cotangent, 'ctx', split_axis=3, concat_axis=2, tiled=True)  18.6 us
  transfers between devices with their start and end apart: 7, of which 3 were waited for; matrix products, arithmetic and copies ran while one was open for 36% of the time, Pallas kernels for 0%

commit v1 on v0

v1 whole, which is shorter than its diff:
```python
import functools

import jax
import jax.numpy as jnp
import ml_dtypes
import numpy as np
from jax import lax
from jax.experimental import pallas as pl
from jax.experimental.pallas import tpu as pltpu
from jax.sharding import PartitionSpec as P

BF = jnp.bfloat16
F32 = jnp.float32
RIM = 8
VMEM_BYTES = 56 * 1024 * 1024


def dft_table(size):
    freq = np.arange(size)[:, None]
    time = np.arange(size)[None, :]
    angle = (2.0 * np.pi / (2 * size)) * ((freq * time) % (2 * size))
    imag = -np.sin(angle)
    imag[0] = np.where(np.arange(size) % 2 == 0, 1.0, -1.0)
    return np.concatenate([np.cos(angle), imag], 0).astype(ml_dtypes.bfloat16)


def dot(left, right):
    return jnp.dot(left, right, preferred_element_type=F32)


def featurize_kernel(tap_count, lanes, x_ref, halo_ref, g_ref, w_ref, send_ref, qkv_ref, ext_ref):
    rows, width = g_ref.shape
    half = rows // 2
    for part in range(width // lanes):
        cols = slice(part * lanes, (part + 1) * lanes)
        for slot in range(2):
            here = slice(slot * half, (slot + 1) * half)
            made = []
            for j in range(3):
                ext = ext_ref.at[(part * 2 + slot) * 3 + j]
                ext[:RIM] = halo_ref[j, :, cols].astype(F32)[slot * RIM : (slot + 1) * RIM]
                ext[RIM:] = x_ref[j, here, cols].astype(F32)
                total = jnp.zeros((half, lanes), F32)
                for s in range(tap_count):
                    total = total + w_ref[s * 3 + j : s * 3 + j + 1, cols] * ext[RIM - s : RIM - s + half]
                made.append(total.astype(BF))
                qkv_ref[j, here, cols] = made[j]
            query, key, value = (m.astype(F32) for m in made)
            send_ref[part, 0, 0, here] = (key * value).astype(BF)
            send_ref[part, 0, 1, here] = (g_ref[here, cols].astype(F32) * query).astype(BF)


def featurize(x, halo, g, taps, tap_count, nb, n, lanes):
    rows, width = g.shape
    block = nb * lanes
    return pl.pallas_call(
        functools.partial(featurize_kernel, tap_count, lanes),
        grid=(n,),
        in_specs=[
            pl.BlockSpec((3, rows, block), lambda c: (0, 0, c)),
            pl.BlockSpec((3, 2 * RIM, block), lambda c: (0, 0, c)),
            pl.BlockSpec((rows, block), lambda c: (0, c)),
            pl.BlockSpec((taps.shape[0], block), lambda c: (0, c)),
        ],
        out_specs=[
            pl.BlockSpec((nb, 1, 2, rows, lanes), lambda c: (0, c, 0, 0, 0)),
            pl.BlockSpec((3, rows, block), lambda c: (0, 0, c)),
        ],
        out_shape=[
            jax.ShapeDtypeStruct((nb, n, 2, rows, lanes), BF),
            jax.ShapeDtypeStruct((3, rows, width), BF),
        ],
        scratch_shapes=[pltpu.VMEM((nb * 6, rows // 2 + RIM, lanes), F32)],
        compiler_params=pltpu.CompilerParams(vmem_limit_bytes=VMEM_BYTES),
    )(x, halo, g, taps)


def filter_kernel(h_ref, table_ref, out_ref):
    segments, _, size, lanes = out_ref.shape
    scale = 1.0 / size
    for s in range(segments):
        spec = dot(table_ref[...], h_ref[s * size : (s + 1) * size].astype(BF)) * scale
        first = lax.broadcasted_iota(jnp.int32, (size, lanes), 0) == 0
        real, imag = spec[:size], spec[size:]
        out_ref[s, 0] = jnp.where(first, 0.5 * real, real)
        out_ref[s, 1] = jnp.where(first, 0.0, imag)
        out_ref[s, 2] = jnp.where(first, 0.5 * imag, real)


def filter_spectrum(h, table):
    size = table.shape[1]
    segments = h.shape[0] // size
    return pl.pallas_call(
        filter_kernel,
        out_shape=jax.ShapeDtypeStruct((segments, 3, size, h.shape[1]), F32),
        compiler_params=pltpu.CompilerParams(vmem_limit_bytes=VMEM_BYTES),
    )(h, table)


def long_kernel(tile, source_ref, order_ref, recv_ref, filt_ref, table_ref, back_ref, send_ref, cross_ref,
                seq_ref, spec_ref, time_ref):
    nb, n, _, rows, lanes = recv_ref.shape
    size = table_ref.shape[1]
    segments = filt_ref.shape[0]
    half = rows // 2
    cols = nb * lanes

    def gather(p, carry):
        k = source_ref[p]
        start = pl.multiple_of((k % 2) * half, half)
        to = pl.multiple_of(p * half, half)
        for b in range(nb):
            for a in range(2):
                seq_ref[a, pl.ds(to, half), b * lanes : (b + 1) * lanes] = recv_ref[b, k // 2, a, pl.ds(start, half)]
        return carry

    lax.fori_loop(0, 2 * n, gather, 0)

    def tiled(values):
        return jnp.concatenate([values] * nb, 1) if nb > 1 else values

    def shift_sum(now, other, sign):
        return now if other is None else now + sign * other

    for step in range(size // tile):
        at = slice(step * tile, (step + 1) * tile)
        up = slice(size + step * tile, size + (step + 1) * tile)
        if step == 0:
            first = lax.broadcasted_iota(jnp.int32, (tile, cols), 0) == 0
        if segments > 1:
            sign = (1 - 2 * (lax.broadcasted_iota(jnp.int32, (tile, cols), 0) % 2)).astype(F32)
        else:
            sign = None
        gated, back, filt = [], [], []
        for s in range(segments):
            span = slice(s * size, (s + 1) * size)
            gated.append((dot(table_ref[at], seq_ref[0, span]), dot(table_ref[up], seq_ref[0, span])))
            back.append((dot(table_ref[at], seq_ref[1, span]), dot(table_ref[up], seq_ref[1, span])))
            filt.append(tuple(tiled(filt_ref[s, i, at]) for i in range(3)))

        def total(pairs, make):
            re, im = None, None
            for pair in pairs:
                a, b = make(*pair)
                re, im = (a, b) if re is None else (re + a, im + b)
            return re, im

        def through(x, f):
            return x[0] * f[0] - x[1] * f[1], x[0] * f[1] + x[1] * f[2]

        def against(x, f):
            return x[0] * f[0] + x[1] * f[1], x[1] * f[2] - x[0] * f[1]

        def triple(x):
            if step > 0:
                return x[0], x[1], x[0]
            return jnp.where(first, 0.5 * x[0], x[0]), jnp.where(first, 0.0, x[1]), jnp.where(first, 0.5 * x[1], x[0])

        triples = [triple(x) for x in gated]
        conv = [total([(gated[p - d], filt[d]) for d in range(p + 1)], through) for p in range(segments)]
        grad = [total([(back[u], filt[u - p]) for u in range(p, segments)], against) for p in range(segments)]
        cross = [total([(back[u], triples[u - p]) for u in range(p, segments)], against) for p in range(segments)]
        for p in range(segments):
            for i, rows_to in enumerate((at, up)):
                spec_ref[0, p, rows_to] = shift_sum(conv[p][i], conv[p - 1][i] if p else None, sign).astype(BF)
                ahead = p + 1 < segments
                spec_ref[1, p, rows_to] = shift_sum(grad[p][i], grad[p + 1][i] if ahead else None, sign).astype(BF)
                value = shift_sum(cross[p][i], cross[p + 1][i] if ahead else None, sign)
                summed = value[:, :lanes]
                for b in range(1, nb):
                    summed = summed + value[:, b * lanes : (b + 1) * lanes]
                cross_ref[p, rows_to] = (summed * (1.0 / size)).astype(BF)

    for a in range(2):
        time_ref[a, segments * size :] = jnp.zeros((RIM, cols), F32)
        for p in range(segments):
            for step in range(size // tile):
                at = slice(step * tile, (step + 1) * tile)
                time_ref[a, p * size + step * tile : p * size + (step + 1) * tile] = dot(back_ref[at], spec_ref[a, p])

    def scatter(i, carry):
        for a in range(2):
            starts = [pl.multiple_of(order_ref[2 * i + slot] * half, half) for slot in range(2)]
            for b in range(nb):
                lane = slice(b * lanes, (b + 1) * lanes)
                for slot in range(2):
                    send_ref[b, i, a, slot * half : (slot + 1) * half] = time_ref[a, pl.ds(starts[slot], half), lane].astype(BF)
                rims = [time_ref[a, pl.ds(pl.multiple_of(starts[slot] + half, 8), RIM), lane] for slot in range(2)]
                send_ref[b, i, a, rows:] = jnp.concatenate(rims, 0).astype(BF)
        return carry

    lax.fori_loop(0, n, scatter, 0)


def long_conv(source, order, recv, filt, table, back):
    nb, n, _, rows, lanes = recv.shape
    size = table.shape[1]
    segments = filt.shape[0]
    cols = nb * lanes
    whole = pl.BlockSpec(memory_space=pltpu.VMEM)
    scalars = pl.BlockSpec(memory_space=pltpu.SMEM)
    return pl.pallas_call(
        functools.partial(long_kernel, min(256, size)),
        in_specs=[scalars, scalars] + [whole] * 4,
        out_specs=[whole, whole],
        out_shape=[
            jax.ShapeDtypeStruct((nb, n, 2, rows + 2 * RIM, lanes), BF),
            jax.ShapeDtypeStruct((segments, 2 * size, lanes), BF),
        ],
        scratch_shapes=[
            pltpu.VMEM((2, segments * size, cols), BF),
            pltpu.VMEM((2, segments, 2 * size, cols), BF),
            pltpu.VMEM((2, segments * size + RIM, cols), F32),
        ],
        compiler_params=pltpu.CompilerParams(vmem_limit_bytes=VMEM_BYTES),
    )(source, order, recv, filt, table, back)


def filter_grad_kernel(cross_ref, back_ref, out_ref):
    size = back_ref.shape[0]
    for p in range(cross_ref.shape[0]):
        out_ref[p * size : (p + 1) * size] = dot(back_ref[...], cross_ref[p])


def filter_grad(cross, back):
    segments, _, lanes = cross.shape
    return pl.pallas_call(
        filter_grad_kernel,
        out_shape=jax.ShapeDtypeStruct((segments * back.shape[0], lanes), F32),
        compiler_params=pltpu.CompilerParams(vmem_limit_bytes=VMEM_BYTES),
    )(cross, back)


def finish_kernel(tap_count, lanes, recv_ref, qkv_ref, x_ref, g_ref, halo_ref, after_ref, w_ref,
                  mixed_ref, grad_ref, short_ref, ext_ref, gf_ref):
    rows, width = g_ref.shape
    half = rows // 2
    for part in range(width // lanes):
        cols = slice(part * lanes, (part + 1) * lanes)
        short = {}
        for slot in range(2):
            here = slice(slot * half, (slot + 1) * half)
            rim = slice(slot * RIM, (slot + 1) * RIM)

            def longer(main, after):
                return jnp.concatenate([main.astype(F32), after.astype(F32)[rim]], 0)

            conv = longer(recv_ref[part, 0, 0, here], recv_ref[part, 0, 0, rows:])
            gate = longer(recv_ref[part, 0, 1, here], recv_ref[part, 0, 1, rows:])
            key = longer(qkv_ref[1, here, cols], after_ref[0, :, cols])
            value = longer(qkv_ref[2, here, cols], after_ref[1, :, cols])
            g = longer(g_ref[here, cols], after_ref[2, :, cols])
            mixed_ref[here, cols] = (qkv_ref[0, here, cols].astype(F32) * conv[:half]).astype(BF)
            grads = ((g * conv).astype(BF).astype(F32), gate * value, gate * key)
            for j in range(3):
                ext = ext_ref.at[(part * 2 + slot) * 3 + j]
                gf = gf_ref.at[(part * 2 + slot) * 3 + j]
                ext[:RIM] = halo_ref[j, :, cols].astype(F32)[rim]
                ext[RIM:] = x_ref[j, here, cols].astype(F32)
                gf[...] = grads[j]
                total = jnp.zeros((half, lanes), F32)
                for s in range(tap_count):
                    total = total + w_ref[s * 3 + j : s * 3 + j + 1, cols] * gf[s : s + half]
                    term = grads[j][:half] * ext[RIM - s : RIM - s + half]
                    term = jnp.sum(term.reshape(half // 8, 8, lanes), 0)
                    short[s, j] = term if slot == 0 else short[s, j] + term
                grad_ref[j, here, cols] = total.astype(BF)
        for (s, j), term in short.items():
            row = s * 3 + j
            short_ref[part, 0, row : row + 1] = jnp.sum(term, 0, keepdims=True)
        used = tap_count * 3
        short_ref[part, 0, used:] = jnp.zeros((short_ref.shape[2] - used, lanes), F32)


def finish(recv, qkv, x, g, halo, after, taps, tap_count):
    nb, n, _, long_rows, lanes = recv.shape
    rows, width = g.shape
    block = nb * lanes
    short_rows = -(-tap_count * 3 // 8) * 8
    spec3 = pl.BlockSpec((3, rows, block), lambda c: (0, 0, c))
    rim3 = pl.BlockSpec((3, 2 * RIM, block), lambda c: (0, 0, c))
    flat = pl.BlockSpec((rows, block), lambda c: (0, c))
    return pl.pallas_call(
        functools.partial(finish_kernel, tap_count, lanes),
        grid=(n,),
        in_specs=[
            pl.BlockSpec((nb, 1, 2, long_rows, lanes), lambda c: (0, c, 0, 0, 0)),
            spec3, spec3, flat, rim3, rim3,
            pl.BlockSpec((taps.shape[0], block), lambda c: (0, c)),
        ],
        out_specs=[flat, spec3, pl.BlockSpec((nb, 1, short_rows, lanes), lambda c: (0, c, 0, 0))],
        out_shape=[
            jax.ShapeDtypeStruct((rows, width), BF),
            jax.ShapeDtypeStruct((3, rows, width), BF),
            jax.ShapeDtypeStruct((nb, n, short_rows, lanes), F32),
        ],
        scratch_shapes=[pltpu.VMEM((nb * 6, rows // 2 + RIM, lanes), F32)] * 2,
        compiler_params=pltpu.CompilerParams(vmem_limit_bytes=VMEM_BYTES),
    )(recv, qkv, x, g, halo, after, taps)


def on_device(feats, grad_y, short_w, long_h, block_order):
    n = lax.axis_size("ctx")
    dp = lax.axis_size("dp")
    me = lax.axis_index("ctx")
    _, _, rows, width = feats.shape
    half = rows // 2
    channels = width // n
    tap_count = short_w.shape[0]
    seq_rows = rows * n
    spread = channels % (dp * 128) == 0
    nb = dp if spread else 1
    lanes = channels // nb
    axes = ("dp", "ctx") if spread else "ctx"
    size = min(seq_rows, 1024)
    table_np = dft_table(size)
    table = jnp.asarray(table_np)
    back = jnp.asarray(np.ascontiguousarray(table_np.T))
    numbers = jnp.arange(2 * n, dtype=jnp.int32)
    source = jnp.sum(numbers[None, :] * (block_order[None, :] == numbers[:, None]).astype(jnp.int32), axis=1)
    taps = short_w.reshape(tap_count * 3, width)
    x, g = feats[0], grad_y[0]

    flip = lax.dynamic_index_in_dim(block_order, 2 * me, 0, False) != me
    upward = [(j, j + 1) for j in range(n - 1)]
    downward = [(j + 1, j) for j in range(n - 1)]
    last = me == n - 1

    def by_slot(low, high):
        return jnp.concatenate([jnp.where(flip, high, low), jnp.where(flip, low, high)], 1)

    tails = x[:, half - RIM : half], x[:, rows - RIM :]
    low_tail, high_tail = jnp.where(flip, tails[1], tails[0]), jnp.where(flip, tails[0], tails[1])
    low_before = lax.ppermute(low_tail, "ctx", upward)
    high_before = lax.ppermute(high_tail, "ctx", downward)
    halo = by_slot(low_before, jnp.where(last, low_tail, high_before))

    send, qkv = featurize(x, halo, g, taps, tap_count, nb, n, lanes)
    recv = lax.all_to_all(send.reshape((nb * n,) + send.shape[2:]), axes, 0, 0, tiled=True).reshape(send.shape)

    heads = [jnp.stack([qkv[1, r : r + RIM], qkv[2, r : r + RIM], g[r : r + RIM]], 0) for r in (0, half)]
    low_head, high_head = jnp.where(flip, heads[1], heads[0]), jnp.where(flip, heads[0], heads[1])
    low_after = lax.ppermute(low_head, "ctx", downward)
    high_after = lax.ppermute(high_head, "ctx", upward)
    after = by_slot(jnp.where(last, high_head, low_after), high_after)

    mine = lax.dynamic_slice_in_dim(long_h, lax.axis_index("dp") * lanes, lanes, 1) if spread else long_h
    filt = filter_spectrum(mine, table)
    out, cross = long_conv(source, block_order, recv, filt, table, back)
    returned = lax.all_to_all(out.reshape((nb * n,) + out.shape[2:]), axes, 0, 0, tiled=True).reshape(out.shape)
    filter_part = filter_grad(cross, back)
    if spread:
        filter_sum = lax.all_gather(filter_part, "dp", axis=1, tiled=True)
    else:
        filter_sum = lax.psum(filter_part, "dp")
    mixed, grads, short = finish(returned, qkv, x, g, halo, after, taps, tap_count)
    pieces = lax.all_to_all(short.reshape((nb * n,) + short.shape[2:]), axes, 0, 0, tiled=True)
    short_sum = jnp.sum(pieces, 0)[: tap_count * 3]
    if spread:
        short_sum = lax.all_gather(short_sum, "dp", axis=1, tiled=True)
    else:
        short_sum = lax.psum(short_sum, "dp")
    return mixed[None], grads[None], short_sum.reshape(tap_count, 3, channels), filter_sum


def solution(mesh):
    placed = (P("dp", None, "ctx", None), P("dp", "ctx", None), P(), P(None, "ctx"), P())
    return jax.shard_map(
        on_device,
        mesh=mesh,
        in_specs=placed,
        out_specs=(
            P("dp", "ctx", None),
            P("dp", None, "ctx", None),
            P(None, None, "ctx"),
            P(None, "ctx"),
        ),
        check_vma=False,
    )
```

time: 645 us -> 214 us (0.33); the launches traced: 635 us -> 213 us
  matrix products: 196 us -> 0 us
  other arithmetic: 128 us -> 3.4 us
  local copies, waits for them, and re-layouts: 108 us -> 10.1 us
  waiting for transfers between devices: 152 us -> 105 us
  Pallas kernels: 0 us -> 46.2 us
  blocking collectives: 12.9 us -> 5.23 us
    dot_general x36 -> x0, matrix products: 196 us -> none  [the longest x12 76.2 us: along_lanes(): jnp.einsum('cbh,bd->cdh', left, table, precision=HIGH, preferred_element_...]
    unnamed x3 -> x0, other arithmetic: 83.8 us -> none
    all_to_all x4 -> x3, waiting for transfers between devices: 152 us -> 82.2 us  [the longest x1 43.8 us: on_device(): lax.all_to_all(send.reshape((nb * n,) + send.shape[2:]), axes, 0, 0, tile...]
    pallas_call x0 -> x5, Pallas kernels: none -> 46.2 us  [the longest x1 16.7 us: long_conv(): pl.pallas_call(functools.partial(long_kernel, min(256, size)), in_specs=[...]
    unnamed x82 -> x7, local copies, waits for them, and re-layouts: 34.3 us -> 4.97 us
    ppermute x0 -> x4, waiting for transfers between devices: none -> 22.8 us  [the longest x1 17.7 us: on_device(): low_after = lax.ppermute(low_head, 'ctx', downward)]
    reshape x12 -> x2, local copies, waits for them, and re-layouts: 22.4 us -> 0.98 us  [the longest x1 0.96 us: on_device(): taps = short_w.reshape(tap_count * 3, width)]
    all_to_all x6 -> x0, local copies, waits for them, and re-layouts: 19.4 us -> none  [the longest x2 9.29 us: on_device(): lax.all_to_all(grads_back, 'ctx', split_axis=2, concat_axis=3, tiled=True)]
  transfers between devices with their start and end apart: 7 -> 8, of which waited for: 3 -> 6; matrix products, arithmetic and copies ran while one was open for 36% -> 3% of each run, Pallas kernels for 0% -> 10%
where the time goes in v1:
time: 214 us; the launch traced here: 213 us
  waiting for transfers between devices  105 us (49%)
  Pallas kernels  46.2 us (22%)
  starting transfers between devices  28.7 us (13%)
  between operations  14.8 us (7%)
  local copies, waits for them, and re-layouts  10.1 us (5%)
  blocking collectives  5.23 us (2%)
  other arithmetic  3.4 us (2%)
    all_to_all x1, waiting for transfers between devices, on_device(): lax.all_to_all(send.reshape((nb * n,) + send.shape[2:]), axes, 0, 0, tile...  43.8 us
    all_to_all x1, waiting for transfers between devices, on_device(): lax.all_to_all(out.reshape((nb * n,) + out.shape[2:]), axes, 0, 0, tiled=...  24.9 us
    ppermute x1, waiting for transfers between devices, on_device(): low_after = lax.ppermute(low_head, 'ctx', downward)  17.7 us
    pallas_call x1, Pallas kernels, long_conv(): pl.pallas_call(functools.partial(long_kernel, min(256, size)), in_specs=[...  16.7 us
    all_to_all x1, waiting for transfers between devices, on_device(): lax.all_to_all(short.reshape((nb * n,) + short.shape[2:]), axes, 0, 0, ti...  13.5 us
    pallas_call x1, Pallas kernels, finish(): pl.pallas_call(functools.partial(finish_kernel, tap_count, lanes), grid=(...  11.7 us
    pallas_call x1, Pallas kernels, featurize(): pl.pallas_call(functools.partial(featurize_kernel, tap_count, lanes), gri...  8.56 us
    all_to_all x1, starting transfers between devices, on_device(): lax.all_to_all(short.reshape((nb * n,) + short.shape[2:]), axes, 0, 0, ti...  6.33 us
  transfers between devices with their start and end apart: 8, of which 6 were waited for; matrix products, arithmetic and copies ran while one was open for 3% of the time, Pallas kernels for 10%

profile of v1, /device:TPU:0, one launch (start us, length us, event | category | flops | bytes accessed | tf_op | source)
XLA Modules:
  0.0 213.4 jit_solution(1364670765359840173)
XLA Ops:
  7.2 1.4 dynamic_slice.7
  9.2 1.1 broadcast_select_fusion.8
  10.3 1.3 collective-permute-start
  11.6 5.5 %collective-permute-start.1 = (bf16[3,8,4096]{2,1,0:T(8,128)(2,1)S(1)}, bf16[3,8,4096]{2,1,0:T(8,128)(2,1)S(1)}, u32[]{:S(2)}, u32[]{:S(2)}) collective-permute-start(bf16[3,8,4096]{2,1,0:T(8,128)(2,1)S(1)} %get-tuple-element.29), channel_id=1, source_target_pairs={{0,1},{1,2},{2,3},{3,4},{4,5},{5,6},{6,7},{8,9},{9,10},{10,11},{11... | collective-permute-start | bytes 589832 | tf_op jit(solution)/shard_map/ppermute | solution.py:334
  17.1 1.2 copy.14
  18.3 1.0 reshape.34.w_ref
  19.3 0.7 collective-permute-done
  20.1 4.4 %collective-permute-done.1 = bf16[3,8,4096]{2,1,0:T(8,128)(2,1)S(1)} collective-permute-done((bf16[3,8,4096]{2,1,0:T(8,128)(2,1)S(1)}, bf16[3,8,4096]{2,1,0:T(8,128)(2,1)S(1)}, u32[]{:S(2)}, u32[]{:S(2)}) %collective-permute-start.1) | collective-permute-done | bytes 196640 | tf_op jit(solution)/shard_map/ppermute | solution.py:334
  24.5 0.8 pad_maximum_fusion.halo_ref
  25.2 8.6 %shard_map.102 = (bf16[4,8,2,128,128]{4,3,2,1,0:T(8,128)(2,1)}, bf16[3,128,4096]{2,1,0:T(8,128)(2,1)}) custom-call(bf16[3,128,4096]{2,1,0:T(8,128)(2,1)} %bitcast.12, bf16[3,16,4096]{2,1,0:T(8,128)(2,1)} %pad_maximum_fusion.halo_ref, bf16[128,4096]{1,0:T(8,128)(2,1)} %bitcast.14, f32[21,4096]{1,0:T(8,128)} %reshape.34.w_ref), custom_call_target="tpu_custom_call" | custom-call | tf_op jit(solution)/shard_map/pallas_call | solution.py:56
  33.8 5.9 %all-to-all-start = ((bf16[32,2,128,128]{3,2,1,0:T(8,128)(2,1)}), bf16[32,2,128,128]{3,2,1,0:T(8,128)(2,1)}, u32[]{:S(2)}, u32[]{:S(2)}) async-start(bf16[32,2,128,128]{3,2,1,0:T(8,128)(2,1)} %bitcast.17), calls=%async_computation | async-start | bytes 4194304 | tf_op jit(solution)/shard_map/all_to_all | solution.py:339
  39.8 0.9 constant_dynamic-slice_fusion.h_ref
  40.6 4.8 %shard_map.103.filt_ref = f32[1,3,1024,128]{3,2,1,0:T(8,128)} custom-call(f32[1024,128]{1,0:T(8,128)} %constant_dynamic-slice_fusion.h_ref, bf16[2048,1024]{1,0:T(8,128)(2,1)} %constant.30.clone.table_ref), custom_call_target="tpu_custom_call" | custom-call | tf_op jit(solution)/shard_map/pallas_call | solution.py:93
  45.4 0.6 select_reduce_fusion.source_ref
  46.0 43.8 %all-to-all-done = bf16[32,2,128,128]{3,2,1,0:T(8,128)(2,1)} async-done(((bf16[32,2,128,128]{3,2,1,0:T(8,128)(2,1)}), bf16[32,2,128,128]{3,2,1,0:T(8,128)(2,1)}, u32[]{:S(2)}, u32[]{:S(2)}) %all-to-all-start) | async-done | bytes 2097184 | tf_op jit(solution)/shard_map/all_to_all | solution.py:339
  89.8 16.7 %shard_map.104 = (bf16[4,8,2,144,128]{4,3,2,1,0:T(8,128)(2,1)}, bf16[1,2048,128]{2,1,0:T(8,128)(2,1)}) custom-call(s32[16]{0:T(128)} %select_reduce_fusion.source_ref, s32[16]{0:T(128)} %order_ref.1, bf16[4,8,2,128,128]{4,3,2,1,0:T(8,128)(2,1)} %bitcast.4.recv_ref, f32[1,3,1024,128]{3,2,1,0:T(8,128)} %shard_map.103.filt_ref, ...), custom_call_target="tpu_custom_call" | custom-call | tf_op jit(solution)/shard_map/pallas_call | solution.py:202
  106.5 3.5 %all-to-all-start.1 = ((bf16[32,2,144,128]{3,2,1,0:T(8,128)(2,1)}), bf16[32,2,144,128]{3,2,1,0:T(8,128)(2,1)}, u32[]{:S(2)}, u32[]{:S(2)}) async-start(bf16[32,2,144,128]{3,2,1,0:T(8,128)(2,1)} %bitcast.16), calls=%async_computation.1 | async-start | bytes 4718592 | tf_op jit(solution)/shard_map/all_to_all | solution.py:350
  110.1 0.2 all-gather.2.cloned.1.call-start
  110.3 0.9 fusion.1
  111.2 4.4 %shard_map.106 = f32[1024,128]{1,0:T(8,128)} custom-call(bf16[1,2048,128]{2,1,0:T(8,128)(2,1)} %get-tuple-element.17.cross_ref, bf16[1024,2048]{1,0:T(8,128)(2,1)} %constant.31.clone.back_ref), custom_call_target="tpu_custom_call" | custom-call | tf_op jit(solution)/shard_map/pallas_call | solution.py:227
  115.6 1.0 fusion
  116.7 1.3 collective-permute-start.3
  118.0 4.6 %collective-permute-start.2 = (bf16[3,8,4096]{2,1,0:T(8,128)(2,1)S(1)}, bf16[3,8,4096]{2,1,0:T(8,128)(2,1)S(1)}, u32[]{:S(2)}, u32[]{:S(2)}) collective-permute-start(bf16[3,8,4096]{2,1,0:T(8,128)(2,1)S(1)} %get-tuple-element.37), channel_id=1, source_target_pairs={{0,1},{1,2},{2,3},{3,4},{4,5},{5,6},{6,7},{8,9},{9,10},{10,11},{11... | collective-permute-start | bytes 589832 | tf_op jit(solution)/shard_map/ppermute | solution.py:344
  122.5 17.7 %collective-permute-done.3 = bf16[3,8,4096]{2,1,0:T(8,128)(2,1)S(1)} collective-permute-done((bf16[3,8,4096]{2,1,0:T(8,128)(2,1)S(1)}, bf16[3,8,4096]{2,1,0:T(8,128)(2,1)S(1)}, u32[]{:S(2)}, u32[]{:S(2)}) %collective-permute-start.3) | collective-permute-done | bytes 196640 | tf_op jit(solution)/shard_map/ppermute | solution.py:343
  140.3 0.8 pad_maximum_fusion.1.after_ref
  141.1 24.9 %all-to-all-done.1 = bf16[32,2,144,128]{3,2,1,0:T(8,128)(2,1)} async-done(((bf16[32,2,144,128]{3,2,1,0:T(8,128)(2,1)}), bf16[32,2,144,128]{3,2,1,0:T(8,128)(2,1)}, u32[]{:S(2)}, u32[]{:S(2)}) %all-to-all-start.1) | async-done | bytes 2359328 | tf_op jit(solution)/shard_map/all_to_all | solution.py:350
  166.0 11.7 %shard_map.105 = (bf16[128,4096]{1,0:T(8,128)(2,1)}, bf16[3,128,4096]{2,1,0:T(8,128)(2,1)}, f32[4,8,24,128]{3,2,1,0:T(8,128)}) custom-call(bf16[4,8,2,144,128]{4,3,2,1,0:T(8,128)(2,1)} %bitcast.6.recv_ref, bf16[3,128,4096]{2,1,0:T(8,128)(2,1)} %get-tuple-element.13.qkv_ref, bf16[3,128,4096]{2,1,0:T(8,128)(2,1)} %bitcast.13, bf16[128,4096]{1,0:T(8,128)(2,1)} %bitcast.15, ...), custom_call_target="tpu_custom_call" | custom-call | tf_op jit(solution)/shard_map/pallas_call | solution.py:283
  177.7 6.3 %all-to-all-start.2 = ((f32[32,24,128]{2,1,0:T(8,128)}), f32[32,24,128]{2,1,0:T(8,128)S(1)}, u32[]{:S(2)}, u32[]{:S(2)}) async-start(f32[32,24,128]{2,1,0:T(8,128)} %bitcast.18), calls=%async_computation.2 | async-start | bytes 786432 | tf_op jit(solution)/shard_map/all_to_all | solution.py:357
  184.0 13.5 %all-to-all-done.2 = f32[32,24,128]{2,1,0:T(8,128)S(1)} async-done(((f32[32,24,128]{2,1,0:T(8,128)}), f32[32,24,128]{2,1,0:T(8,128)S(1)}, u32[]{:S(2)}, u32[]{:S(2)}) %all-to-all-start.2) | async-done | bytes 393248 | tf_op jit(solution)/shard_map/all_to_all | solution.py:357
  197.6 5.2 %all_gather.6 = f32[21,512]{1,0:T(8,128)S(1)} all-gather(f32[21,128]{1,0:T(8,128)S(1)} %bitcast.19), channel_id=1, replica_groups=mesh['dp'=4,'ctx'=8] {'dp'}, dimensions={1}, use_global_device_ids=true | all-gather | bytes 53760 | tf_op jit(solution)/shard_map/all_gather | solution.py:360
  202.9 0.6 copy.15
  203.5 3.1 %copy.17 = f32[1024,512]{1,0:T(8,128)} copy(f32[1024,512]{1,0:T(8,128)} %all-gather.2.cloned.1.call-done) | data formatting | bytes 4194304
  (12 shorter events, 0.2 us)
Async XLA Ops:
  7.2 32.6 %copy-start = (f32[1024,512]{1,0:T(8,128)S(1)}, f32[1024,512]{1,0:T(8,128)}, u32[]{:S(2)}) copy-start(f32[1024,512]{1,0:T(8,128)} %param.10) | copy-start | bytes 6291460
  10.3 9.8 %collective-permute-start = (bf16[3,8,4096]{2,1,0:T(8,128)(2,1)S(1)}, bf16[3,8,4096]{2,1,0:T(8,128)(2,1)S(1)}, u32[]{:S(2)}, u32[]{:S(2)}) collective-permute-start(bf16[3,8,4096]{2,1,0:T(8,128)(2,1)S(1)} %get-tuple-element.28), channel_id=1, source_target_pairs={{1,0},{2,1},{3,2},{4,3},{5,4},{6,5},{7,6},{9,8},{10,9},{11,10},{12... | collective-permute-start | bytes 589832 | tf_op jit(solution)/shard_map/ppermute | solution.py:335
  11.6 12.8 %collective-permute-start.1 = (bf16[3,8,4096]{2,1,0:T(8,128)(2,1)S(1)}, bf16[3,8,4096]{2,1,0:T(8,128)(2,1)S(1)}, u32[]{:S(2)}, u32[]{:S(2)}) collective-permute-start(bf16[3,8,4096]{2,1,0:T(8,128)(2,1)S(1)} %get-tuple-element.29), channel_id=1, source_target_pairs={{0,1},{1,2},{2,3},{3,4},{4,5},{5,6},{6,7},{8,9},{9,10},{10,11},{11... | collective-permute-start | bytes 589832 | tf_op jit(solution)/shard_map/ppermute | solution.py:334
  33.8 56.0 %all-to-all-start = ((bf16[32,2,128,128]{3,2,1,0:T(8,128)(2,1)}), bf16[32,2,128,128]{3,2,1,0:T(8,128)(2,1)}, u32[]{:S(2)}, u32[]{:S(2)}) async-start(bf16[32,2,128,128]{3,2,1,0:T(8,128)(2,1)} %bitcast.17), calls=%async_computation | async-start | bytes 4194304 | tf_op jit(solution)/shard_map/all_to_all | solution.py:339
  40.6 4.8 %copy-start.1 = (s32[16]{0:T(128)S(1)}, s32[16]{0:T(128)}, u32[]{:S(2)}) copy-start(s32[16]{0:T(128)} %order_ref.1) | copy-start | bytes 196
  106.5 59.5 %all-to-all-start.1 = ((bf16[32,2,144,128]{3,2,1,0:T(8,128)(2,1)}), bf16[32,2,144,128]{3,2,1,0:T(8,128)(2,1)}, u32[]{:S(2)}, u32[]{:S(2)}) async-start(bf16[32,2,144,128]{3,2,1,0:T(8,128)(2,1)} %bitcast.16), calls=%async_computation.1 | async-start | bytes 4718592 | tf_op jit(solution)/shard_map/all_to_all | solution.py:350
  110.1 73.9 %all-gather.2.cloned.1.call-start = ((), (), s32[]{:S(2)}) async-start(), calls=%async_computation.3 | async-start | bytes 2621440 | tf_op jit(solution)/shard_map/all_gather | solution.py:353
  116.7 23.6 %collective-permute-start.3 = (bf16[3,8,4096]{2,1,0:T(8,128)(2,1)S(1)}, bf16[3,8,4096]{2,1,0:T(8,128)(2,1)S(1)}, u32[]{:S(2)}, u32[]{:S(2)}) collective-permute-start(bf16[3,8,4096]{2,1,0:T(8,128)(2,1)S(1)} %get-tuple-element.36), channel_id=1, source_target_pairs={{1,0},{2,1},{3,2},{4,3},{5,4},{6,5},{7,6},{9,8},{10,9},{11,10},{12... | collective-permute-start | bytes 589832 | tf_op jit(solution)/shard_map/ppermute | solution.py:343
  118.0 22.3 %collective-permute-start.2 = (bf16[3,8,4096]{2,1,0:T(8,128)(2,1)S(1)}, bf16[3,8,4096]{2,1,0:T(8,128)(2,1)S(1)}, u32[]{:S(2)}, u32[]{:S(2)}) collective-permute-start(bf16[3,8,4096]{2,1,0:T(8,128)(2,1)S(1)} %get-tuple-element.37), channel_id=1, source_target_pairs={{0,1},{1,2},{2,3},{3,4},{4,5},{5,6},{6,7},{8,9},{9,10},{10,11},{11... | collective-permute-start | bytes 589832 | tf_op jit(solution)/shard_map/ppermute | solution.py:344
  177.7 19.9 %all-to-all-start.2 = ((f32[32,24,128]{2,1,0:T(8,128)}), f32[32,24,128]{2,1,0:T(8,128)S(1)}, u32[]{:S(2)}, u32[]{:S(2)}) async-start(f32[32,24,128]{2,1,0:T(8,128)} %bitcast.18), calls=%async_computation.2 | async-start | bytes 786432 | tf_op jit(solution)/shard_map/all_to_all | solution.py:357
Sparse Core Ops, SparseCore 0:
  115.7 32.0 all-gather.1

commit v2 on v0

v2 whole, which is shorter than its diff:
```python
import functools

import jax
import jax.numpy as jnp
import ml_dtypes
import numpy as np
from jax import lax
from jax.experimental import pallas as pl
from jax.experimental.pallas import tpu as pltpu
from jax.sharding import PartitionSpec as P

BF = jnp.bfloat16
F32 = jnp.float32
RIM = 8
PARAMS = pltpu.CompilerParams(vmem_limit_bytes=56 * 1024 * 1024)
ANYWHERE = pl.BlockSpec(memory_space=pltpu.HBM)
VECTOR = pl.BlockSpec(memory_space=pltpu.VMEM)
SCALAR = pl.BlockSpec(memory_space=pltpu.SMEM)


def dft_tables(size):
    half = size // 2
    freq = np.arange(half)[:, None]
    tables = []
    for parity in range(2):
        time = 2 * np.arange(half)[None, :] + parity
        angle = (2.0 * np.pi / (2 * size)) * ((freq * time) % (2 * size))
        imag = -np.sin(angle)
        middle = np.pi / 2 * time[0]
        imag[0] = np.round(-np.sin(middle) if parity else np.cos(middle))
        tables.append(np.concatenate([np.cos(angle), imag], 0))
    forward = np.stack(tables).astype(ml_dtypes.bfloat16)
    return forward, np.ascontiguousarray(forward.transpose(0, 2, 1))


def dot(left, right):
    return jnp.dot(left, right, preferred_element_type=F32)


def each_part(width, body):
    lanes = min(128, width)

    def step(part, carry):
        body(pl.ds(pl.multiple_of(part * lanes, lanes), lanes))
        return carry

    lax.fori_loop(0, width // lanes, step, 0)


def chunk_at(index, channels):
    return pl.ds(pl.multiple_of(index * channels, channels), channels)


def featurize_kernel(tap_count, pieces, where_ref, x_hbm, g_hbm, halo_ref, w_ref, *refs):
    sends_hbm, qkv_hbm = refs[:pieces], refs[pieces]
    x_buf, g_buf, send_buf, qkv_buf, ext_ref, load_sem, store_sem = refs[pieces + 1 :]
    _, _, rows, channels = x_buf.shape
    half = rows // 2

    def loads(i):
        chunk = chunk_at(where_ref[i], channels)
        return [
            pltpu.make_async_copy(x_hbm.at[:, :, chunk], x_buf.at[i], load_sem.at[0, i]),
            pltpu.make_async_copy(g_hbm.at[:, chunk], g_buf.at[i], load_sem.at[1, i]),
        ]

    def stores(i):
        chunk = chunk_at(where_ref[i], channels)
        return [
            pltpu.make_async_copy(send_buf.at[i], sends_hbm[i], store_sem.at[0, i]),
            pltpu.make_async_copy(qkv_buf.at[i], qkv_hbm.at[:, :, chunk], store_sem.at[1, i]),
        ]

    for i in range(pieces):
        for copy in loads(i):
            copy.start()
    for i in range(pieces):
        for copy in loads(i):
            copy.wait()

        def body(cols):
            lanes = ext_ref.shape[-1]
            wide = pl.ds(pl.multiple_of(where_ref[i] * channels + cols.start, lanes), lanes)
            for slot in range(2):
                here = slice(slot * half, (slot + 1) * half)
                made = []
                for j in range(3):
                    ext = ext_ref.at[slot * 3 + j]
                    ext[:RIM] = halo_ref[j, :, wide].astype(F32)[slot * RIM : (slot + 1) * RIM]
                    ext[RIM:] = x_buf[i, j, here, cols].astype(F32)
                    total = jnp.zeros((half, lanes), F32)
                    for s in range(tap_count):
                        total = total + w_ref[s * 3 + j : s * 3 + j + 1, wide] * ext[RIM - s : RIM - s + half]
                    made.append(total.astype(BF))
                    qkv_buf[i, j, here, cols] = made[j]
                query, key, value = (m.astype(F32) for m in made)
                for a, sent in enumerate((key * value, g_buf[i, here, cols].astype(F32) * query)):
                    turn = ext_ref.at[slot * 3 + a, RIM:]
                    turn[...] = sent
                    for e in range(2):
                        send_buf[i, a, slot, e, :, cols] = turn[pl.ds(e, half // 2, stride=2)].astype(BF)

        each_part(channels, body)
        for copy in stores(i):
            copy.start()
    for i in range(pieces):
        for copy in stores(i):
            copy.wait()


def featurize(chunks, x, g, halo, taps, tap_count):
    rows, width = g.shape
    pieces = chunks.shape[0]
    channels = width // pieces
    *sends, qkv = pl.pallas_call(
        functools.partial(featurize_kernel, tap_count, pieces),
        in_specs=[SCALAR, ANYWHERE, ANYWHERE, VECTOR, VECTOR],
        out_specs=[ANYWHERE] * (pieces + 1),
        out_shape=[jax.ShapeDtypeStruct((2, 2, 2, rows // 4, channels), BF)] * pieces
        + [jax.ShapeDtypeStruct((3, rows, width), BF)],
        scratch_shapes=[
            pltpu.VMEM((pieces, 3, rows, channels), BF),
            pltpu.VMEM((pieces, rows, channels), BF),
            pltpu.VMEM((pieces, 2, 2, 2, rows // 4, channels), BF),
            pltpu.VMEM((pieces, 3, rows, channels), BF),
            pltpu.VMEM((6, rows // 2 + RIM, min(128, channels)), F32),
            pltpu.SemaphoreType.DMA((2, pieces)),
            pltpu.SemaphoreType.DMA((2, pieces)),
        ],
        compiler_params=PARAMS,
    )(chunks, x, g, halo, taps)
    return sends, qkv


def first_row(shape):
    return lax.broadcasted_iota(jnp.int32, shape, 0) == 0


def unite(even, odd, first):
    plus = even[0] + odd[0], even[1] + odd[1]
    minus = even[0] - odd[0], odd[1] - even[1]
    if first is not None:
        plus = plus[0], jnp.where(first, even[1], plus[1])
        minus = minus[0], jnp.where(first, odd[1], minus[1])
    return plus + minus


def divide(spec, first):
    plus_re, plus_im, minus_re, minus_im = spec
    even_im, odd_im = plus_im - minus_im, plus_im + minus_im
    if first is not None:
        even_im, odd_im = jnp.where(first, plus_im, even_im), jnp.where(first, minus_im, odd_im)
    return plus_re + minus_re, even_im, plus_re - minus_re, odd_im


def times(x, f, first, sign):
    def add(a, b):
        return a + b if sign > 0 else a - b

    out = []
    for i in (0, 2):
        re = add(x[i] * f[i], -(x[i + 1] * f[i + 1]))
        im = add(x[i + 1] * f[i], x[i] * f[i + 1])
        out += [re, im]
    if first is not None:
        middle_re = add(x[1] * f[1], -(x[3] * f[3]))
        middle_im = add(x[3] * f[1], x[1] * f[3])
        out = [
            jnp.where(first, 0.5 * (x[0] * f[0]), out[0]),
            jnp.where(first, middle_re, out[1]),
            jnp.where(first, 0.5 * (x[2] * f[2]), out[2]),
            jnp.where(first, middle_im, out[3]),
        ]
    return tuple(out)


def filter_kernel(h_ref, table_ref, out_ref, turn_ref):
    segments, _, half, width = out_ref.shape
    lanes = turn_ref.shape[-1]
    size = 2 * half
    for part in range(width // lanes):
        cols = slice(part * lanes, (part + 1) * lanes)
        turn_ref[part] = h_ref[:, cols]
        first = first_row((half, lanes))
        for s in range(segments):
            parts = []
            for e in range(2):
                time = turn_ref[part, pl.ds(s * size + e, half, stride=2)]
                made = dot(table_ref[e], time.astype(BF)) * (1.0 / size)
                parts.append((made[:half], made[half:]))
            for i, value in enumerate(unite(*parts, first)):
                out_ref[s, i, :, cols] = value


def filter_spectrum(h, table):
    size = table.shape[1]
    rows, width = h.shape
    lanes = min(128, width)
    return pl.pallas_call(
        filter_kernel,
        out_shape=jax.ShapeDtypeStruct((rows // size, 4, size // 2, width), F32),
        scratch_shapes=[pltpu.VMEM((width // lanes, rows, lanes), F32)],
        compiler_params=PARAMS,
    )(h, table)


def long_kernel(tile, n, from_ref, to_ref, filt_hbm, table_hbm, back_hbm, *refs):
    recvs_hbm, send_hbm, cross_hbm = refs[:n], refs[n], refs[n + 1]
    filt_ref, table_ref, back_ref, seq_ref, spec_ref, time_ref, cross_ref, const_sem, in_sem, out_sem = refs[n + 2 :]
    _, _, _, quarter, cols = recvs_hbm[0].shape
    _, size, freqs = table_ref.shape
    segments = filt_ref.shape[0]
    constants = [
        pltpu.make_async_copy(source, target, const_sem.at[i])
        for i, (source, target) in enumerate(((table_hbm, table_ref), (filt_hbm, filt_ref), (back_hbm, back_ref)))
    ]

    def block(position):
        return pl.ds(pl.multiple_of(position * quarter, quarter), quarter)

    arrivals = [
        pltpu.make_async_copy(
            recvs_hbm[i].at[:, slot], seq_ref.at[:, :, block(from_ref[2 * i + slot])], in_sem.at[slot, i]
        )
        for i in range(n) for slot in range(2)
    ]

    def departures(a):
        return [
            pltpu.make_async_copy(
                time_ref.at[a, :, block(to_ref[2 * i + slot])], send_hbm.at[i, a, slot], out_sem.at[a, slot, i]
            )
            for i in range(n) for slot in range(2)
        ]

    constants[0].start()
    for copy in arrivals:
        copy.start()
    constants[0].wait()
    for copy in arrivals:
        copy.wait()
    constants[1].start()
    constants[2].start()

    def total(terms):
        out = terms[0]
        for term in terms[1:]:
            out = tuple(x + y for x, y in zip(out, term))
        return out

    for step in range(freqs // tile):
        at = slice(step * tile, (step + 1) * tile)
        up = slice(freqs + step * tile, freqs + (step + 1) * tile)
        first = first_row((tile, cols)) if step == 0 else None
        sign = (1 - 2 * (lax.broadcasted_iota(jnp.int32, (tile, cols), 0) % 2)).astype(F32) if segments > 1 else None
        spectra = [[], []]
        for s in range(segments):
            span = slice(s * freqs, (s + 1) * freqs)
            for a in range(2):
                parts = [(dot(table_ref[e, at], seq_ref[a, e, span]), dot(table_ref[e, up], seq_ref[a, e, span]))
                         for e in range(2)]
                spectra[a].append(unite(*parts, first))
        if step == 0:
            constants[1].wait()
        filt = [[filt_ref[s, i, at] for i in range(4)] for s in range(segments)]
        gated, back = spectra
        conv = [total([times(gated[p - d], filt[d], first, 1) for d in range(p + 1)]) for p in range(segments)]
        grad = [total([times(back[u], filt[u - p], first, -1) for u in range(p, segments)]) for p in range(segments)]
        cross = [total([times(back[u], gated[u - p], first, -1) for u in range(p, segments)]) for p in range(segments)]

        def wrapped(values, p, other):
            if not 0 <= other < segments:
                return values[p]
            return tuple(x + sign * y for x, y in zip(values[p], values[other]))

        for p in range(segments):
            for a, value in enumerate((wrapped(conv, p, p - 1), wrapped(grad, p, p + 1))):
                for i, part in enumerate(divide(value, first)):
                    spec_ref[a, i // 2, p, at if i % 2 == 0 else up] = part.astype(BF)
            for i, part in enumerate(divide(wrapped(cross, p, p + 1), first)):
                cross_ref[p, i // 2, at if i % 2 == 0 else up] = (part * (1.0 / size)).astype(BF)

    cross_copy = pltpu.make_async_copy(cross_ref, cross_hbm, const_sem.at[0])
    cross_copy.start()
    constants[2].wait()
    for a in range(2):
        for e in range(2):
            for p in range(segments):
                for step in range(freqs // tile):
                    at = slice(step * tile, (step + 1) * tile)
                    to = slice(p * freqs + step * tile, p * freqs + (step + 1) * tile)
                    time_ref[a, e, to] = dot(back_ref[e, at], spec_ref[a, e, p]).astype(BF)
        for copy in departures(a):
            copy.start()
    for a in range(2):
        for copy in departures(a):
            copy.wait()
    cross_copy.wait()


def long_conv(come_from, go_to, recvs, filt, table, back):
    n = len(recvs)
    _, _, _, quarter, cols = recvs[0].shape
    _, size, freqs = table.shape
    segments = filt.shape[0]
    return pl.pallas_call(
        functools.partial(long_kernel, min(256, freqs), n),
        in_specs=[SCALAR, SCALAR] + [ANYWHERE] * (n + 3),
        out_specs=[ANYWHERE] * 2,
        out_shape=[
            jax.ShapeDtypeStruct((n, 2, 2, 2, quarter, cols), BF),
            jax.ShapeDtypeStruct((segments, 2, size, cols), BF),
        ],
        scratch_shapes=[
            pltpu.VMEM(filt.shape, F32),
            pltpu.VMEM(table.shape, BF),
            pltpu.VMEM(back.shape, BF),
            pltpu.VMEM((2, 2, segments * freqs, cols), BF),
            pltpu.VMEM((2, 2, segments, size, cols), BF),
            pltpu.VMEM((2, 2, segments * freqs, cols), BF),
            pltpu.VMEM((segments, 2, size, cols), BF),
            pltpu.SemaphoreType.DMA((3,)),
            pltpu.SemaphoreType.DMA((2, n)),
            pltpu.SemaphoreType.DMA((2, 2, n)),
        ],
        compiler_params=PARAMS,
    )(come_from, go_to, filt, table, back, *recvs)


def filter_grad_kernel(cross_ref, back_ref, out_ref, turn_ref):
    segments = cross_ref.shape[0]
    _, freqs, size = back_ref.shape
    parts, _, lanes = turn_ref.shape
    for p in range(segments):
        for e in range(2):
            value = dot(back_ref[e], cross_ref[p, e])
            for i in range(parts):
                turn_ref[i, pl.ds(p * size + e, freqs, stride=2)] = value[:, i * lanes : (i + 1) * lanes]
    for i in range(parts):
        out_ref[:, i * lanes : (i + 1) * lanes] = turn_ref[i].astype(BF)


def filter_grad(cross, back):
    segments, _, size, cols = cross.shape
    lanes = min(128, cols)
    return pl.pallas_call(
        filter_grad_kernel,
        out_shape=jax.ShapeDtypeStruct((segments * size, cols), BF),
        scratch_shapes=[pltpu.VMEM((cols // lanes, segments * size, lanes), F32)],
        compiler_params=PARAMS,
    )(cross, back)


def in_order(recv, a, slot, cols, turn):
    for e in range(2):
        turn[pl.ds(e, turn.shape[0] // 2, stride=2)] = recv[a, slot, e, :, cols].astype(F32)
    return turn[...]


def tap_kernel(tap_count, recv_hbm, qkv_hbm, x_hbm, g_hbm, halo_ref, short_ref, head_ref,
               recv_buf, kv_buf, x_buf, g_buf, ext_ref, turn_ref, load_sem):
    n, rows, channels = g_buf.shape
    half = rows // 2
    lanes = ext_ref.shape[-1]

    def loads(c):
        chunk = chunk_at(c, channels)
        return [
            pltpu.make_async_copy(recv_hbm.at[c], recv_buf.at[c], load_sem.at[0, c]),
            pltpu.make_async_copy(qkv_hbm.at[1:, :, chunk], kv_buf.at[c], load_sem.at[1, c]),
            pltpu.make_async_copy(x_hbm.at[:, :, chunk], x_buf.at[c], load_sem.at[2, c]),
            pltpu.make_async_copy(g_hbm.at[:, chunk], g_buf.at[c], load_sem.at[3, c]),
        ]

    for c in range(n):
        for copy in loads(c):
            copy.start()

    def one_chunk(c, carry):
        for copy in loads(c):
            copy.wait()

        def body(cols):
            wide = pl.ds(pl.multiple_of(c * channels + cols.start, lanes), lanes)
            short, heads = {}, [[], [], []]
            for slot in range(2):
                here = slice(slot * half, (slot + 1) * half)
                conv, gate = (in_order(recv_buf.at[c], a, slot, cols, turn_ref.at[slot * 2 + a]) for a in range(2))
                key, value = (kv_buf[c, j, here, cols].astype(F32) for j in range(2))
                g = g_buf[c, here, cols].astype(F32)
                grads = ((g * conv).astype(BF).astype(F32), gate * value, gate * key)
                for j in range(3):
                    ext = ext_ref.at[slot * 3 + j]
                    ext[:RIM] = halo_ref[j, :, wide].astype(F32)[slot * RIM : (slot + 1) * RIM]
                    ext[RIM:] = x_buf[c, j, here, cols].astype(F32)
                    heads[j].append(grads[j][:RIM])
                    for s in range(tap_count):
                        term = grads[j] * ext[RIM - s : RIM - s + half]
                        term = jnp.sum(term.reshape(half // 8, 8, lanes), 0)
                        short[s, j] = term if slot == 0 else short[s, j] + term
            lines = [jnp.sum(short[s, j], 0, keepdims=True) for s in range(tap_count) for j in range(3)]
            lines.append(jnp.zeros((short_ref.shape[1] - len(lines), lanes), F32))
            short_ref[c, :, cols] = jnp.concatenate(lines, 0).astype(BF)
            for j in range(3):
                head_ref[j, :, wide] = jnp.concatenate(heads[j], 0).astype(BF)

        each_part(channels, body)
        return carry

    lax.fori_loop(0, n, one_chunk, 0)


def tap_grads(recv, qkv, x, g, halo, tap_count):
    rows, width = g.shape
    n, channels = recv.shape[0], recv.shape[-1]
    lanes = min(128, channels)
    short_rows = -(-tap_count * 3 // 16) * 16
    return pl.pallas_call(
        functools.partial(tap_kernel, tap_count),
        in_specs=[ANYWHERE] * 4 + [VECTOR],
        out_specs=[VECTOR, VECTOR],
        out_shape=[
            jax.ShapeDtypeStruct((n, short_rows, channels), BF),
            jax.ShapeDtypeStruct((3, 2 * RIM, width), BF),
        ],
        scratch_shapes=[
            pltpu.VMEM(recv.shape, BF),
            pltpu.VMEM((n, 2, rows, channels), BF),
            pltpu.VMEM((n, 3, rows, channels), BF),
            pltpu.VMEM((n, rows, channels), BF),
            pltpu.VMEM((6, rows // 2 + RIM, lanes), F32),
            pltpu.VMEM((4, rows // 2, lanes), F32),
            pltpu.SemaphoreType.DMA((4, n)),
        ],
        compiler_params=PARAMS,
    )(recv, qkv, x, g, halo)


def finish_kernel(tap_count, recv_hbm, qkv_hbm, g_hbm, w_ref, mixed_hbm, grad_hbm, open_ref,
                  recv_buf, qkv_buf, g_buf, mixed_buf, grad_buf, gf_ref, turn_ref, load_sem, store_sem):
    n, rows, channels = g_buf.shape
    half = rows // 2
    lanes = gf_ref.shape[-1]

    def loads(c):
        chunk = chunk_at(c, channels)
        return [
            pltpu.make_async_copy(recv_hbm.at[c], recv_buf.at[c], load_sem.at[0, c]),
            pltpu.make_async_copy(qkv_hbm.at[:, :, chunk], qkv_buf.at[c], load_sem.at[1, c]),
            pltpu.make_async_copy(g_hbm.at[:, chunk], g_buf.at[c], load_sem.at[2, c]),
        ]

    def stores(c):
        chunk = chunk_at(c, channels)
        return [
            pltpu.make_async_copy(mixed_buf.at[c], mixed_hbm.at[:, chunk], store_sem.at[0, c]),
            pltpu.make_async_copy(grad_buf.at[c], grad_hbm.at[:, :, chunk], store_sem.at[1, c]),
        ]

    for c in range(n):
        for copy in loads(c):
            copy.start()

    def one_chunk(c, carry):
        for copy in loads(c):
            copy.wait()

        def body(cols):
            wide = pl.ds(pl.multiple_of(c * channels + cols.start, lanes), lanes)
            rest = [[], [], []]
            for slot in range(2):
                here = slice(slot * half, (slot + 1) * half)
                conv, gate = (in_order(recv_buf.at[c], a, slot, cols, turn_ref.at[slot * 2 + a]) for a in range(2))
                query, key, value = (qkv_buf[c, j, here, cols].astype(F32) for j in range(3))
                g = g_buf[c, here, cols].astype(F32)
                mixed_buf[c, here, cols] = (query * conv).astype(BF)
                grads = ((g * conv).astype(BF).astype(F32), gate * value, gate * key)
                for j in range(3):
                    gf = gf_ref.at[slot * 3 + j]
                    gf[:half] = grads[j]
                    gf[half:] = jnp.zeros((RIM, lanes), F32)
                    total = jnp.zeros((half, lanes), F32)
                    for s in range(tap_count):
                        total = total + w_ref[s * 3 + j : s * 3 + j + 1, wide] * gf[s : s + half]
                    grad_buf[c, j, here, cols] = total.astype(BF)
                    rest[j].append(total[half - RIM :])
            for j in range(3):
                open_ref[j, :, wide] = jnp.concatenate(rest[j], 0)

        each_part(channels, body)
        for copy in stores(c):
            copy.start()
        return carry

    lax.fori_loop(0, n, one_chunk, 0)
    for c in range(n):
        for copy in stores(c):
            copy.wait()


def finish(recv, qkv, g, taps, tap_count):
    rows, width = g.shape
    n, channels = recv.shape[0], recv.shape[-1]
    lanes = min(128, channels)
    return pl.pallas_call(
        functools.partial(finish_kernel, tap_count),
        in_specs=[ANYWHERE] * 3 + [VECTOR],
        out_specs=[ANYWHERE, ANYWHERE, VECTOR],
        out_shape=[
            jax.ShapeDtypeStruct((rows, width), BF),
            jax.ShapeDtypeStruct((3, rows, width), BF),
            jax.ShapeDtypeStruct((3, 2 * RIM, width), F32),
        ],
        scratch_shapes=[
            pltpu.VMEM(recv.shape, BF),
            pltpu.VMEM((n, 3, rows, channels), BF),
            pltpu.VMEM((n, rows, channels), BF),
            pltpu.VMEM((n, rows, channels), BF),
            pltpu.VMEM((n, 3, rows, channels), BF),
            pltpu.VMEM((6, rows // 2 + RIM, lanes), F32),
            pltpu.VMEM((4, rows // 2, lanes), F32),
            pltpu.SemaphoreType.DMA((3, n)),
            pltpu.SemaphoreType.DMA((2, n)),
        ],
        compiler_params=PARAMS,
    )(recv, qkv, g, taps)


def close_kernel(tap_count, old_hbm, open_ref, after_ref, w_ref, grad_hbm, tile_buf, gf_ref, load_sem, store_sem):
    rows = grad_hbm.shape[1]
    tile = 2 * RIM

    def moves(slot):
        place = grad_hbm.at[:, (slot + 1) * rows // 2 - tile : (slot + 1) * rows // 2]
        return (pltpu.make_async_copy(place, tile_buf.at[slot], load_sem.at[slot]),
                pltpu.make_async_copy(tile_buf.at[slot], place, store_sem.at[slot]))

    for slot in range(2):
        moves(slot)[0].start()
    for slot in range(2):
        moves(slot)[0].wait()

    def body(cols):
        for slot in range(2):
            rim = slice(slot * RIM, (slot + 1) * RIM)
            for j in range(3):
                gf = gf_ref.at[slot * 3 + j]
                gf[:RIM] = jnp.zeros((RIM, gf.shape[1]), F32)
                gf[RIM:] = after_ref[j, :, cols].astype(F32)[rim]
                total = open_ref[j, rim, cols]
                for s in range(1, tap_count):
                    total = total + w_ref[s * 3 + j : s * 3 + j + 1, cols] * gf[s : s + RIM]
                kept = tile_buf[slot, j, :, cols].astype(F32)[: tile - RIM]
                tile_buf[slot, j, :, cols] = jnp.concatenate([kept, total], 0).astype(BF)

    each_part(grad_hbm.shape[2], body)
    for slot in range(2):
        moves(slot)[1].start()
    for slot in range(2):
        moves(slot)[1].wait()


def close(grads, opened, after, taps, tap_count):
    width = grads.shape[2]
    return pl.pallas_call(
        functools.partial(close_kernel, tap_count),
        in_specs=[ANYWHERE, VECTOR, VECTOR, VECTOR],
        out_specs=ANYWHERE,
        out_shape=jax.ShapeDtypeStruct(grads.shape, BF),
        scratch_shapes=[
            pltpu.VMEM((2, 3, 2 * RIM, width), BF),
            pltpu.VMEM((6, 2 * RIM, min(128, width)), F32),
            pltpu.SemaphoreType.DMA((2,)),
            pltpu.SemaphoreType.DMA((2,)),
        ],
        input_output_aliases={0: 0},
        compiler_params=PARAMS,
    )(grads, opened, after, taps)


def sum_over_dp(value, keep):
    hop = 1
    total = value
    while hop < lax.axis_size("dp"):
        sent = total.astype(keep)
        other = lax.ppermute(sent, "dp", [(j, j ^ hop) for j in range(lax.axis_size("dp"))])
        total = sent.astype(F32) + other.astype(F32)
        hop *= 2
    return total


def on_device(feats, grad_y, short_w, long_h, block_order):
    n = lax.axis_size("ctx")
    me = lax.axis_index("ctx")
    _, _, rows, width = feats.shape
    half = rows // 2
    channels = width // n
    tap_count = short_w.shape[0]
    table, back = (jnp.asarray(t) for t in dft_tables(min(rows * n, 1024)))
    taps = short_w.reshape(tap_count * 3, width)
    x, g = feats[0], grad_y[0]
    numbers = jnp.arange(2 * n, dtype=jnp.int32)
    flip = jnp.sum(jnp.where(numbers == 2 * me, block_order, 0)) != me
    upward = [(j, j + 1) for j in range(n - 1)]
    downward = [(j + 1, j) for j in range(n - 1)]
    last = me == n - 1

    def by_slot(low, high):
        return jnp.concatenate([jnp.where(flip, high, low), jnp.where(flip, low, high)], 1)

    tails = x[:, half - RIM : half], x[:, rows - RIM :]
    low_tail, high_tail = jnp.where(flip, tails[1], tails[0]), jnp.where(flip, tails[0], tails[1])
    low_before = lax.ppermute(low_tail, "ctx", upward)
    high_before = lax.ppermute(high_tail, "ctx", downward)
    halo = by_slot(low_before, jnp.where(last, low_tail, high_before))
    hops = sorted(range(1, n), key=lambda s: abs(s - n // 2)) + [0]
    chunks = (me + jnp.asarray(hops, jnp.int32)) % n
    sends, qkv = featurize(chunks, x, g, halo, taps, tap_count)
    recvs = [lax.ppermute(sent, "ctx", [(j, (j + s) % n) for j in range(n)]) if s else sent
             for s, sent in zip(hops, sends)]
    long_h, qkv = lax.optimization_barrier((long_h, qkv))
    filt = filter_spectrum(long_h, table)
    origins = (me - jnp.asarray(hops, jnp.int32) + n) % n
    wanted = 2 * jnp.repeat(origins, 2) + numbers % 2
    come_from = jnp.sum(jnp.where(wanted[:, None] == numbers[None, :], block_order[None, :], 0), 1).astype(jnp.int32)
    out, cross = long_conv(come_from, block_order, recvs, filt, table, back)

    returned = lax.all_to_all(out, "ctx", 0, 0, tiled=True)
    filter_sum = sum_over_dp(filter_grad(cross, back), BF)
    returned, filter_sum = lax.optimization_barrier((returned, filter_sum))
    short, heads = tap_grads(returned, qkv, x, g, halo, tap_count)
    pieces = lax.all_to_all(short, "ctx", 0, 0, tiled=True)
    heads = heads[:, :RIM], heads[:, RIM:]
    low_head, high_head = jnp.where(flip, heads[1], heads[0]), jnp.where(flip, heads[0], heads[1])
    low_after = lax.ppermute(low_head, "ctx", downward)
    high_after = lax.ppermute(high_head, "ctx", upward)
    after = by_slot(jnp.where(last, high_head, low_after), high_after)
    mixed, grads, opened = finish(returned, qkv, g, taps, tap_count)
    grads = close(grads, opened, after, taps, tap_count)
    short_sum = sum_over_dp(jnp.sum(pieces.astype(F32), 0)[: tap_count * 3], F32)
    return mixed[None], grads[None], short_sum.reshape(tap_count, 3, channels), filter_sum


def solution(mesh):
    placed = (P("dp", None, "ctx", None), P("dp", "ctx", None), P(), P(None, "ctx"), P())
    return jax.shard_map(
        on_device,
        mesh=mesh,
        in_specs=placed,
        out_specs=(
            P("dp", "ctx", None),
            P("dp", None, "ctx", None),
            P(None, None, "ctx"),
            P(None, "ctx"),
        ),
        check_vma=False,
    )
```

time: 645 us -> 181 us (0.28); the launches traced: 635 us -> 181 us
  matrix products: 196 us -> 0 us
  other arithmetic: 128 us -> 9.49 us
  local copies, waits for them, and re-layouts: 108 us -> 5.15 us
  waiting for transfers between devices: 152 us -> 71.8 us
  Pallas kernels: 0 us -> 54.4 us
  starting transfers between devices: 22.6 us -> 38.1 us
  between operations: 14.8 us -> 1.56 us
  blocking collectives: 12.9 us -> 0 us
    dot_general x36 -> x0, matrix products: 196 us -> none  [the longest x12 76.2 us: along_lanes(): jnp.einsum('cbh,bd->cdh', left, table, precision=HIGH, preferred_element_...]
    all_to_all x4 -> x2, waiting for transfers between devices: 152 us -> 12.5 us  [the longest x1 12.5 us: on_device(): returned = lax.all_to_all(out, 'ctx', 0, 0, tiled=True)]
    unnamed x3 -> x0, other arithmetic: 83.8 us -> none
    ppermute x0 -> x15, waiting for transfers between devices: none -> 59.3 us  [the longest x4 27.7 us: sum_over_dp(): lax.ppermute(sent, 'dp', [(j, j ^ hop) for j in range(lax.axis_size('dp'))])]
    pallas_call x0 -> x7, Pallas kernels: none -> 54.4 us  [the longest x1 13.1 us: long_conv(): pl.pallas_call(functools.partial(long_kernel, min(256, freqs), n), in_spe...]
    unnamed x82 -> x24, local copies, waits for them, and re-layouts: 34.3 us -> 4.05 us
    ppermute x0 -> x15, starting transfers between devices: none -> 29.1 us  [the longest x7 13.3 us: on_device(): lax.ppermute(sent, 'ctx', [(j, (j + s) % n) for j in range(n)])]
    reshape x12 -> x2, local copies, waits for them, and re-layouts: 22.4 us -> 0.94 us  [the longest x1 0.92 us: on_device(): taps = short_w.reshape(tap_count * 3, width)]
  transfers between devices with their start and end apart: 7 -> 17, of which waited for: 3 -> 9; matrix products, arithmetic and copies ran while one was open for 36% -> 5% of each run, Pallas kernels for 0% -> 14%
where the time goes in v2:
time: 181 us
  waiting for transfers between devices  71.8 us (40%)
  Pallas kernels  54.4 us (30%)
  starting transfers between devices  38.1 us (21%)
  other arithmetic  9.49 us (5%)
  local copies, waits for them, and re-layouts  5.15 us (3%)
    ppermute x4, waiting for transfers between devices, sum_over_dp(): lax.ppermute(sent, 'dp', [(j, j ^ hop) for j in range(lax.axis_size('dp'))])  27.7 us
    ppermute x7, waiting for transfers between devices, on_device(): lax.ppermute(sent, 'ctx', [(j, (j + s) % n) for j in range(n)])  26.9 us
    ppermute x7, starting transfers between devices, on_device(): lax.ppermute(sent, 'ctx', [(j, (j + s) % n) for j in range(n)])  13.3 us
    pallas_call x1, Pallas kernels, long_conv(): pl.pallas_call(functools.partial(long_kernel, min(256, freqs), n), in_spe...  13.1 us
    all_to_all x1, waiting for transfers between devices, on_device(): returned = lax.all_to_all(out, 'ctx', 0, 0, tiled=True)  12.5 us
    pallas_call x1, Pallas kernels, finish(): pl.pallas_call(functools.partial(finish_kernel, tap_count), in_specs=[ANY...  8.75 us
    pallas_call x1, Pallas kernels, tap_grads(): pl.pallas_call(functools.partial(tap_kernel, tap_count), in_specs=[ANYWHE...  8.55 us
    pallas_call x1, Pallas kernels, featurize(): pl.pallas_call(functools.partial(featurize_kernel, tap_count, pieces), in...  8.15 us
  transfers between devices with their start and end apart: 17, of which 9 were waited for; matrix products, arithmetic and copies ran while one was open for 5% of the time, Pallas kernels for 14%

profile of v2, /device:TPU:0, one launch (start us, length us, event | category | flops | bytes accessed | tf_op | source)
XLA Modules:
  0.0 180.5 jit_solution(15888261818759147333)
XLA Ops:
  0.7 1.3 fusion.3
  3.7 1.3 collective-permute-start
  5.0 5.5 %collective-permute-start.1 = (bf16[3,8,4096]{2,1,0:T(8,128)(2,1)S(1)}, bf16[3,8,4096]{2,1,0:T(8,128)(2,1)S(1)}, u32[]{:S(2)}, u32[]{:S(2)}) collective-permute-start(bf16[3,8,4096]{2,1,0:T(8,128)(2,1)S(1)} %get-tuple-element.53), channel_id=1, source_target_pairs={{0,1},{1,2},{2,3},{3,4},{4,5},{5,6},{6,7},{8,9},{9,10},{10,11},{11... | collective-permute-start | bytes 589832 | tf_op jit(solution)/shard_map/ppermute | solution.py:613
  10.5 1.2 copy.17
  13.4 4.4 %collective-permute-done.1 = bf16[3,8,4096]{2,1,0:T(8,128)(2,1)S(1)} collective-permute-done((bf16[3,8,4096]{2,1,0:T(8,128)(2,1)S(1)}, bf16[3,8,4096]{2,1,0:T(8,128)(2,1)S(1)}, u32[]{:S(2)}, u32[]{:S(2)}) %collective-permute-start.1) | collective-permute-done | bytes 196640 | tf_op jit(solution)/shard_map/ppermute | solution.py:613
  18.7 8.2 %shard_map.120 = (bf16[2,2,2,32,512]{4,3,2,1,0:T(8,128)(2,1)}, bf16[2,2,2,32,512]{4,3,2,1,0:T(8,128)(2,1)}, bf16[2,2,2,32,512]{4,3,2,1,0:T(8,128)(2,1)}, bf16[2,...) custom-call(s32[8]{0:T(128)} %get-tuple-element.60.where_ref, ...), custom_call_target="tpu_custom_call" | custom-call | tf_op jit(solution)/shard_map/pallas_call | solution.py:115
  26.8 2.7 %collective-permute-start.2 = (bf16[2,2,2,32,512]{4,3,2,1,0:T(8,128)(2,1)}, bf16[2,2,2,32,512]{4,3,2,1,0:T(8,128)(2,1)S(1)}, u32[]{:S(2)}, u32[]{:S(2)}) collective-permute-start(bf16[2,2,2,32,512]{4,3,2,1,0:T(8,128)(2,1)} %get-tuple-element.26), channel_id=1, source_target_pairs={{0,4},{1,5},{2,6},{3,7},{4,0},{5,1},{6,2},{7,3},{8,12},{9,13},{10,... | collective-permute-start | bytes 786440 | tf_op jit(solution)/shard_map/ppermute | solution.py:619
  30.6 2.9 %collective-permute-start.4 = (bf16[2,2,2,32,512]{4,3,2,1,0:T(8,128)(2,1)}, bf16[2,2,2,32,512]{4,3,2,1,0:T(8,128)(2,1)S(1)}, u32[]{:S(2)}, u32[]{:S(2)}) collective-permute-start(bf16[2,2,2,32,512]{4,3,2,1,0:T(8,128)(2,1)} %get-tuple-element.28), channel_id=1, source_target_pairs={{0,5},{1,6},{2,7},{3,0},{4,1},{5,2},{6,3},{7,4},{8,13},{9,14},{10,... | collective-permute-start | bytes 786440 | tf_op jit(solution)/shard_map/ppermute | solution.py:619
  33.5 1.6 collective-permute-start.5
  35.1 2.3 %collective-permute-start.6 = (bf16[2,2,2,32,512]{4,3,2,1,0:T(8,128)(2,1)}, bf16[2,2,2,32,512]{4,3,2,1,0:T(8,128)(2,1)S(1)}, u32[]{:S(2)}, u32[]{:S(2)}) collective-permute-start(bf16[2,2,2,32,512]{4,3,2,1,0:T(8,128)(2,1)} %get-tuple-element.30), channel_id=1, source_target_pairs={{0,6},{1,7},{2,0},{3,1},{4,2},{5,3},{6,4},{7,5},{8,14},{9,15},{10,... | collective-permute-start | bytes 786440 | tf_op jit(solution)/shard_map/ppermute | solution.py:619
  37.3 22.4 %collective-permute-done.2.refs_0_ = bf16[2,2,2,32,512]{4,3,2,1,0:T(8,128)(2,1)S(1)} collective-permute-done((bf16[2,2,2,32,512]{4,3,2,1,0:T(8,128)(2,1)}, bf16[2,2,2,32,512]{4,3,2,1,0:T(8,128)(2,1)S(1)}, u32[]{:S(2)}, u32[]{:S(2)}) %collective-permute-start.2) | collective-permute-done | bytes 262176 | tf_op jit(solution)/shard_map/ppermute | solution.py:619
  59.8 1.8 collective-permute-done.3.refs_1_
  61.6 2.9 %collective-permute-start.8 = (bf16[2,2,2,32,512]{4,3,2,1,0:T(8,128)(2,1)}, bf16[2,2,2,32,512]{4,3,2,1,0:T(8,128)(2,1)S(1)}, u32[]{:S(2)}, u32[]{:S(2)}) collective-permute-start(bf16[2,2,2,32,512]{4,3,2,1,0:T(8,128)(2,1)} %get-tuple-element.32), channel_id=1, source_target_pairs={{0,7},{1,0},{2,1},{3,2},{4,3},{5,4},{6,5},{7,6},{8,15},{9,8},{10,9... | collective-permute-start | bytes 786440 | tf_op jit(solution)/shard_map/ppermute | solution.py:619
  65.2 6.6 %shard_map.121.filt_hbm = f32[1,4,512,512]{3,2,1,0:T(8,128)} custom-call(f32[1024,512]{1,0:T(8,128)} %h_ref, bf16[2,1024,512]{2,1,0:T(8,128)(2,1)} %constant.51.clone.table_ref.table_hbm), custom_call_target="tpu_custom_call" | custom-call | tf_op jit(solution)/shard_map/pallas_call | solution.py:199
  71.9 2.7 %collective-permute-done.7.refs_5_ = bf16[2,2,2,32,512]{4,3,2,1,0:T(8,128)(2,1)S(1)} collective-permute-done((bf16[2,2,2,32,512]{4,3,2,1,0:T(8,128)(2,1)}, bf16[2,2,2,32,512]{4,3,2,1,0:T(8,128)(2,1)S(1)}, u32[]{:S(2)}, u32[]{:S(2)}) %collective-permute-start.7) | collective-permute-done | bytes 262176 | tf_op jit(solution)/shard_map/ppermute | solution.py:619
  75.4 13.1 %shard_map.122 = (bf16[8,2,2,2,32,512]{5,4,3,2,1,0:T(8,128)(2,1)}, bf16[1,2,1024,512]{3,2,1,0:T(8,128)(2,1)}) custom-call(s32[16]{0:T(128)} %select_reduce_fusion.from_ref, s32[16]{0:T(128)} %to_ref.1, f32[1,4,512,512]{3,2,1,0:T(8,128)} %shard_map.121.filt_hbm, bf16[2,1024,512]{2,1,0:T(8,128)(2,1)} %constant.51.clone.table_ref.table_hbm, ...), custom_call_target="tpu_custom_call" | custom-call | tf_op jit(solution)/shard_map/pallas_call | solution.py:306
  88.5 5.4 %all-to-all-start = ((bf16[8,2,2,2,32,512]{5,4,3,2,1,0:T(8,128)(2,1)}), bf16[8,2,2,2,32,512]{5,4,3,2,1,0:T(8,128)(2,1)S(1)}, u32[]{:S(2)}, u32[]{:S(2)}) async-start(bf16[8,2,2,2,32,512]{5,4,3,2,1,0:T(8,128)(2,1)} %get-tuple-element.34), calls=%async_computation | async-start | bytes 4194304 | tf_op jit(solution)/shard_map/all_to_all | solution.py:628
  93.9 4.6 %shard_map.123 = bf16[1024,512]{1,0:T(8,128)(2,1)} custom-call(bf16[1,2,1024,512]{3,2,1,0:T(8,128)(2,1)} %get-tuple-element.35.cross_ref, bf16[2,512,1024]{2,1,0:T(8,128)(2,1)} %constant.52.clone.back_hbm.back_ref), custom_call_target="tpu_custom_call" | custom-call | tf_op jit(solution)/shard_map/pallas_call | solution.py:346
  98.5 2.9 %collective-permute-done.9 = bf16[1024,512]{1,0:T(8,128)(2,1)S(1)} collective-permute-done((bf16[1024,512]{1,0:T(8,128)(2,1)}, bf16[1024,512]{1,0:T(8,128)(2,1)S(1)}, u32[]{:S(2)}, u32[]{:S(2)}) %collective-permute-start.9) | collective-permute-done | bytes 1048608 | tf_op jit(solution)/shard_map/ppermute | solution.py:586
  101.4 1.5 add_convert_fusion
  102.9 1.6 collective-permute-start.10
  104.5 23.7 %collective-permute-done.10 = bf16[1024,512]{1,0:T(8,128)(2,1)S(1)} collective-permute-done((bf16[1024,512]{1,0:T(8,128)(2,1)S(1)}, bf16[1024,512]{1,0:T(8,128)(2,1)S(1)}, u32[]{:S(2)}, u32[]{:S(2)}) %collective-permute-start.10) | collective-permute-done | bytes 1048608 | tf_op jit(solution)/shard_map/ppermute | solution.py:586
  128.2 1.6 convert_add_fusion
  129.8 12.5 %all-to-all-done.recv_hbm = bf16[8,2,2,2,32,512]{5,4,3,2,1,0:T(8,128)(2,1)S(1)} async-done(((bf16[8,2,2,2,32,512]{5,4,3,2,1,0:T(8,128)(2,1)}), bf16[8,2,2,2,32,512]{5,4,3,2,1,0:T(8,128)(2,1)S(1)}, u32[]{:S(2)}, u32[]{:S(2)}) %all-to-all-start) | async-done | bytes 2097184 | tf_op jit(solution)/shard_map/all_to_all | solution.py:628
  142.3 1.4 copy-done
  143.7 8.6 %shard_map.125 = (bf16[8,32,512]{2,1,0:T(8,128)(2,1)}, bf16[3,16,4096]{2,1,0:T(8,128)(2,1)}) custom-call(bf16[8,2,2,2,32,512]{5,4,3,2,1,0:T(8,128)(2,1)} %copy-done, bf16[3,128,4096]{2,1,0:T(8,128)(2,1)} %get-tuple-element.37.qkv_hbm, bf16[3,128,4096]{2,1,0:T(8,128)(2,1)} %bitcast.6, bf16[128,4096]{1,0:T(8,128)(2,1)} %bitcast.8, ...), custom_call_target="tpu_custom_call" | custom-call | tf_op jit(solution)/shard_map/pallas_call | solution.py:418
  152.2 3.6 %all-to-all-start.1 = ((bf16[8,32,512]{2,1,0:T(8,128)(2,1)}), bf16[8,32,512]{2,1,0:T(8,128)(2,1)S(1)}, u32[]{:S(2)}, u32[]{:S(2)}) async-start(bf16[8,32,512]{2,1,0:T(8,128)(2,1)} %get-tuple-element.42), calls=%async_computation.1 | async-start | bytes 524288 | tf_op jit(solution)/shard_map/all_to_all | solution.py:632
  156.9 1.3 collective-permute-start.12
  158.2 4.6 %collective-permute-start.11 = (bf16[3,8,4096]{2,1,0:T(8,128)(2,1)S(1)}, bf16[3,8,4096]{2,1,0:T(8,128)(2,1)S(1)}, u32[]{:S(2)}, u32[]{:S(2)}) collective-permute-start(bf16[3,8,4096]{2,1,0:T(8,128)(2,1)S(1)} %get-tuple-element.59), channel_id=1, source_target_pairs={{0,1},{1,2},{2,3},{3,4},{4,5},{5,6},{6,7},{8,9},{9,10},{10,11},{11... | collective-permute-start | bytes 589832 | tf_op jit(solution)/shard_map/ppermute | solution.py:636
  162.8 8.7 %shard_map.124 = (bf16[128,4096]{1,0:T(8,128)(2,1)}, bf16[3,128,4096]{2,1,0:T(8,128)(2,1)}, f32[3,16,4096]{2,1,0:T(8,128)}) custom-call(bf16[8,2,2,2,32,512]{5,4,3,2,1,0:T(8,128)(2,1)} %copy-done, bf16[3,128,4096]{2,1,0:T(8,128)(2,1)} %get-tuple-element.37.qkv_hbm, bf16[128,4096]{1,0:T(8,128)(2,1)} %bitcast.9, f32[21,4096]{1,0:T(8,128)} %reshape.33.w_ref), custom_call_target="tpu_custom_call" | custom-call | tf_op jit(solution)/shard_map/pallas_call | solution.py:505
  172.9 1.5 collective-permute-start.14
  175.3 4.5 %shard_map.126 = bf16[3,128,4096]{2,1,0:T(8,128)(2,1)} custom-call(bf16[3,128,4096]{2,1,0:T(8,128)(2,1)} %get-tuple-element.39.old_hbm, f32[3,16,4096]{2,1,0:T(8,128)} %get-tuple-element.40.open_ref, bf16[3,16,4096]{2,1,0:T(8,128)(2,1)} %pad_maximum_fusion.1.after_ref, f32[21,4096]{1,0:T(8,128)} %reshape.33.w_ref), custom_call_target="tpu_custom_call", output_to_operand_aliasing={{}: (0, {})} | custom-call | tf_op jit(solution)/shard_map/pallas_call | solution.py:565
  (53 shorter events, 10.0 us)
Async XLA Ops:
  0.6 12.0 %copy-start.9 = (s32[8]{0:T(128)S(1)}, s32[8]{0:T(128)}, u32[]{:S(2)}) copy-start(s32[8]{0:T(128)} %constant.56) | copy-start | bytes 100
  0.6 12.0 %copy-start.10 = (s32[8]{0:T(128)S(1)}, s32[8]{0:T(128)}, u32[]{:S(2)}) copy-start(s32[8]{0:T(128)} %constant.53.clone) | copy-start | bytes 100
  3.7 9.8 %collective-permute-start = (bf16[3,8,4096]{2,1,0:T(8,128)(2,1)S(1)}, bf16[3,8,4096]{2,1,0:T(8,128)(2,1)S(1)}, u32[]{:S(2)}, u32[]{:S(2)}) collective-permute-start(bf16[3,8,4096]{2,1,0:T(8,128)(2,1)S(1)} %get-tuple-element.52), channel_id=1, source_target_pairs={{1,0},{2,1},{3,2},{4,3},{5,4},{6,5},{7,6},{9,8},{10,9},{11,10},{12... | collective-permute-start | bytes 589832 | tf_op jit(solution)/shard_map/ppermute | solution.py:614
  5.0 12.8 %collective-permute-start.1 = (bf16[3,8,4096]{2,1,0:T(8,128)(2,1)S(1)}, bf16[3,8,4096]{2,1,0:T(8,128)(2,1)S(1)}, u32[]{:S(2)}, u32[]{:S(2)}) collective-permute-start(bf16[3,8,4096]{2,1,0:T(8,128)(2,1)S(1)} %get-tuple-element.53), channel_id=1, source_target_pairs={{0,1},{1,2},{2,3},{3,4},{4,5},{5,6},{6,7},{8,9},{9,10},{10,11},{11... | collective-permute-start | bytes 589832 | tf_op jit(solution)/shard_map/ppermute | solution.py:613
  18.7 45.9 %copy-start.8 = (s32[16]{0:T(128)S(1)}, s32[16]{0:T(128)}, u32[]{:S(2)}) copy-start(s32[16]{0:T(128)} %to_ref.1) | copy-start | bytes 196
  26.8 33.0 %collective-permute-start.2 = (bf16[2,2,2,32,512]{4,3,2,1,0:T(8,128)(2,1)}, bf16[2,2,2,32,512]{4,3,2,1,0:T(8,128)(2,1)S(1)}, u32[]{:S(2)}, u32[]{:S(2)}) collective-permute-start(bf16[2,2,2,32,512]{4,3,2,1,0:T(8,128)(2,1)} %get-tuple-element.26), channel_id=1, source_target_pairs={{0,4},{1,5},{2,6},{3,7},{4,0},{5,1},{6,2},{7,3},{8,12},{9,13},{10,... | collective-permute-start | bytes 786440 | tf_op jit(solution)/shard_map/ppermute | solution.py:619
  29.5 32.1 %collective-permute-start.3 = (bf16[2,2,2,32,512]{4,3,2,1,0:T(8,128)(2,1)}, bf16[2,2,2,32,512]{4,3,2,1,0:T(8,128)(2,1)S(1)}, u32[]{:S(2)}, u32[]{:S(2)}) collective-permute-start(bf16[2,2,2,32,512]{4,3,2,1,0:T(8,128)(2,1)} %get-tuple-element.27), channel_id=1, source_target_pairs={{0,3},{1,4},{2,5},{3,6},{4,7},{5,0},{6,1},{7,2},{8,11},{9,12},{10,... | collective-permute-start | bytes 786440 | tf_op jit(solution)/shard_map/ppermute | solution.py:619
  30.6 41.3 %collective-permute-start.4 = (bf16[2,2,2,32,512]{4,3,2,1,0:T(8,128)(2,1)}, bf16[2,2,2,32,512]{4,3,2,1,0:T(8,128)(2,1)S(1)}, u32[]{:S(2)}, u32[]{:S(2)}) collective-permute-start(bf16[2,2,2,32,512]{4,3,2,1,0:T(8,128)(2,1)} %get-tuple-element.28), channel_id=1, source_target_pairs={{0,5},{1,6},{2,7},{3,0},{4,1},{5,2},{6,3},{7,4},{8,13},{9,14},{10,... | collective-permute-start | bytes 786440 | tf_op jit(solution)/shard_map/ppermute | solution.py:619
  33.5 38.4 %collective-permute-start.5 = (bf16[2,2,2,32,512]{4,3,2,1,0:T(8,128)(2,1)}, bf16[2,2,2,32,512]{4,3,2,1,0:T(8,128)(2,1)S(1)}, u32[]{:S(2)}, u32[]{:S(2)}) collective-permute-start(bf16[2,2,2,32,512]{4,3,2,1,0:T(8,128)(2,1)} %get-tuple-element.29), channel_id=1, source_target_pairs={{0,2},{1,3},{2,4},{3,5},{4,6},{5,7},{6,0},{7,1},{8,10},{9,11},{10,... | collective-permute-start | bytes 786440 | tf_op jit(solution)/shard_map/ppermute | solution.py:619
  35.1 36.8 %collective-permute-start.6 = (bf16[2,2,2,32,512]{4,3,2,1,0:T(8,128)(2,1)}, bf16[2,2,2,32,512]{4,3,2,1,0:T(8,128)(2,1)S(1)}, u32[]{:S(2)}, u32[]{:S(2)}) collective-permute-start(bf16[2,2,2,32,512]{4,3,2,1,0:T(8,128)(2,1)} %get-tuple-element.30), channel_id=1, source_target_pairs={{0,6},{1,7},{2,0},{3,1},{4,2},{5,3},{6,4},{7,5},{8,14},{9,15},{10,... | collective-permute-start | bytes 786440 | tf_op jit(solution)/shard_map/ppermute | solution.py:619
  59.8 12.1 %copy-start.1 = (bf16[2,2,2,32,512]{4,3,2,1,0:T(8,128)(2,1)}, bf16[2,2,2,32,512]{4,3,2,1,0:T(8,128)(2,1)S(1)}, u32[]{:S(2)}) copy-start(bf16[2,2,2,32,512]{4,3,2,1,0:T(8,128)(2,1)S(1)} %collective-permute-done.2.refs_0_) | copy-start | bytes 786436
  59.8 14.8 %collective-permute-start.7 = (bf16[2,2,2,32,512]{4,3,2,1,0:T(8,128)(2,1)}, bf16[2,2,2,32,512]{4,3,2,1,0:T(8,128)(2,1)S(1)}, u32[]{:S(2)}, u32[]{:S(2)}) collective-permute-start(bf16[2,2,2,32,512]{4,3,2,1,0:T(8,128)(2,1)} %get-tuple-element.31), channel_id=1, source_target_pairs={{0,1},{1,2},{2,3},{3,4},{4,5},{5,6},{6,7},{7,0},{8,9},{9,10},{10,1... | collective-permute-start | bytes 786440 | tf_op jit(solution)/shard_map/ppermute | solution.py:619
  61.6 10.3 %copy-start.2 = (bf16[2,2,2,32,512]{4,3,2,1,0:T(8,128)(2,1)}, bf16[2,2,2,32,512]{4,3,2,1,0:T(8,128)(2,1)S(1)}, u32[]{:S(2)}) copy-start(bf16[2,2,2,32,512]{4,3,2,1,0:T(8,128)(2,1)S(1)} %collective-permute-done.3.refs_1_) | copy-start | bytes 786436
  61.6 13.0 %collective-permute-start.8 = (bf16[2,2,2,32,512]{4,3,2,1,0:T(8,128)(2,1)}, bf16[2,2,2,32,512]{4,3,2,1,0:T(8,128)(2,1)S(1)}, u32[]{:S(2)}, u32[]{:S(2)}) collective-permute-start(bf16[2,2,2,32,512]{4,3,2,1,0:T(8,128)(2,1)} %get-tuple-element.32), channel_id=1, source_target_pairs={{0,7},{1,0},{2,1},{3,2},{4,3},{5,4},{6,5},{7,6},{8,15},{9,8},{10,9... | collective-permute-start | bytes 786440 | tf_op jit(solution)/shard_map/ppermute | solution.py:619
  71.9 2.7 %copy-start.3 = (bf16[2,2,2,32,512]{4,3,2,1,0:T(8,128)(2,1)}, bf16[2,2,2,32,512]{4,3,2,1,0:T(8,128)(2,1)S(1)}, u32[]{:S(2)}) copy-start(bf16[2,2,2,32,512]{4,3,2,1,0:T(8,128)(2,1)S(1)} %collective-permute-done.4.refs_2_) | copy-start | bytes 786436
  71.9 2.7 %copy-start.4 = (bf16[2,2,2,32,512]{4,3,2,1,0:T(8,128)(2,1)}, bf16[2,2,2,32,512]{4,3,2,1,0:T(8,128)(2,1)S(1)}, u32[]{:S(2)}) copy-start(bf16[2,2,2,32,512]{4,3,2,1,0:T(8,128)(2,1)S(1)} %collective-permute-done.5.refs_3_) | copy-start | bytes 786436
  71.9 2.7 %copy-start.5 = (bf16[2,2,2,32,512]{4,3,2,1,0:T(8,128)(2,1)}, bf16[2,2,2,32,512]{4,3,2,1,0:T(8,128)(2,1)S(1)}, u32[]{:S(2)}) copy-start(bf16[2,2,2,32,512]{4,3,2,1,0:T(8,128)(2,1)S(1)} %collective-permute-done.6.refs_4_) | copy-start | bytes 786436
  74.6 0.7 copy-start.6
  74.6 0.8 copy-start.7
  88.5 53.8 %all-to-all-start = ((bf16[8,2,2,2,32,512]{5,4,3,2,1,0:T(8,128)(2,1)}), bf16[8,2,2,2,32,512]{5,4,3,2,1,0:T(8,128)(2,1)S(1)}, u32[]{:S(2)}, u32[]{:S(2)}) async-start(bf16[8,2,2,2,32,512]{5,4,3,2,1,0:T(8,128)(2,1)} %get-tuple-element.34), calls=%async_computation | async-start | bytes 4194304 | tf_op jit(solution)/shard_map/all_to_all | solution.py:628
  98.5 2.9 %collective-permute-start.9 = (bf16[1024,512]{1,0:T(8,128)(2,1)}, bf16[1024,512]{1,0:T(8,128)(2,1)S(1)}, u32[]{:S(2)}, u32[]{:S(2)}) collective-permute-start(bf16[1024,512]{1,0:T(8,128)(2,1)} %shard_map.123), channel_id=1, source_target_pairs={{0,8},{8,0},{16,24},{24,16},{1,9},{9,1},{17,25},{25,17},{2,10},{10... | collective-permute-start | bytes 3145736 | tf_op jit(solution)/shard_map/ppermute | solution.py:586
  102.9 25.3 %collective-permute-start.10 = (bf16[1024,512]{1,0:T(8,128)(2,1)S(1)}, bf16[1024,512]{1,0:T(8,128)(2,1)S(1)}, u32[]{:S(2)}, u32[]{:S(2)}) collective-permute-start(bf16[1024,512]{1,0:T(8,128)(2,1)S(1)} %add_convert_fusion), channel_id=1, source_target_pairs={{0,16},{8,24},{16,0},{24,8},{1,17},{9,25},{17,1},{25,9},{2,18},{10... | collective-permute-start | bytes 3145736 | tf_op jit(solution)/shard_map/ppermute | solution.py:586
  142.3 1.4 copy-start
  152.2 19.3 %all-to-all-start.1 = ((bf16[8,32,512]{2,1,0:T(8,128)(2,1)}), bf16[8,32,512]{2,1,0:T(8,128)(2,1)S(1)}, u32[]{:S(2)}, u32[]{:S(2)}) async-start(bf16[8,32,512]{2,1,0:T(8,128)(2,1)} %get-tuple-element.42), calls=%async_computation.1 | async-start | bytes 524288 | tf_op jit(solution)/shard_map/all_to_all | solution.py:632
  156.9 14.8 %collective-permute-start.12 = (bf16[3,8,4096]{2,1,0:T(8,128)(2,1)S(1)}, bf16[3,8,4096]{2,1,0:T(8,128)(2,1)S(1)}, u32[]{:S(2)}, u32[]{:S(2)}) collective-permute-start(bf16[3,8,4096]{2,1,0:T(8,128)(2,1)S(1)} %get-tuple-element.58), channel_id=1, source_target_pairs={{1,0},{2,1},{3,2},{4,3},{5,4},{6,5},{7,6},{9,8},{10,9},{11,10},{12... | collective-permute-start | bytes 589832 | tf_op jit(solution)/shard_map/ppermute | solution.py:635
  158.2 13.5 %collective-permute-start.11 = (bf16[3,8,4096]{2,1,0:T(8,128)(2,1)S(1)}, bf16[3,8,4096]{2,1,0:T(8,128)(2,1)S(1)}, u32[]{:S(2)}, u32[]{:S(2)}) collective-permute-start(bf16[3,8,4096]{2,1,0:T(8,128)(2,1)S(1)} %get-tuple-element.59), channel_id=1, source_target_pairs={{0,1},{1,2},{2,3},{3,4},{4,5},{5,6},{6,7},{8,9},{9,10},{10,11},{11... | collective-permute-start | bytes 589832 | tf_op jit(solution)/shard_map/ppermute | solution.py:636
  171.6 1.3 collective-permute-start.13
  172.9 6.9 %collective-permute-start.14 = (f32[21,512]{1,0:T(8,128)S(1)}, f32[21,512]{1,0:T(8,128)S(1)}, u32[]{:S(2)}, u32[]{:S(2)}) collective-permute-start(f32[21,512]{1,0:T(8,128)S(1)} %slice_add_fusion), channel_id=1, source_target_pairs={{0,16},{8,24},{16,0},{24,8},{1,17},{9,25},{17,1},{25,9},{2,18},{10... | collective-permute-start | bytes 129032 | tf_op jit(solution)/shard_map/ppermute | solution.py:586

commit v3 on v2

--- a/solution.py
+++ b/solution.py
@@ -12,7 +12,8 @@
 BF = jnp.bfloat16
 F32 = jnp.float32
 RIM = 8
-PARAMS = pltpu.CompilerParams(vmem_limit_bytes=56 * 1024 * 1024)
+STRIP = 16
+PARAMS = pltpu.CompilerParams(vmem_limit_bytes=63 * 1024 * 1024)
 ANYWHERE = pl.BlockSpec(memory_space=pltpu.HBM)
 VECTOR = pl.BlockSpec(memory_space=pltpu.VMEM)
 SCALAR = pl.BlockSpec(memory_space=pltpu.SMEM)
@@ -206,7 +207,7 @@
 
 def long_kernel(tile, n, from_ref, to_ref, filt_hbm, table_hbm, back_hbm, *refs):
     recvs_hbm, send_hbm, cross_hbm = refs[:n], refs[n], refs[n + 1]
-    filt_ref, table_ref, back_ref, seq_ref, spec_ref, time_ref, cross_ref, const_sem, in_sem, out_sem = refs[n + 2 :]
+    filt_ref, table_ref, back_ref, seq_ref, spec_ref, time_ref, cross_ref, mat_ref, const_sem, in_sem, out_sem = refs[n + 2 :]
     _, _, _, quarter, cols = recvs_hbm[0].shape
     _, size, freqs = table_ref.shape
     segments = filt_ref.shape[0]
@@ -236,11 +237,20 @@
     constants[0].start()
     for copy in arrivals:
         copy.start()
+    constants[1].start()
+    constants[2].start()
     constants[0].wait()
     for copy in arrivals:
         copy.wait()
-    constants[1].start()
-    constants[2].start()
+
+    for a in range(2):
+        for s in range(segments):
+            span = slice(s * freqs, (s + 1) * freqs)
+            for e in range(2):
+                for step in range(size // tile):
+                    at = slice(step * tile, (step + 1) * tile)
+                    mat_ref[a, s, e, at] = dot(table_ref[e, at], seq_ref[a, e, span])
+    constants[1].wait()
 
     def total(terms):
         out = terms[0]
@@ -248,38 +258,43 @@
             out = tuple(x + y for x, y in zip(out, term))
         return out
 
-    for step in range(freqs // tile):
-        at = slice(step * tile, (step + 1) * tile)
-        up = slice(freqs + step * tile, freqs + (step + 1) * tile)
-        first = first_row((tile, cols)) if step == 0 else None
-        sign = (1 - 2 * (lax.broadcasted_iota(jnp.int32, (tile, cols), 0) % 2)).astype(F32) if segments > 1 else None
-        spectra = [[], []]
-        for s in range(segments):
-            span = slice(s * freqs, (s + 1) * freqs)
-            for a in range(2):
-                parts = [(dot(table_ref[e, at], seq_ref[a, e, span]), dot(table_ref[e, up], seq_ref[a, e, span]))
-                         for e in range(2)]
-                spectra[a].append(unite(*parts, first))
-        if step == 0:
-            constants[1].wait()
-        filt = [[filt_ref[s, i, at] for i in range(4)] for s in range(segments)]
-        gated, back = spectra
+    def wrapped(values, p, other, sign):
+        if not 0 <= other < segments:
+            return values[p]
+        return tuple(x + sign * y for x, y in zip(values[p], values[other]))
+
+    def combine(row, lane, first):
+        at, up = pl.ds(row, STRIP), pl.ds(freqs + row, STRIP)
+        shape = (STRIP, lane.stop - lane.start)
+        sign = (1 - 2 * (lax.broadcasted_iota(jnp.int32, shape, 0) % 2)).astype(F32) if segments > 1 else None
+        first = first_row(shape) if first else None
+        gated, back = (
+            [unite(*((mat_ref[a, s, e, at, lane], mat_ref[a, s, e, up, lane]) for e in range(2)), first)
+             for s in range(segments)]
+            for a in range(2)
+        )
+        filt = [[filt_ref[s, i, at, lane] for i in range(4)] for s in range(segments)]
         conv = [total([times(gated[p - d], filt[d], first, 1) for d in range(p + 1)]) for p in range(segments)]
         grad = [total([times(back[u], filt[u - p], first, -1) for u in range(p, segments)]) for p in range(segments)]
         cross = [total([times(back[u], gated[u - p], first, -1) for u in range(p, segments)]) for p in range(segments)]
-
-        def wrapped(values, p, other):
-            if not 0 <= other < segments:
-                return values[p]
-            return tuple(x + sign * y for x, y in zip(values[p], values[other]))
-
         for p in range(segments):
-            for a, value in enumerate((wrapped(conv, p, p - 1), wrapped(grad, p, p + 1))):
+            for a, value in enumerate((wrapped(conv, p, p - 1, sign), wrapped(grad, p, p + 1, sign))):
                 for i, part in enumerate(divide(value, first)):
-                    spec_ref[a, i // 2, p, at if i % 2 == 0 else up] = part.astype(BF)
-            for i, part in enumerate(divide(wrapped(cross, p, p + 1), first)):
-                cross_ref[p, i // 2, at if i % 2 == 0 else up] = (part * (1.0 / size)).astype(BF)
-
+                    spec_ref[a, i // 2, p, at if i % 2 == 0 else up, lane] = part.astype(BF)
+            for i, part in enumerate(divide(wrapped(cross, p, p + 1, sign), first)):
+                cross_ref[p, i // 2, at if i % 2 == 0 else up, lane] = (part * (1.0 / size)).astype(BF)
+
+    lanes = min(128, cols)
+    groups = [slice(part * lanes, (part + 1) * lanes) for part in range(cols // lanes)]
+
+    def strip(i, carry):
+        for lane in groups:
+            combine(pl.multiple_of(i * STRIP, STRIP), lane, False)
+        return carry
+
+    for lane in groups:
+        combine(0, lane, True)
+    lax.fori_loop(1, freqs // STRIP, strip, 0)
     cross_copy = pltpu.make_async_copy(cross_ref, cross_hbm, const_sem.at[0])
     cross_copy.start()
     constants[2].wait()
@@ -319,6 +334,7 @@
             pltpu.VMEM((2, 2, segments, size, cols), BF),
             pltpu.VMEM((2, 2, segments * freqs, cols), BF),
             pltpu.VMEM((segments, 2, size, cols), BF),
+            pltpu.VMEM((2, segments, 2, size, cols), F32),
             pltpu.SemaphoreType.DMA((3,)),
             pltpu.SemaphoreType.DMA((2, n)),
             pltpu.SemaphoreType.DMA((2, 2, n)),

time: 181 us -> 179 us (0.989)
  local copies, waits for them, and re-layouts: 5.15 us -> 2.99 us
    unnamed x24 -> x14, local copies, waits for them, and re-layouts: 4.05 us -> 1.9 us
where the time goes in v3:
time: 179 us; the launch traced here: 178 us
  waiting for transfers between devices  71.9 us (40%)
  Pallas kernels  53.1 us (30%)
  starting transfers between devices  38.4 us (21%)
  other arithmetic  10.2 us (6%)
  local copies, waits for them, and re-layouts  2.99 us (2%)
    ppermute x4, waiting for transfers between devices, sum_over_dp(): lax.ppermute(sent, 'dp', [(j, j ^ hop) for j in range(lax.axis_size('dp'))])  27.7 us
    ppermute x7, waiting for transfers between devices, on_device(): lax.ppermute(sent, 'ctx', [(j, (j + s) % n) for j in range(n)])  26.9 us
    ppermute x7, starting transfers between devices, on_device(): lax.ppermute(sent, 'ctx', [(j, (j + s) % n) for j in range(n)])  13.4 us
    all_to_all x1, waiting for transfers between devices, on_device(): returned = lax.all_to_all(out, 'ctx', 0, 0, tiled=True)  12.6 us
    pallas_call x1, Pallas kernels, long_conv(): pl.pallas_call(functools.partial(long_kernel, min(256, freqs), n), in_spe...  12 us
    pallas_call x1, Pallas kernels, finish(): pl.pallas_call(functools.partial(finish_kernel, tap_count), in_specs=[ANY...  8.74 us
    pallas_call x1, Pallas kernels, tap_grads(): pl.pallas_call(functools.partial(tap_kernel, tap_count), in_specs=[ANYWHE...  8.55 us
    pallas_call x1, Pallas kernels, featurize(): pl.pallas_call(functools.partial(featurize_kernel, tap_count, pieces), in...  8.11 us
  transfers between devices with their start and end apart: 17, of which 9 were waited for; matrix products, arithmetic and copies ran while one was open for 5% of the time, Pallas kernels for 14%

profile of v3, /device:TPU:0, one launch (start us, length us, event | category | flops | bytes accessed | tf_op | source)
XLA Modules:
  0.0 178.1 jit_solution(17427161642017103464)
XLA Ops:
  0.7 1.3 fusion.3
  3.7 1.3 collective-permute-start
  5.0 5.5 %collective-permute-start.1 = (bf16[3,8,4096]{2,1,0:T(8,128)(2,1)S(1)}, bf16[3,8,4096]{2,1,0:T(8,128)(2,1)S(1)}, u32[]{:S(2)}, u32[]{:S(2)}) collective-permute-start(bf16[3,8,4096]{2,1,0:T(8,128)(2,1)S(1)} %get-tuple-element.53), channel_id=1, source_target_pairs={{0,1},{1,2},{2,3},{3,4},{4,5},{5,6},{6,7},{8,9},{9,10},{10,11},{11... | collective-permute-start | bytes 589832 | tf_op jit(solution)/shard_map/ppermute | solution.py:629
  10.5 1.2 copy.17
  13.4 4.4 %collective-permute-done.1 = bf16[3,8,4096]{2,1,0:T(8,128)(2,1)S(1)} collective-permute-done((bf16[3,8,4096]{2,1,0:T(8,128)(2,1)S(1)}, bf16[3,8,4096]{2,1,0:T(8,128)(2,1)S(1)}, u32[]{:S(2)}, u32[]{:S(2)}) %collective-permute-start.1) | collective-permute-done | bytes 196640 | tf_op jit(solution)/shard_map/ppermute | solution.py:629
  18.7 8.1 %shard_map.120 = (bf16[2,2,2,32,512]{4,3,2,1,0:T(8,128)(2,1)}, bf16[2,2,2,32,512]{4,3,2,1,0:T(8,128)(2,1)}, bf16[2,2,2,32,512]{4,3,2,1,0:T(8,128)(2,1)}, bf16[2,...) custom-call(s32[8]{0:T(128)} %get-tuple-element.60.where_ref, ...), custom_call_target="tpu_custom_call" | custom-call | tf_op jit(solution)/shard_map/pallas_call | solution.py:116
  26.8 2.8 %collective-permute-start.2 = (bf16[2,2,2,32,512]{4,3,2,1,0:T(8,128)(2,1)}, bf16[2,2,2,32,512]{4,3,2,1,0:T(8,128)(2,1)S(1)}, u32[]{:S(2)}, u32[]{:S(2)}) collective-permute-start(bf16[2,2,2,32,512]{4,3,2,1,0:T(8,128)(2,1)} %get-tuple-element.26), channel_id=1, source_target_pairs={{0,4},{1,5},{2,6},{3,7},{4,0},{5,1},{6,2},{7,3},{8,12},{9,13},{10,... | collective-permute-start | bytes 786440 | tf_op jit(solution)/shard_map/ppermute | solution.py:635
  30.6 3.0 %collective-permute-start.4 = (bf16[2,2,2,32,512]{4,3,2,1,0:T(8,128)(2,1)}, bf16[2,2,2,32,512]{4,3,2,1,0:T(8,128)(2,1)S(1)}, u32[]{:S(2)}, u32[]{:S(2)}) collective-permute-start(bf16[2,2,2,32,512]{4,3,2,1,0:T(8,128)(2,1)} %get-tuple-element.28), channel_id=1, source_target_pairs={{0,5},{1,6},{2,7},{3,0},{4,1},{5,2},{6,3},{7,4},{8,13},{9,14},{10,... | collective-permute-start | bytes 786440 | tf_op jit(solution)/shard_map/ppermute | solution.py:635
  33.5 1.5 collective-permute-start.5
  35.1 2.3 %collective-permute-start.6 = (bf16[2,2,2,32,512]{4,3,2,1,0:T(8,128)(2,1)}, bf16[2,2,2,32,512]{4,3,2,1,0:T(8,128)(2,1)}, u32[]{:S(2)}, u32[]{:S(2)}) collective-permute-start(bf16[2,2,2,32,512]{4,3,2,1,0:T(8,128)(2,1)} %get-tuple-element.30), channel_id=1, source_target_pairs={{0,6},{1,7},{2,0},{3,1},{4,2},{5,3},{6,4},{7,5},{8,14},{9,15},{10,... | collective-permute-start | bytes 786440 | tf_op jit(solution)/shard_map/ppermute | solution.py:635
  37.4 22.4 %collective-permute-done.2.refs_0_ = bf16[2,2,2,32,512]{4,3,2,1,0:T(8,128)(2,1)S(1)} collective-permute-done((bf16[2,2,2,32,512]{4,3,2,1,0:T(8,128)(2,1)}, bf16[2,2,2,32,512]{4,3,2,1,0:T(8,128)(2,1)S(1)}, u32[]{:S(2)}, u32[]{:S(2)}) %collective-permute-start.2) | collective-permute-done | bytes 262176 | tf_op jit(solution)/shard_map/ppermute | solution.py:635
  59.7 1.8 %collective-permute-done.3.refs_1_ = bf16[2,2,2,32,512]{4,3,2,1,0:T(8,128)(2,1)S(1)} collective-permute-done((bf16[2,2,2,32,512]{4,3,2,1,0:T(8,128)(2,1)}, bf16[2,2,2,32,512]{4,3,2,1,0:T(8,128)(2,1)S(1)}, u32[]{:S(2)}, u32[]{:S(2)}) %collective-permute-start.3) | collective-permute-done | bytes 262176 | tf_op jit(solution)/shard_map/ppermute | solution.py:635
  61.6 2.9 %collective-permute-start.8 = (bf16[2,2,2,32,512]{4,3,2,1,0:T(8,128)(2,1)}, bf16[2,2,2,32,512]{4,3,2,1,0:T(8,128)(2,1)}, u32[]{:S(2)}, u32[]{:S(2)}) collective-permute-start(bf16[2,2,2,32,512]{4,3,2,1,0:T(8,128)(2,1)} %get-tuple-element.32), channel_id=1, source_target_pairs={{0,7},{1,0},{2,1},{3,2},{4,3},{5,4},{6,5},{7,6},{8,15},{9,8},{10,9... | collective-permute-start | bytes 786440 | tf_op jit(solution)/shard_map/ppermute | solution.py:635
  65.2 6.6 %shard_map.121.filt_hbm = f32[1,4,512,512]{3,2,1,0:T(8,128)} custom-call(f32[1024,512]{1,0:T(8,128)} %h_ref, bf16[2,1024,512]{2,1,0:T(8,128)(2,1)} %constant.51.clone.table_ref.table_hbm), custom_call_target="tpu_custom_call" | custom-call | tf_op jit(solution)/shard_map/pallas_call | solution.py:200
  71.8 2.7 %collective-permute-done.7.refs_5_ = bf16[2,2,2,32,512]{4,3,2,1,0:T(8,128)(2,1)} collective-permute-done((bf16[2,2,2,32,512]{4,3,2,1,0:T(8,128)(2,1)}, bf16[2,2,2,32,512]{4,3,2,1,0:T(8,128)(2,1)}, u32[]{:S(2)}, u32[]{:S(2)}) %collective-permute-start.7) | collective-permute-done | bytes 262176 | tf_op jit(solution)/shard_map/ppermute | solution.py:635
  74.6 12.0 %shard_map.122 = (bf16[8,2,2,2,32,512]{5,4,3,2,1,0:T(8,128)(2,1)}, bf16[1,2,1024,512]{3,2,1,0:T(8,128)(2,1)}) custom-call(s32[16]{0:T(128)} %select_reduce_fusion.from_ref, s32[16]{0:T(128)} %to_ref.1, f32[1,4,512,512]{3,2,1,0:T(8,128)} %shard_map.121.filt_hbm, bf16[2,1024,512]{2,1,0:T(8,128)(2,1)} %constant.51.clone.table_ref.table_hbm, ...), custom_call_target="tpu_custom_call" | custom-call | tf_op jit(solution)/shard_map/pallas_call | solution.py:321
  86.5 5.6 %all-to-all-start = ((bf16[8,2,2,2,32,512]{5,4,3,2,1,0:T(8,128)(2,1)}), bf16[8,2,2,2,32,512]{5,4,3,2,1,0:T(8,128)(2,1)}, u32[]{:S(2)}, u32[]{:S(2)}) async-start(bf16[8,2,2,2,32,512]{5,4,3,2,1,0:T(8,128)(2,1)} %get-tuple-element.34), calls=%async_computation | async-start | bytes 4194304 | tf_op jit(solution)/shard_map/all_to_all | solution.py:644
  92.1 4.6 %shard_map.123 = bf16[1024,512]{1,0:T(8,128)(2,1)} custom-call(bf16[1,2,1024,512]{3,2,1,0:T(8,128)(2,1)} %get-tuple-element.35.cross_ref, bf16[2,512,1024]{2,1,0:T(8,128)(2,1)} %constant.52.clone.back_hbm.back_ref), custom_call_target="tpu_custom_call" | custom-call | tf_op jit(solution)/shard_map/pallas_call | solution.py:362
  96.7 2.9 %collective-permute-done.9 = bf16[1024,512]{1,0:T(8,128)(2,1)S(1)} collective-permute-done((bf16[1024,512]{1,0:T(8,128)(2,1)}, bf16[1024,512]{1,0:T(8,128)(2,1)S(1)}, u32[]{:S(2)}, u32[]{:S(2)}) %collective-permute-start.9) | collective-permute-done | bytes 1048608 | tf_op jit(solution)/shard_map/ppermute | solution.py:602
  99.6 1.5 add_convert_fusion
  101.1 1.6 collective-permute-start.10
  102.7 23.7 %collective-permute-done.10 = bf16[1024,512]{1,0:T(8,128)(2,1)S(1)} collective-permute-done((bf16[1024,512]{1,0:T(8,128)(2,1)S(1)}, bf16[1024,512]{1,0:T(8,128)(2,1)S(1)}, u32[]{:S(2)}, u32[]{:S(2)}) %collective-permute-start.10) | collective-permute-done | bytes 1048608 | tf_op jit(solution)/shard_map/ppermute | solution.py:602
  126.4 1.6 convert_add_fusion
  128.0 12.6 %all-to-all-done.recv_hbm = bf16[8,2,2,2,32,512]{5,4,3,2,1,0:T(8,128)(2,1)} async-done(((bf16[8,2,2,2,32,512]{5,4,3,2,1,0:T(8,128)(2,1)}), bf16[8,2,2,2,32,512]{5,4,3,2,1,0:T(8,128)(2,1)}, u32[]{:S(2)}, u32[]{:S(2)}) %all-to-all-start) | async-done | bytes 2097184 | tf_op jit(solution)/shard_map/all_to_all | solution.py:644
  140.6 8.6 %shard_map.125 = (bf16[8,32,512]{2,1,0:T(8,128)(2,1)}, bf16[3,16,4096]{2,1,0:T(8,128)(2,1)}) custom-call(bf16[8,2,2,2,32,512]{5,4,3,2,1,0:T(8,128)(2,1)} %all-to-all-done.recv_hbm, bf16[3,128,4096]{2,1,0:T(8,128)(2,1)} %get-tuple-element.37.qkv_hbm, bf16[3,128,4096]{2,1,0:T(8,128)(2,1)} %bitcast.6, bf16[128,4096]{1,0:T(8,128)(2,1)} %bitcast.8, ...), custom_call_target="tpu_custom_call" | custom-call | tf_op jit(solution)/shard_map/pallas_call | solution.py:434
  149.2 3.6 %all-to-all-start.1 = ((bf16[8,32,512]{2,1,0:T(8,128)(2,1)}), bf16[8,32,512]{2,1,0:T(8,128)(2,1)S(1)}, u32[]{:S(2)}, u32[]{:S(2)}) async-start(bf16[8,32,512]{2,1,0:T(8,128)(2,1)} %get-tuple-element.42), calls=%async_computation.1 | async-start | bytes 524288 | tf_op jit(solution)/shard_map/all_to_all | solution.py:648
  152.9 1.7 broadcast_select_fusion.4
  154.6 1.3 collective-permute-start.12
  155.9 4.6 %collective-permute-start.11 = (bf16[3,8,4096]{2,1,0:T(8,128)(2,1)S(1)}, bf16[3,8,4096]{2,1,0:T(8,128)(2,1)S(1)}, u32[]{:S(2)}, u32[]{:S(2)}) collective-permute-start(bf16[3,8,4096]{2,1,0:T(8,128)(2,1)S(1)} %get-tuple-element.59), channel_id=1, source_target_pairs={{0,1},{1,2},{2,3},{3,4},{4,5},{5,6},{6,7},{8,9},{9,10},{10,11},{11... | collective-permute-start | bytes 589832 | tf_op jit(solution)/shard_map/ppermute | solution.py:652
  160.4 8.7 %shard_map.124 = (bf16[128,4096]{1,0:T(8,128)(2,1)}, bf16[3,128,4096]{2,1,0:T(8,128)(2,1)}, f32[3,16,4096]{2,1,0:T(8,128)}) custom-call(bf16[8,2,2,2,32,512]{5,4,3,2,1,0:T(8,128)(2,1)} %all-to-all-done.recv_hbm, bf16[3,128,4096]{2,1,0:T(8,128)(2,1)} %get-tuple-element.37.qkv_hbm, bf16[128,4096]{1,0:T(8,128)(2,1)} %bitcast.9, f32[21,4096]{1,0:T(8,128)} %reshape.33.w_ref), custom_call_target="tpu_custom_call" | custom-call | tf_op jit(solution)/shard_map/pallas_call | solution.py:521
  170.6 1.6 collective-permute-start.14
  172.9 4.5 %shard_map.126 = bf16[3,128,4096]{2,1,0:T(8,128)(2,1)} custom-call(bf16[3,128,4096]{2,1,0:T(8,128)(2,1)} %get-tuple-element.39.old_hbm, f32[3,16,4096]{2,1,0:T(8,128)} %get-tuple-element.40.open_ref, bf16[3,16,4096]{2,1,0:T(8,128)(2,1)} %pad_maximum_fusion.1.after_ref, f32[21,4096]{1,0:T(8,128)} %reshape.33.w_ref), custom_call_target="tpu_custom_call", output_to_operand_aliasing={{}: (0, {})} | custom-call | tf_op jit(solution)/shard_map/pallas_call | solution.py:581
  (43 shorter events, 8.1 us)
Async XLA Ops:
  0.6 12.0 %copy-start.4 = (s32[8]{0:T(128)S(1)}, s32[8]{0:T(128)}, u32[]{:S(2)}) copy-start(s32[8]{0:T(128)} %constant.56) | copy-start | bytes 100
  0.6 12.0 %copy-start.5 = (s32[8]{0:T(128)S(1)}, s32[8]{0:T(128)}, u32[]{:S(2)}) copy-start(s32[8]{0:T(128)} %constant.53.clone) | copy-start | bytes 100
  3.7 9.8 %collective-permute-start = (bf16[3,8,4096]{2,1,0:T(8,128)(2,1)S(1)}, bf16[3,8,4096]{2,1,0:T(8,128)(2,1)S(1)}, u32[]{:S(2)}, u32[]{:S(2)}) collective-permute-start(bf16[3,8,4096]{2,1,0:T(8,128)(2,1)S(1)} %get-tuple-element.52), channel_id=1, source_target_pairs={{1,0},{2,1},{3,2},{4,3},{5,4},{6,5},{7,6},{9,8},{10,9},{11,10},{12... | collective-permute-start | bytes 589832 | tf_op jit(solution)/shard_map/ppermute | solution.py:630
  5.0 12.8 %collective-permute-start.1 = (bf16[3,8,4096]{2,1,0:T(8,128)(2,1)S(1)}, bf16[3,8,4096]{2,1,0:T(8,128)(2,1)S(1)}, u32[]{:S(2)}, u32[]{:S(2)}) collective-permute-start(bf16[3,8,4096]{2,1,0:T(8,128)(2,1)S(1)} %get-tuple-element.53), channel_id=1, source_target_pairs={{0,1},{1,2},{2,3},{3,4},{4,5},{5,6},{6,7},{8,9},{9,10},{10,11},{11... | collective-permute-start | bytes 589832 | tf_op jit(solution)/shard_map/ppermute | solution.py:629
  18.7 45.8 %copy-start.3 = (s32[16]{0:T(128)S(1)}, s32[16]{0:T(128)}, u32[]{:S(2)}) copy-start(s32[16]{0:T(128)} %to_ref.1) | copy-start | bytes 196
  26.8 33.0 %collective-permute-start.2 = (bf16[2,2,2,32,512]{4,3,2,1,0:T(8,128)(2,1)}, bf16[2,2,2,32,512]{4,3,2,1,0:T(8,128)(2,1)S(1)}, u32[]{:S(2)}, u32[]{:S(2)}) collective-permute-start(bf16[2,2,2,32,512]{4,3,2,1,0:T(8,128)(2,1)} %get-tuple-element.26), channel_id=1, source_target_pairs={{0,4},{1,5},{2,6},{3,7},{4,0},{5,1},{6,2},{7,3},{8,12},{9,13},{10,... | collective-permute-start | bytes 786440 | tf_op jit(solution)/shard_map/ppermute | solution.py:635
  29.6 32.0 %collective-permute-start.3 = (bf16[2,2,2,32,512]{4,3,2,1,0:T(8,128)(2,1)}, bf16[2,2,2,32,512]{4,3,2,1,0:T(8,128)(2,1)S(1)}, u32[]{:S(2)}, u32[]{:S(2)}) collective-permute-start(bf16[2,2,2,32,512]{4,3,2,1,0:T(8,128)(2,1)} %get-tuple-element.27), channel_id=1, source_target_pairs={{0,3},{1,4},{2,5},{3,6},{4,7},{5,0},{6,1},{7,2},{8,11},{9,12},{10,... | collective-permute-start | bytes 786440 | tf_op jit(solution)/shard_map/ppermute | solution.py:635
  30.6 41.2 %collective-permute-start.4 = (bf16[2,2,2,32,512]{4,3,2,1,0:T(8,128)(2,1)}, bf16[2,2,2,32,512]{4,3,2,1,0:T(8,128)(2,1)S(1)}, u32[]{:S(2)}, u32[]{:S(2)}) collective-permute-start(bf16[2,2,2,32,512]{4,3,2,1,0:T(8,128)(2,1)} %get-tuple-element.28), channel_id=1, source_target_pairs={{0,5},{1,6},{2,7},{3,0},{4,1},{5,2},{6,3},{7,4},{8,13},{9,14},{10,... | collective-permute-start | bytes 786440 | tf_op jit(solution)/shard_map/ppermute | solution.py:635
  33.5 38.3 %collective-permute-start.5 = (bf16[2,2,2,32,512]{4,3,2,1,0:T(8,128)(2,1)}, bf16[2,2,2,32,512]{4,3,2,1,0:T(8,128)(2,1)}, u32[]{:S(2)}, u32[]{:S(2)}) collective-permute-start(bf16[2,2,2,32,512]{4,3,2,1,0:T(8,128)(2,1)} %get-tuple-element.29), channel_id=1, source_target_pairs={{0,2},{1,3},{2,4},{3,5},{4,6},{5,7},{6,0},{7,1},{8,10},{9,11},{10,... | collective-permute-start | bytes 786440 | tf_op jit(solution)/shard_map/ppermute | solution.py:635
  35.1 36.7 %collective-permute-start.6 = (bf16[2,2,2,32,512]{4,3,2,1,0:T(8,128)(2,1)}, bf16[2,2,2,32,512]{4,3,2,1,0:T(8,128)(2,1)}, u32[]{:S(2)}, u32[]{:S(2)}) collective-permute-start(bf16[2,2,2,32,512]{4,3,2,1,0:T(8,128)(2,1)} %get-tuple-element.30), channel_id=1, source_target_pairs={{0,6},{1,7},{2,0},{3,1},{4,2},{5,3},{6,4},{7,5},{8,14},{9,15},{10,... | collective-permute-start | bytes 786440 | tf_op jit(solution)/shard_map/ppermute | solution.py:635
  59.7 12.1 %copy-start = (bf16[2,2,2,32,512]{4,3,2,1,0:T(8,128)(2,1)}, bf16[2,2,2,32,512]{4,3,2,1,0:T(8,128)(2,1)S(1)}, u32[]{:S(2)}) copy-start(bf16[2,2,2,32,512]{4,3,2,1,0:T(8,128)(2,1)S(1)} %collective-permute-done.2.refs_0_) | copy-start | bytes 786436
  59.7 14.8 %collective-permute-start.7 = (bf16[2,2,2,32,512]{4,3,2,1,0:T(8,128)(2,1)}, bf16[2,2,2,32,512]{4,3,2,1,0:T(8,128)(2,1)}, u32[]{:S(2)}, u32[]{:S(2)}) collective-permute-start(bf16[2,2,2,32,512]{4,3,2,1,0:T(8,128)(2,1)} %get-tuple-element.31), channel_id=1, source_target_pairs={{0,1},{1,2},{2,3},{3,4},{4,5},{5,6},{6,7},{7,0},{8,9},{9,10},{10,1... | collective-permute-start | bytes 786440 | tf_op jit(solution)/shard_map/ppermute | solution.py:635
  61.6 10.2 %copy-start.1 = (bf16[2,2,2,32,512]{4,3,2,1,0:T(8,128)(2,1)}, bf16[2,2,2,32,512]{4,3,2,1,0:T(8,128)(2,1)S(1)}, u32[]{:S(2)}) copy-start(bf16[2,2,2,32,512]{4,3,2,1,0:T(8,128)(2,1)S(1)} %collective-permute-done.3.refs_1_) | copy-start | bytes 786436
  61.6 13.0 %collective-permute-start.8 = (bf16[2,2,2,32,512]{4,3,2,1,0:T(8,128)(2,1)}, bf16[2,2,2,32,512]{4,3,2,1,0:T(8,128)(2,1)}, u32[]{:S(2)}, u32[]{:S(2)}) collective-permute-start(bf16[2,2,2,32,512]{4,3,2,1,0:T(8,128)(2,1)} %get-tuple-element.32), channel_id=1, source_target_pairs={{0,7},{1,0},{2,1},{3,2},{4,3},{5,4},{6,5},{7,6},{8,15},{9,8},{10,9... | collective-permute-start | bytes 786440 | tf_op jit(solution)/shard_map/ppermute | solution.py:635
  71.8 2.8 %copy-start.2 = (bf16[2,2,2,32,512]{4,3,2,1,0:T(8,128)(2,1)}, bf16[2,2,2,32,512]{4,3,2,1,0:T(8,128)(2,1)S(1)}, u32[]{:S(2)}) copy-start(bf16[2,2,2,32,512]{4,3,2,1,0:T(8,128)(2,1)S(1)} %collective-permute-done.4.refs_2_) | copy-start | bytes 786436
  86.5 54.1 %all-to-all-start = ((bf16[8,2,2,2,32,512]{5,4,3,2,1,0:T(8,128)(2,1)}), bf16[8,2,2,2,32,512]{5,4,3,2,1,0:T(8,128)(2,1)}, u32[]{:S(2)}, u32[]{:S(2)}) async-start(bf16[8,2,2,2,32,512]{5,4,3,2,1,0:T(8,128)(2,1)} %get-tuple-element.34), calls=%async_computation | async-start | bytes 4194304 | tf_op jit(solution)/shard_map/all_to_all | solution.py:644
  96.7 2.9 %collective-permute-start.9 = (bf16[1024,512]{1,0:T(8,128)(2,1)}, bf16[1024,512]{1,0:T(8,128)(2,1)S(1)}, u32[]{:S(2)}, u32[]{:S(2)}) collective-permute-start(bf16[1024,512]{1,0:T(8,128)(2,1)} %shard_map.123), channel_id=1, source_target_pairs={{0,8},{8,0},{16,24},{24,16},{1,9},{9,1},{17,25},{25,17},{2,10},{10... | collective-permute-start | bytes 3145736 | tf_op jit(solution)/shard_map/ppermute | solution.py:602
  101.1 25.3 %collective-permute-start.10 = (bf16[1024,512]{1,0:T(8,128)(2,1)S(1)}, bf16[1024,512]{1,0:T(8,128)(2,1)S(1)}, u32[]{:S(2)}, u32[]{:S(2)}) collective-permute-start(bf16[1024,512]{1,0:T(8,128)(2,1)S(1)} %add_convert_fusion), channel_id=1, source_target_pairs={{0,16},{8,24},{16,0},{24,8},{1,17},{9,25},{17,1},{25,9},{2,18},{10... | collective-permute-start | bytes 3145736 | tf_op jit(solution)/shard_map/ppermute | solution.py:602
  149.2 20.0 %all-to-all-start.1 = ((bf16[8,32,512]{2,1,0:T(8,128)(2,1)}), bf16[8,32,512]{2,1,0:T(8,128)(2,1)S(1)}, u32[]{:S(2)}, u32[]{:S(2)}) async-start(bf16[8,32,512]{2,1,0:T(8,128)(2,1)} %get-tuple-element.42), calls=%async_computation.1 | async-start | bytes 524288 | tf_op jit(solution)/shard_map/all_to_all | solution.py:648
  154.6 14.8 %collective-permute-start.12 = (bf16[3,8,4096]{2,1,0:T(8,128)(2,1)}, bf16[3,8,4096]{2,1,0:T(8,128)(2,1)S(1)}, u32[]{:S(2)}, u32[]{:S(2)}) collective-permute-start(bf16[3,8,4096]{2,1,0:T(8,128)(2,1)} %get-tuple-element.58), channel_id=1, source_target_pairs={{1,0},{2,1},{3,2},{4,3},{5,4},{6,5},{7,6},{9,8},{10,9},{11,10},{12... | collective-permute-start | bytes 589832 | tf_op jit(solution)/shard_map/ppermute | solution.py:651
  155.9 13.5 %collective-permute-start.11 = (bf16[3,8,4096]{2,1,0:T(8,128)(2,1)S(1)}, bf16[3,8,4096]{2,1,0:T(8,128)(2,1)S(1)}, u32[]{:S(2)}, u32[]{:S(2)}) collective-permute-start(bf16[3,8,4096]{2,1,0:T(8,128)(2,1)S(1)} %get-tuple-element.59), channel_id=1, source_target_pairs={{0,1},{1,2},{2,3},{3,4},{4,5},{5,6},{6,7},{8,9},{9,10},{10,11},{11... | collective-permute-start | bytes 589832 | tf_op jit(solution)/shard_map/ppermute | solution.py:652
  169.2 1.3 collective-permute-start.13
  170.6 6.9 %collective-permute-start.14 = (f32[21,512]{1,0:T(8,128)S(1)}, f32[21,512]{1,0:T(8,128)S(1)}, u32[]{:S(2)}, u32[]{:S(2)}) collective-permute-start(f32[21,512]{1,0:T(8,128)S(1)} %slice_add_fusion), channel_id=1, source_target_pairs={{0,16},{8,24},{16,0},{24,8},{1,17},{9,25},{17,1},{25,9},{2,18},{10... | collective-permute-start | bytes 129032 | tf_op jit(solution)/shard_map/ppermute | solution.py:602

commit v4 on v3

--- a/solution.py
+++ b/solution.py
@@ -13,6 +13,7 @@
 F32 = jnp.float32
 RIM = 8
 STRIP = 16
+UNROLL = 4
 PARAMS = pltpu.CompilerParams(vmem_limit_bytes=63 * 1024 * 1024)
 ANYWHERE = pl.BlockSpec(memory_space=pltpu.HBM)
 VECTOR = pl.BlockSpec(memory_space=pltpu.VMEM)
@@ -45,7 +46,7 @@
         body(pl.ds(pl.multiple_of(part * lanes, lanes), lanes))
         return carry
 
-    lax.fori_loop(0, width // lanes, step, 0)
+    lax.fori_loop(0, width // lanes, step, 0, unroll=min(UNROLL, width // lanes))
 
 
 def chunk_at(index, channels):
@@ -155,17 +156,14 @@
 
 
 def times(x, f, first, sign):
-    def add(a, b):
-        return a + b if sign > 0 else a - b
-
-    out = []
-    for i in (0, 2):
-        re = add(x[i] * f[i], -(x[i + 1] * f[i + 1]))
-        im = add(x[i + 1] * f[i], x[i] * f[i + 1])
-        out += [re, im]
+    def pair(x_re, x_im, f_re, f_im):
+        if sign > 0:
+            return x_re * f_re - x_im * f_im, x_im * f_re + x_re * f_im
+        return x_re * f_re + x_im * f_im, x_im * f_re - x_re * f_im
+
+    out = [*pair(x[0], x[1], f[0], f[1]), *pair(x[2], x[3], f[2], f[3])]
     if first is not None:
-        middle_re = add(x[1] * f[1], -(x[3] * f[3]))
-        middle_im = add(x[3] * f[1], x[1] * f[3])
+        middle_re, middle_im = pair(x[1], x[3], f[1], f[3])
         out = [
             jnp.where(first, 0.5 * (x[0] * f[0]), out[0]),
             jnp.where(first, middle_re, out[1]),
@@ -282,7 +280,7 @@
                 for i, part in enumerate(divide(value, first)):
                     spec_ref[a, i // 2, p, at if i % 2 == 0 else up, lane] = part.astype(BF)
             for i, part in enumerate(divide(wrapped(cross, p, p + 1, sign), first)):
-                cross_ref[p, i // 2, at if i % 2 == 0 else up, lane] = (part * (1.0 / size)).astype(BF)
+                cross_ref[p, i // 2, at if i % 2 == 0 else up, lane] = part.astype(BF)
 
     lanes = min(128, cols)
     groups = [slice(part * lanes, (part + 1) * lanes) for part in range(cols // lanes)]
@@ -349,7 +347,7 @@
     parts, _, lanes = turn_ref.shape
     for p in range(segments):
         for e in range(2):
-            value = dot(back_ref[e], cross_ref[p, e])
+            value = dot(back_ref[e], cross_ref[p, e]) * (1.0 / size)
             for i in range(parts):
                 turn_ref[i, pl.ds(p * size + e, freqs, stride=2)] = value[:, i * lanes : (i + 1) * lanes]
     for i in range(parts):
@@ -542,7 +540,13 @@
     )(recv, qkv, g, taps)
 
 
-def close_kernel(tap_count, old_hbm, open_ref, after_ref, w_ref, grad_hbm, tile_buf, gf_ref, load_sem, store_sem):
+def swapped(order_ref):
+    me = lax.axis_index("ctx")
+    return ((order_ref[2 * me] != me) != (me % 2 == 1)).astype(jnp.int32)
+
+
+def close_kernel(tap_count, order_ref, old_hbm, open_ref, inner_ref, outer_ref, own_ref, w_ref, grad_hbm,
+                 rim_ref, tile_buf, gf_ref, load_sem, store_sem):
     rows = grad_hbm.shape[1]
     tile = 2 * RIM
 
@@ -553,6 +557,10 @@
 
     for slot in range(2):
         moves(slot)[0].start()
+    swap = swapped(order_ref)
+    last = lax.axis_index("ctx") == lax.axis_size("ctx") - 1
+    rim_ref[swap] = inner_ref[...].astype(F32)
+    rim_ref[1 - swap] = jnp.where(last, own_ref[...].astype(F32), outer_ref[...].astype(F32))
     for slot in range(2):
         moves(slot)[0].wait()
 
@@ -562,7 +570,7 @@
             for j in range(3):
                 gf = gf_ref.at[slot * 3 + j]
                 gf[:RIM] = jnp.zeros((RIM, gf.shape[1]), F32)
-                gf[RIM:] = after_ref[j, :, cols].astype(F32)[rim]
+                gf[RIM:] = rim_ref[slot, j, :, cols]
                 total = open_ref[j, rim, cols]
                 for s in range(1, tap_count):
                     total = total + w_ref[s * 3 + j : s * 3 + j + 1, cols] * gf[s : s + RIM]
@@ -576,22 +584,23 @@
         moves(slot)[1].wait()
 
 
-def close(grads, opened, after, taps, tap_count):
+def close(order, grads, opened, inner, outer, own, taps, tap_count):
     width = grads.shape[2]
     return pl.pallas_call(
         functools.partial(close_kernel, tap_count),
-        in_specs=[ANYWHERE, VECTOR, VECTOR, VECTOR],
+        in_specs=[SCALAR, ANYWHERE] + [VECTOR] * 5,
         out_specs=ANYWHERE,
         out_shape=jax.ShapeDtypeStruct(grads.shape, BF),
         scratch_shapes=[
+            pltpu.VMEM((2, 3, RIM, width), F32),
             pltpu.VMEM((2, 3, 2 * RIM, width), BF),
             pltpu.VMEM((6, 2 * RIM, min(128, width)), F32),
             pltpu.SemaphoreType.DMA((2,)),
             pltpu.SemaphoreType.DMA((2,)),
         ],
-        input_output_aliases={0: 0},
+        input_output_aliases={1: 0},
         compiler_params=PARAMS,
-    )(grads, opened, after, taps)
+    )(order, grads, opened, inner, outer, own, taps)
 
 
 def sum_over_dp(value, keep):
@@ -617,18 +626,19 @@
     x, g = feats[0], grad_y[0]
     numbers = jnp.arange(2 * n, dtype=jnp.int32)
     flip = jnp.sum(jnp.where(numbers == 2 * me, block_order, 0)) != me
-    upward = [(j, j + 1) for j in range(n - 1)]
-    downward = [(j + 1, j) for j in range(n - 1)]
+    swap = flip != (me % 2 == 1)
     last = me == n - 1
 
-    def by_slot(low, high):
-        return jnp.concatenate([jnp.where(flip, high, low), jnp.where(flip, low, high)], 1)
+    def trade(inner, outer):
+        got_inner = lax.ppermute(inner, "ctx", [(j, j ^ 1) for j in range(n)])
+        got_outer = lax.ppermute(outer, "ctx", [(j, j + 1 if j % 2 else j - 1) for j in range(1, n - 1)])
+        return got_inner, got_outer
 
     tails = x[:, half - RIM : half], x[:, rows - RIM :]
-    low_tail, high_tail = jnp.where(flip, tails[1], tails[0]), jnp.where(flip, tails[0], tails[1])
-    low_before = lax.ppermute(low_tail, "ctx", upward)
-    high_before = lax.ppermute(high_tail, "ctx", downward)
-    halo = by_slot(low_before, jnp.where(last, low_tail, high_before))
+    own = jnp.where(swap, tails[0], tails[1])
+    inner, outer = trade(jnp.where(swap, tails[1], tails[0]), own)
+    outer = jnp.where(last, own, outer)
+    halo = jnp.concatenate([jnp.where(swap, inner, outer), jnp.where(swap, outer, inner)], 1)
     hops = sorted(range(1, n), key=lambda s: abs(s - n // 2)) + [0]
     chunks = (me + jnp.asarray(hops, jnp.int32)) % n
     sends, qkv = featurize(chunks, x, g, halo, taps, tap_count)
@@ -647,12 +657,11 @@
     short, heads = tap_grads(returned, qkv, x, g, halo, tap_count)
     pieces = lax.all_to_all(short, "ctx", 0, 0, tiled=True)
     heads = heads[:, :RIM], heads[:, RIM:]
-    low_head, high_head = jnp.where(flip, heads[1], heads[0]), jnp.where(flip, heads[0], heads[1])
-    low_after = lax.ppermute(low_head, "ctx", downward)
-    high_after = lax.ppermute(high_head, "ctx", upward)
-    after = by_slot(jnp.where(last, high_head, low_after), high_after)
+    own = jnp.where(swap, heads[1], heads[0])
+    inner, outer = trade(jnp.where(swap, heads[0], heads[1]), own)
     mixed, grads, opened = finish(returned, qkv, g, taps, tap_count)
-    grads = close(grads, opened, after, taps, tap_count)
+    pieces, inner, outer, opened = lax.optimization_barrier((pieces, inner, outer, opened))
+    grads = close(block_order, grads, opened, inner, outer, own, taps, tap_count)
     short_sum = sum_over_dp(jnp.sum(pieces.astype(F32), 0)[: tap_count * 3], F32)
     return mixed[None], grads[None], short_sum.reshape(tap_count, 3, channels), filter_sum
 

time: 179 us -> 171 us (0.955)
  starting transfers between devices: 38.4 us -> 35 us
  waiting for transfers between devices: 71.9 us -> 69.8 us
    ppermute x4, starting transfers between devices: 12.6 us -> 7 us  [the longest x2 5.01 us: trade(): got_inner = lax.ppermute(inner, 'ctx', [(j, j ^ 1) for j in range(n)])]
    ppermute x7, waiting for transfers between devices: 26.9 us -> 23.3 us  [on_device(): lax.ppermute(sent, 'ctx', [(j, (j + s) % n) for j in range(n)])]
    ppermute x7, starting transfers between devices: 13.4 us -> 16 us  [on_device(): lax.ppermute(sent, 'ctx', [(j, (j + s) % n) for j in range(n)])]
  transfers between devices with their start and end apart: 17 -> 17, of which waited for: 9 -> 7; matrix products, arithmetic and copies ran while one was open for 5% -> 5% of each run, Pallas kernels for 14% -> 14%
where the time goes in v4:
time: 171 us; the launch traced here: 170 us
  waiting for transfers between devices  69.8 us (41%)
  Pallas kernels  52.1 us (30%)
  starting transfers between devices  35 us (20%)
  other arithmetic  8.69 us (5%)
  local copies, waits for them, and re-layouts  3.01 us (2%)
    ppermute x4, waiting for transfers between devices, sum_over_dp(): lax.ppermute(sent, 'dp', [(j, j ^ hop) for j in range(lax.axis_size('dp'))])  27.8 us
    ppermute x7, waiting for transfers between devices, on_device(): lax.ppermute(sent, 'ctx', [(j, (j + s) % n) for j in range(n)])  23.3 us
    ppermute x7, starting transfers between devices, on_device(): lax.ppermute(sent, 'ctx', [(j, (j + s) % n) for j in range(n)])  16 us
    all_to_all x1, waiting for transfers between devices, on_device(): returned = lax.all_to_all(out, 'ctx', 0, 0, tiled=True)  13.7 us
    pallas_call x1, Pallas kernels, long_conv(): pl.pallas_call(functools.partial(long_kernel, min(256, freqs), n), in_spe...  11.7 us
    pallas_call x1, Pallas kernels, finish(): pl.pallas_call(functools.partial(finish_kernel, tap_count), in_specs=[ANY...  8.5 us
    pallas_call x1, Pallas kernels, tap_grads(): pl.pallas_call(functools.partial(tap_kernel, tap_count), in_specs=[ANYWHE...  8.33 us
    pallas_call x1, Pallas kernels, featurize(): pl.pallas_call(functools.partial(featurize_kernel, tap_count, pieces), in...  7.98 us
  transfers between devices with their start and end apart: 17, of which 7 were waited for; matrix products, arithmetic and copies ran while one was open for 5% of the time, Pallas kernels for 14%

profile of v4, /device:TPU:0, one launch (start us, length us, event | category | flops | bytes accessed | tf_op | source)
XLA Modules:
  0.0 170.2 jit_solution(17428967546980695009)
XLA Ops:
  0.7 1.3 fusion.3
  2.6 1.1 broadcast_select_fusion.5
  3.7 3.0 %collective-permute-start = (bf16[3,8,4096]{2,1,0:T(8,128)(2,1)S(1)}, bf16[3,8,4096]{2,1,0:T(8,128)(2,1)S(1)}, u32[]{:S(2)}, u32[]{:S(2)}) collective-permute-start(bf16[3,8,4096]{2,1,0:T(8,128)(2,1)S(1)} %get-tuple-element.61), channel_id=1, source_target_pairs={{0,1},{1,0},{2,3},{3,2},{4,5},{5,4},{6,7},{7,6},{8,9},{9,8},{10,11... | collective-permute-start | bytes 589832 | tf_op jit(solution)/shard_map/ppermute | solution.py:633
  7.4 1.2 copy.17
  10.1 5.0 %collective-permute-done = bf16[3,8,4096]{2,1,0:T(8,128)(2,1)S(1)} collective-permute-done((bf16[3,8,4096]{2,1,0:T(8,128)(2,1)S(1)}, bf16[3,8,4096]{2,1,0:T(8,128)(2,1)S(1)}, u32[]{:S(2)}, u32[]{:S(2)}) %collective-permute-start) | collective-permute-done | bytes 196640 | tf_op jit(solution)/shard_map/ppermute | solution.py:633
  16.0 8.0 %shard_map.120 = (bf16[2,2,2,32,512]{4,3,2,1,0:T(8,128)(2,1)}, bf16[2,2,2,32,512]{4,3,2,1,0:T(8,128)(2,1)}, bf16[2,2,2,32,512]{4,3,2,1,0:T(8,128)(2,1)}, bf16[2,...) custom-call(s32[8]{0:T(128)} %get-tuple-element.66.where_ref, ...), custom_call_target="tpu_custom_call" | custom-call | tf_op jit(solution)/shard_map/pallas_call | solution.py:117
  23.9 3.6 %collective-permute-start.2 = (bf16[2,2,2,32,512]{4,3,2,1,0:T(8,128)(2,1)}, bf16[2,2,2,32,512]{4,3,2,1,0:T(8,128)(2,1)S(1)}, u32[]{:S(2)}, u32[]{:S(2)}) collective-permute-start(bf16[2,2,2,32,512]{4,3,2,1,0:T(8,128)(2,1)} %get-tuple-element.30), channel_id=1, source_target_pairs={{0,4},{1,5},{2,6},{3,7},{4,0},{5,1},{6,2},{7,3},{8,12},{9,13},{10,... | collective-permute-start | bytes 786440 | tf_op jit(solution)/shard_map/ppermute | solution.py:645
  27.7 3.8 %collective-permute-start.4 = (bf16[2,2,2,32,512]{4,3,2,1,0:T(8,128)(2,1)}, bf16[2,2,2,32,512]{4,3,2,1,0:T(8,128)(2,1)S(1)}, u32[]{:S(2)}, u32[]{:S(2)}) collective-permute-start(bf16[2,2,2,32,512]{4,3,2,1,0:T(8,128)(2,1)} %get-tuple-element.32), channel_id=1, source_target_pairs={{0,5},{1,6},{2,7},{3,0},{4,1},{5,2},{6,3},{7,4},{8,13},{9,14},{10,... | collective-permute-start | bytes 786440 | tf_op jit(solution)/shard_map/ppermute | solution.py:645
  31.5 1.6 collective-permute-start.5
  33.1 2.3 %collective-permute-start.6 = (bf16[2,2,2,32,512]{4,3,2,1,0:T(8,128)(2,1)}, bf16[2,2,2,32,512]{4,3,2,1,0:T(8,128)(2,1)}, u32[]{:S(2)}, u32[]{:S(2)}) collective-permute-start(bf16[2,2,2,32,512]{4,3,2,1,0:T(8,128)(2,1)} %get-tuple-element.34), channel_id=1, source_target_pairs={{0,6},{1,7},{2,0},{3,1},{4,2},{5,3},{6,4},{7,5},{8,14},{9,15},{10,... | collective-permute-start | bytes 786440 | tf_op jit(solution)/shard_map/ppermute | solution.py:645
  35.4 21.2 %collective-permute-done.2.refs_0_ = bf16[2,2,2,32,512]{4,3,2,1,0:T(8,128)(2,1)S(1)} collective-permute-done((bf16[2,2,2,32,512]{4,3,2,1,0:T(8,128)(2,1)}, bf16[2,2,2,32,512]{4,3,2,1,0:T(8,128)(2,1)S(1)}, u32[]{:S(2)}, u32[]{:S(2)}) %collective-permute-start.2) | collective-permute-done | bytes 262176 | tf_op jit(solution)/shard_map/ppermute | solution.py:645
  56.6 4.7 %collective-permute-start.8 = (bf16[2,2,2,32,512]{4,3,2,1,0:T(8,128)(2,1)}, bf16[2,2,2,32,512]{4,3,2,1,0:T(8,128)(2,1)}, u32[]{:S(2)}, u32[]{:S(2)}) collective-permute-start(bf16[2,2,2,32,512]{4,3,2,1,0:T(8,128)(2,1)} %get-tuple-element.36), channel_id=1, source_target_pairs={{0,7},{1,0},{2,1},{3,2},{4,3},{5,4},{6,5},{7,6},{8,15},{9,8},{10,9... | collective-permute-start | bytes 786440 | tf_op jit(solution)/shard_map/ppermute | solution.py:645
  62.0 6.6 %shard_map.121.filt_hbm = f32[1,4,512,512]{3,2,1,0:T(8,128)} custom-call(f32[1024,512]{1,0:T(8,128)} %h_ref, bf16[2,1024,512]{2,1,0:T(8,128)(2,1)} %constant.58.clone.table_ref.table_hbm), custom_call_target="tpu_custom_call" | custom-call | tf_op jit(solution)/shard_map/pallas_call | solution.py:198
  68.7 2.0 %collective-permute-done.7.refs_5_ = bf16[2,2,2,32,512]{4,3,2,1,0:T(8,128)(2,1)} collective-permute-done((bf16[2,2,2,32,512]{4,3,2,1,0:T(8,128)(2,1)}, bf16[2,2,2,32,512]{4,3,2,1,0:T(8,128)(2,1)}, u32[]{:S(2)}, u32[]{:S(2)}) %collective-permute-start.7) | collective-permute-done | bytes 262176 | tf_op jit(solution)/shard_map/ppermute | solution.py:645
  70.7 11.7 %shard_map.122 = (bf16[8,2,2,2,32,512]{5,4,3,2,1,0:T(8,128)(2,1)}, bf16[1,2,1024,512]{3,2,1,0:T(8,128)(2,1)}) custom-call(s32[16]{0:T(128)} %select_reduce_fusion.from_ref, s32[16]{0:T(128)} %order_ref.1, f32[1,4,512,512]{3,2,1,0:T(8,128)} %shard_map.121.filt_hbm, bf16[2,1024,512]{2,1,0:T(8,128)(2,1)} %constant.58.clone.table_ref.table_hbm, ...), custom_call_target="tpu_custom_call" | custom-call | tf_op jit(solution)/shard_map/pallas_call | solution.py:319
  82.4 5.4 %all-to-all-start = ((bf16[8,2,2,2,32,512]{5,4,3,2,1,0:T(8,128)(2,1)}), bf16[8,2,2,2,32,512]{5,4,3,2,1,0:T(8,128)(2,1)}, u32[]{:S(2)}, u32[]{:S(2)}) async-start(bf16[8,2,2,2,32,512]{5,4,3,2,1,0:T(8,128)(2,1)} %get-tuple-element.38), calls=%async_computation | async-start | bytes 4194304 | tf_op jit(solution)/shard_map/all_to_all | solution.py:654
  87.9 4.6 %shard_map.123 = bf16[1024,512]{1,0:T(8,128)(2,1)} custom-call(bf16[1,2,1024,512]{3,2,1,0:T(8,128)(2,1)} %get-tuple-element.39.cross_ref, bf16[2,512,1024]{2,1,0:T(8,128)(2,1)} %constant.59.clone.back_hbm.back_ref), custom_call_target="tpu_custom_call" | custom-call | tf_op jit(solution)/shard_map/pallas_call | solution.py:360
  92.5 2.9 %collective-permute-done.9 = bf16[1024,512]{1,0:T(8,128)(2,1)S(1)} collective-permute-done((bf16[1024,512]{1,0:T(8,128)(2,1)}, bf16[1024,512]{1,0:T(8,128)(2,1)S(1)}, u32[]{:S(2)}, u32[]{:S(2)}) %collective-permute-start.9) | collective-permute-done | bytes 1048608 | tf_op jit(solution)/shard_map/ppermute | solution.py:611
  95.3 1.5 add_convert_fusion
  96.9 1.6 collective-permute-start.10
  98.4 23.7 %collective-permute-done.10 = bf16[1024,512]{1,0:T(8,128)(2,1)S(1)} collective-permute-done((bf16[1024,512]{1,0:T(8,128)(2,1)S(1)}, bf16[1024,512]{1,0:T(8,128)(2,1)S(1)}, u32[]{:S(2)}, u32[]{:S(2)}) %collective-permute-start.10) | collective-permute-done | bytes 1048608 | tf_op jit(solution)/shard_map/ppermute | solution.py:611
  122.1 1.6 convert_add_fusion
  123.7 13.7 %all-to-all-done.recv_hbm = bf16[8,2,2,2,32,512]{5,4,3,2,1,0:T(8,128)(2,1)} async-done(((bf16[8,2,2,2,32,512]{5,4,3,2,1,0:T(8,128)(2,1)}), bf16[8,2,2,2,32,512]{5,4,3,2,1,0:T(8,128)(2,1)}, u32[]{:S(2)}, u32[]{:S(2)}) %all-to-all-start) | async-done | bytes 2097184 | tf_op jit(solution)/shard_map/all_to_all | solution.py:654
  137.5 8.3 %shard_map.125 = (bf16[8,32,512]{2,1,0:T(8,128)(2,1)}, bf16[3,16,4096]{2,1,0:T(8,128)(2,1)}) custom-call(bf16[8,2,2,2,32,512]{5,4,3,2,1,0:T(8,128)(2,1)} %all-to-all-done.recv_hbm, bf16[3,128,4096]{2,1,0:T(8,128)(2,1)} %get-tuple-element.41.qkv_hbm, bf16[3,128,4096]{2,1,0:T(8,128)(2,1)} %bitcast.6, bf16[128,4096]{1,0:T(8,128)(2,1)} %bitcast.8, ...), custom_call_target="tpu_custom_call" | custom-call | tf_op jit(solution)/shard_map/pallas_call | solution.py:432
  145.8 3.4 %all-to-all-start.1 = ((bf16[8,32,512]{2,1,0:T(8,128)(2,1)}), bf16[8,32,512]{2,1,0:T(8,128)(2,1)S(1)}, u32[]{:S(2)}, u32[]{:S(2)}) async-start(bf16[8,32,512]{2,1,0:T(8,128)(2,1)} %get-tuple-element.44), calls=%async_computation.1 | async-start | bytes 524288 | tf_op jit(solution)/shard_map/all_to_all | solution.py:658
  149.2 1.1 broadcast_select_fusion.1
  150.3 2.0 %collective-permute-start.11 = (bf16[3,8,4096]{2,1,0:T(8,128)(2,1)S(1)}, bf16[3,8,4096]{2,1,0:T(8,128)(2,1)S(1)}, u32[]{:S(2)}, u32[]{:S(2)}) collective-permute-start(bf16[3,8,4096]{2,1,0:T(8,128)(2,1)S(1)} %get-tuple-element.65), channel_id=1, source_target_pairs={{0,1},{1,0},{2,3},{3,2},{4,5},{5,4},{6,7},{7,6},{8,9},{9,8},{10,11... | collective-permute-start | bytes 589832 | tf_op jit(solution)/shard_map/ppermute | solution.py:633
  152.3 1.3 collective-permute-start.12
  153.6 8.5 %shard_map.124 = (bf16[128,4096]{1,0:T(8,128)(2,1)}, bf16[3,128,4096]{2,1,0:T(8,128)(2,1)}, f32[3,16,4096]{2,1,0:T(8,128)}) custom-call(bf16[8,2,2,2,32,512]{5,4,3,2,1,0:T(8,128)(2,1)} %all-to-all-done.recv_hbm, bf16[3,128,4096]{2,1,0:T(8,128)(2,1)} %get-tuple-element.41.qkv_hbm, bf16[128,4096]{1,0:T(8,128)(2,1)} %bitcast.9, f32[21,4096]{1,0:T(8,128)} %reshape.33.w_ref), custom_call_target="tpu_custom_call" | custom-call | tf_op jit(solution)/shard_map/pallas_call | solution.py:519
  162.3 1.2 collective-permute-done.13
  163.5 1.6 collective-permute-start.14
  165.1 4.4 %shard_map.126 = bf16[3,128,4096]{2,1,0:T(8,128)(2,1)} custom-call(s32[16]{0:T(128)} %order_ref.1, bf16[3,128,4096]{2,1,0:T(8,128)(2,1)} %get-tuple-element.43.old_hbm, f32[3,16,4096]{2,1,0:T(8,128)} %get-tuple-element.47.open_ref, bf16[3,8,4096]{2,1,0:T(8,128)(2,1)} %copy-done.4, ...), custom_call_target="tpu_custom_call", output_to_operand_aliasing={{}: (1, {})} | custom-call | tf_op jit(solution)/shard_map/pallas_call | solution.py:589
  (45 shorter events, 4.7 us)
Async XLA Ops:
  0.6 8.9 %copy-start.6 = (s32[8]{0:T(128)S(1)}, s32[8]{0:T(128)}, u32[]{:S(2)}) copy-start(s32[8]{0:T(128)} %constant.63) | copy-start | bytes 100
  0.6 8.9 %copy-start.7 = (s32[8]{0:T(128)S(1)}, s32[8]{0:T(128)}, u32[]{:S(2)}) copy-start(s32[8]{0:T(128)} %constant.60.clone) | copy-start | bytes 100
  3.7 11.4 %collective-permute-start = (bf16[3,8,4096]{2,1,0:T(8,128)(2,1)S(1)}, bf16[3,8,4096]{2,1,0:T(8,128)(2,1)S(1)}, u32[]{:S(2)}, u32[]{:S(2)}) collective-permute-start(bf16[3,8,4096]{2,1,0:T(8,128)(2,1)S(1)} %get-tuple-element.61), channel_id=1, source_target_pairs={{0,1},{1,0},{2,3},{3,2},{4,5},{5,4},{6,7},{7,6},{8,9},{9,8},{10,11... | collective-permute-start | bytes 589832 | tf_op jit(solution)/shard_map/ppermute | solution.py:633
  6.7 8.4 %collective-permute-start.1 = (bf16[3,8,4096]{2,1,0:T(8,128)(2,1)S(1)}, bf16[3,8,4096]{2,1,0:T(8,128)(2,1)S(1)}, u32[]{:S(2)}, u32[]{:S(2)}) collective-permute-start(bf16[3,8,4096]{2,1,0:T(8,128)(2,1)S(1)} %get-tuple-element.60), channel_id=1, source_target_pairs={{1,2},{2,1},{3,4},{4,3},{5,6},{6,5},{9,10},{10,9},{11,12},{12,11},... | collective-permute-start | bytes 589832 | tf_op jit(solution)/shard_map/ppermute | solution.py:634
  16.0 45.4 %copy-start.5 = (s32[16]{0:T(128)S(1)}, s32[16]{0:T(128)}, u32[]{:S(2)}) copy-start(s32[16]{0:T(128)} %order_ref.1) | copy-start | bytes 196
  23.9 32.7 %collective-permute-start.2 = (bf16[2,2,2,32,512]{4,3,2,1,0:T(8,128)(2,1)}, bf16[2,2,2,32,512]{4,3,2,1,0:T(8,128)(2,1)S(1)}, u32[]{:S(2)}, u32[]{:S(2)}) collective-permute-start(bf16[2,2,2,32,512]{4,3,2,1,0:T(8,128)(2,1)} %get-tuple-element.30), channel_id=1, source_target_pairs={{0,4},{1,5},{2,6},{3,7},{4,0},{5,1},{6,2},{7,3},{8,12},{9,13},{10,... | collective-permute-start | bytes 786440 | tf_op jit(solution)/shard_map/ppermute | solution.py:645
  27.6 29.1 %collective-permute-start.3 = (bf16[2,2,2,32,512]{4,3,2,1,0:T(8,128)(2,1)}, bf16[2,2,2,32,512]{4,3,2,1,0:T(8,128)(2,1)S(1)}, u32[]{:S(2)}, u32[]{:S(2)}) collective-permute-start(bf16[2,2,2,32,512]{4,3,2,1,0:T(8,128)(2,1)} %get-tuple-element.31), channel_id=1, source_target_pairs={{0,3},{1,4},{2,5},{3,6},{4,7},{5,0},{6,1},{7,2},{8,11},{9,12},{10,... | collective-permute-start | bytes 786440 | tf_op jit(solution)/shard_map/ppermute | solution.py:645
  27.7 40.9 %collective-permute-start.4 = (bf16[2,2,2,32,512]{4,3,2,1,0:T(8,128)(2,1)}, bf16[2,2,2,32,512]{4,3,2,1,0:T(8,128)(2,1)S(1)}, u32[]{:S(2)}, u32[]{:S(2)}) collective-permute-start(bf16[2,2,2,32,512]{4,3,2,1,0:T(8,128)(2,1)} %get-tuple-element.32), channel_id=1, source_target_pairs={{0,5},{1,6},{2,7},{3,0},{4,1},{5,2},{6,3},{7,4},{8,13},{9,14},{10,... | collective-permute-start | bytes 786440 | tf_op jit(solution)/shard_map/ppermute | solution.py:645
  31.5 37.1 %collective-permute-start.5 = (bf16[2,2,2,32,512]{4,3,2,1,0:T(8,128)(2,1)}, bf16[2,2,2,32,512]{4,3,2,1,0:T(8,128)(2,1)}, u32[]{:S(2)}, u32[]{:S(2)}) collective-permute-start(bf16[2,2,2,32,512]{4,3,2,1,0:T(8,128)(2,1)} %get-tuple-element.33), channel_id=1, source_target_pairs={{0,2},{1,3},{2,4},{3,5},{4,6},{5,7},{6,0},{7,1},{8,10},{9,11},{10,... | collective-permute-start | bytes 786440 | tf_op jit(solution)/shard_map/ppermute | solution.py:645
  33.1 35.6 %collective-permute-start.6 = (bf16[2,2,2,32,512]{4,3,2,1,0:T(8,128)(2,1)}, bf16[2,2,2,32,512]{4,3,2,1,0:T(8,128)(2,1)}, u32[]{:S(2)}, u32[]{:S(2)}) collective-permute-start(bf16[2,2,2,32,512]{4,3,2,1,0:T(8,128)(2,1)} %get-tuple-element.34), channel_id=1, source_target_pairs={{0,6},{1,7},{2,0},{3,1},{4,2},{5,3},{6,4},{7,5},{8,14},{9,15},{10,... | collective-permute-start | bytes 786440 | tf_op jit(solution)/shard_map/ppermute | solution.py:645
  56.6 12.1 %copy-start.1 = (bf16[2,2,2,32,512]{4,3,2,1,0:T(8,128)(2,1)}, bf16[2,2,2,32,512]{4,3,2,1,0:T(8,128)(2,1)S(1)}, u32[]{:S(2)}) copy-start(bf16[2,2,2,32,512]{4,3,2,1,0:T(8,128)(2,1)S(1)} %collective-permute-done.2.refs_0_) | copy-start | bytes 786436
  56.6 14.1 %collective-permute-start.7 = (bf16[2,2,2,32,512]{4,3,2,1,0:T(8,128)(2,1)}, bf16[2,2,2,32,512]{4,3,2,1,0:T(8,128)(2,1)}, u32[]{:S(2)}, u32[]{:S(2)}) collective-permute-start(bf16[2,2,2,32,512]{4,3,2,1,0:T(8,128)(2,1)} %get-tuple-element.35), channel_id=1, source_target_pairs={{0,1},{1,2},{2,3},{3,4},{4,5},{5,6},{6,7},{7,0},{8,9},{9,10},{10,1... | collective-permute-start | bytes 786440 | tf_op jit(solution)/shard_map/ppermute | solution.py:645
  56.6 12.0 %copy-start.2 = (bf16[2,2,2,32,512]{4,3,2,1,0:T(8,128)(2,1)}, bf16[2,2,2,32,512]{4,3,2,1,0:T(8,128)(2,1)S(1)}, u32[]{:S(2)}) copy-start(bf16[2,2,2,32,512]{4,3,2,1,0:T(8,128)(2,1)S(1)} %collective-permute-done.3.refs_1_) | copy-start | bytes 786436
  56.6 14.1 %collective-permute-start.8 = (bf16[2,2,2,32,512]{4,3,2,1,0:T(8,128)(2,1)}, bf16[2,2,2,32,512]{4,3,2,1,0:T(8,128)(2,1)}, u32[]{:S(2)}, u32[]{:S(2)}) collective-permute-start(bf16[2,2,2,32,512]{4,3,2,1,0:T(8,128)(2,1)} %get-tuple-element.36), channel_id=1, source_target_pairs={{0,7},{1,0},{2,1},{3,2},{4,3},{5,4},{6,5},{7,6},{8,15},{9,8},{10,9... | collective-permute-start | bytes 786440 | tf_op jit(solution)/shard_map/ppermute | solution.py:645
  68.7 2.1 %copy-start.3 = (bf16[2,2,2,32,512]{4,3,2,1,0:T(8,128)(2,1)}, bf16[2,2,2,32,512]{4,3,2,1,0:T(8,128)(2,1)S(1)}, u32[]{:S(2)}) copy-start(bf16[2,2,2,32,512]{4,3,2,1,0:T(8,128)(2,1)S(1)} %collective-permute-done.4.refs_2_) | copy-start | bytes 786436
  82.4 55.0 %all-to-all-start = ((bf16[8,2,2,2,32,512]{5,4,3,2,1,0:T(8,128)(2,1)}), bf16[8,2,2,2,32,512]{5,4,3,2,1,0:T(8,128)(2,1)}, u32[]{:S(2)}, u32[]{:S(2)}) async-start(bf16[8,2,2,2,32,512]{5,4,3,2,1,0:T(8,128)(2,1)} %get-tuple-element.38), calls=%async_computation | async-start | bytes 4194304 | tf_op jit(solution)/shard_map/all_to_all | solution.py:654
  92.5 2.9 %collective-permute-start.9 = (bf16[1024,512]{1,0:T(8,128)(2,1)}, bf16[1024,512]{1,0:T(8,128)(2,1)S(1)}, u32[]{:S(2)}, u32[]{:S(2)}) collective-permute-start(bf16[1024,512]{1,0:T(8,128)(2,1)} %shard_map.123), channel_id=1, source_target_pairs={{0,8},{8,0},{16,24},{24,16},{1,9},{9,1},{17,25},{25,17},{2,10},{10... | collective-permute-start | bytes 3145736 | tf_op jit(solution)/shard_map/ppermute | solution.py:611
  96.9 25.3 %collective-permute-start.10 = (bf16[1024,512]{1,0:T(8,128)(2,1)S(1)}, bf16[1024,512]{1,0:T(8,128)(2,1)S(1)}, u32[]{:S(2)}, u32[]{:S(2)}) collective-permute-start(bf16[1024,512]{1,0:T(8,128)(2,1)S(1)} %add_convert_fusion), channel_id=1, source_target_pairs={{0,16},{8,24},{16,0},{24,8},{1,17},{9,25},{17,1},{25,9},{2,18},{10... | collective-permute-start | bytes 3145736 | tf_op jit(solution)/shard_map/ppermute | solution.py:611
  145.8 16.3 %all-to-all-start.1 = ((bf16[8,32,512]{2,1,0:T(8,128)(2,1)}), bf16[8,32,512]{2,1,0:T(8,128)(2,1)S(1)}, u32[]{:S(2)}, u32[]{:S(2)}) async-start(bf16[8,32,512]{2,1,0:T(8,128)(2,1)} %get-tuple-element.44), calls=%async_computation.1 | async-start | bytes 524288 | tf_op jit(solution)/shard_map/all_to_all | solution.py:658
  150.3 11.8 %copy-start = (bf16[3,8,4096]{2,1,0:T(8,128)(2,1)}, bf16[3,8,4096]{2,1,0:T(8,128)(2,1)S(1)}, u32[]{:S(2)}) copy-start(bf16[3,8,4096]{2,1,0:T(8,128)(2,1)S(1)} %get-tuple-element.64.own_ref) | copy-start | bytes 589828
  150.3 11.8 %collective-permute-start.11 = (bf16[3,8,4096]{2,1,0:T(8,128)(2,1)S(1)}, bf16[3,8,4096]{2,1,0:T(8,128)(2,1)S(1)}, u32[]{:S(2)}, u32[]{:S(2)}) collective-permute-start(bf16[3,8,4096]{2,1,0:T(8,128)(2,1)S(1)} %get-tuple-element.65), channel_id=1, source_target_pairs={{0,1},{1,0},{2,3},{3,2},{4,5},{5,4},{6,7},{7,6},{8,9},{9,8},{10,11... | collective-permute-start | bytes 589832 | tf_op jit(solution)/shard_map/ppermute | solution.py:633
  152.3 9.9 %collective-permute-start.12 = (bf16[3,8,4096]{2,1,0:T(8,128)(2,1)S(1)}, bf16[3,8,4096]{2,1,0:T(8,128)(2,1)}, u32[]{:S(2)}, u32[]{:S(2)}) collective-permute-start(bf16[3,8,4096]{2,1,0:T(8,128)(2,1)S(1)} %get-tuple-element.64.own_ref), channel_id=1, source_target_pairs={{1,2},{2,1},{3,4},{4,3},{5,6},{6,5},{9,10},{10,9},{11,12},{12,11},... | collective-permute-start | bytes 589832 | tf_op jit(solution)/shard_map/ppermute | solution.py:634
  162.1 3.0 %copy-start.4 = (bf16[3,8,4096]{2,1,0:T(8,128)(2,1)}, bf16[3,8,4096]{2,1,0:T(8,128)(2,1)S(1)}, u32[]{:S(2)}) copy-start(bf16[3,8,4096]{2,1,0:T(8,128)(2,1)S(1)} %collective-permute-done.11.inner_ref) | copy-start | bytes 589828
  162.2 1.3 collective-permute-start.13
  163.5 6.0 %collective-permute-start.14 = (f32[21,512]{1,0:T(8,128)S(1)}, f32[21,512]{1,0:T(8,128)S(1)}, u32[]{:S(2)}, u32[]{:S(2)}) collective-permute-start(f32[21,512]{1,0:T(8,128)S(1)} %slice_add_fusion), channel_id=1, source_target_pairs={{0,16},{8,24},{16,0},{24,8},{1,17},{9,25},{17,1},{25,9},{2,18},{10... | collective-permute-start | bytes 129032 | tf_op jit(solution)/shard_map/ppermute | solution.py:611

commit v5 on v4

--- a/solution.py
+++ b/solution.py
@@ -90,9 +90,9 @@
                     ext = ext_ref.at[slot * 3 + j]
                     ext[:RIM] = halo_ref[j, :, wide].astype(F32)[slot * RIM : (slot + 1) * RIM]
                     ext[RIM:] = x_buf[i, j, here, cols].astype(F32)
-                    total = jnp.zeros((half, lanes), F32)
-                    for s in range(tap_count):
-                        total = total + w_ref[s * 3 + j : s * 3 + j + 1, wide] * ext[RIM - s : RIM - s + half]
+                    total = w_ref[j, :1, wide] * ext[RIM : RIM + half]
+                    for s in range(1, tap_count):
+                        total = total + w_ref[j, s : s + 1, wide] * ext[RIM - s : RIM - s + half]
                     made.append(total.astype(BF))
                     qkv_buf[i, j, here, cols] = made[j]
                 query, key, value = (m.astype(F32) for m in made)
@@ -412,8 +412,11 @@
                         term = grads[j] * ext[RIM - s : RIM - s + half]
                         term = jnp.sum(term.reshape(half // 8, 8, lanes), 0)
                         short[s, j] = term if slot == 0 else short[s, j] + term
-            lines = [jnp.sum(short[s, j], 0, keepdims=True) for s in range(tap_count) for j in range(3)]
-            lines.append(jnp.zeros((short_ref.shape[1] - len(lines), lanes), F32))
+            lines = []
+            for j in range(3):
+                lines += [jnp.sum(short[s, j], 0, keepdims=True) for s in range(tap_count)]
+                lines.append(jnp.zeros((RIM - tap_count, lanes), F32))
+            lines.append(jnp.zeros((short_ref.shape[1] - 3 * RIM, lanes), F32))
             short_ref[c, :, cols] = jnp.concatenate(lines, 0).astype(BF)
             for j in range(3):
                 head_ref[j, :, wide] = jnp.concatenate(heads[j], 0).astype(BF)
@@ -428,7 +431,7 @@
     rows, width = g.shape
     n, channels = recv.shape[0], recv.shape[-1]
     lanes = min(128, channels)
-    short_rows = -(-tap_count * 3 // 16) * 16
+    short_rows = -(-3 * RIM // 16) * 16
     return pl.pallas_call(
         functools.partial(tap_kernel, tap_count),
         in_specs=[ANYWHERE] * 4 + [VECTOR],
@@ -493,9 +496,9 @@
                     gf = gf_ref.at[slot * 3 + j]
                     gf[:half] = grads[j]
                     gf[half:] = jnp.zeros((RIM, lanes), F32)
-                    total = jnp.zeros((half, lanes), F32)
-                    for s in range(tap_count):
-                        total = total + w_ref[s * 3 + j : s * 3 + j + 1, wide] * gf[s : s + half]
+                    total = w_ref[j, :1, wide] * grads[j]
+                    for s in range(1, tap_count):
+                        total = total + w_ref[j, s : s + 1, wide] * gf[s : s + half]
                     grad_buf[c, j, here, cols] = total.astype(BF)
                     rest[j].append(total[half - RIM :])
             for j in range(3):
@@ -550,19 +553,23 @@
     rows = grad_hbm.shape[1]
     tile = 2 * RIM
 
-    def moves(slot):
-        place = grad_hbm.at[:, (slot + 1) * rows // 2 - tile : (slot + 1) * rows // 2]
-        return (pltpu.make_async_copy(place, tile_buf.at[slot], load_sem.at[slot]),
-                pltpu.make_async_copy(tile_buf.at[slot], place, store_sem.at[slot]))
+    def place(slot):
+        return grad_hbm.at[:, (slot + 1) * rows // 2 - tile : (slot + 1) * rows // 2]
+
+    def load(slot):
+        return pltpu.make_async_copy(place(slot), tile_buf.at[slot], load_sem.at[slot])
+
+    def store(slot):
+        return pltpu.make_async_copy(tile_buf.at[slot], place(slot), store_sem.at[slot])
 
     for slot in range(2):
-        moves(slot)[0].start()
+        load(slot).start()
     swap = swapped(order_ref)
     last = lax.axis_index("ctx") == lax.axis_size("ctx") - 1
     rim_ref[swap] = inner_ref[...].astype(F32)
     rim_ref[1 - swap] = jnp.where(last, own_ref[...].astype(F32), outer_ref[...].astype(F32))
     for slot in range(2):
-        moves(slot)[0].wait()
+        load(slot).wait()
 
     def body(cols):
         for slot in range(2):
@@ -573,15 +580,15 @@
                 gf[RIM:] = rim_ref[slot, j, :, cols]
                 total = open_ref[j, rim, cols]
                 for s in range(1, tap_count):
-                    total = total + w_ref[s * 3 + j : s * 3 + j + 1, cols] * gf[s : s + RIM]
+                    total = total + w_ref[j, s : s + 1, cols] * gf[s : s + RIM]
                 kept = tile_buf[slot, j, :, cols].astype(F32)[: tile - RIM]
                 tile_buf[slot, j, :, cols] = jnp.concatenate([kept, total], 0).astype(BF)
 
     each_part(grad_hbm.shape[2], body)
     for slot in range(2):
-        moves(slot)[1].start()
+        store(slot).start()
     for slot in range(2):
-        moves(slot)[1].wait()
+        store(slot).wait()
 
 
 def close(order, grads, opened, inner, outer, own, taps, tap_count):
@@ -622,7 +629,7 @@
     channels = width // n
     tap_count = short_w.shape[0]
     table, back = (jnp.asarray(t) for t in dft_tables(min(rows * n, 1024)))
-    taps = short_w.reshape(tap_count * 3, width)
+    taps = short_w.transpose(1, 0, 2)
     x, g = feats[0], grad_y[0]
     numbers = jnp.arange(2 * n, dtype=jnp.int32)
     flip = jnp.sum(jnp.where(numbers == 2 * me, block_order, 0)) != me
@@ -639,7 +646,7 @@
     inner, outer = trade(jnp.where(swap, tails[1], tails[0]), own)
     outer = jnp.where(last, own, outer)
     halo = jnp.concatenate([jnp.where(swap, inner, outer), jnp.where(swap, outer, inner)], 1)
-    hops = sorted(range(1, n), key=lambda s: abs(s - n // 2)) + [0]
+    hops = sorted(range(1, n), key=lambda s: (s != 2, abs(s - n // 2))) + [0]
     chunks = (me + jnp.asarray(hops, jnp.int32)) % n
     sends, qkv = featurize(chunks, x, g, halo, taps, tap_count)
     recvs = [lax.ppermute(sent, "ctx", [(j, (j + s) % n) for j in range(n)]) if s else sent
@@ -662,8 +669,9 @@
     mixed, grads, opened = finish(returned, qkv, g, taps, tap_count)
     pieces, inner, outer, opened = lax.optimization_barrier((pieces, inner, outer, opened))
     grads = close(block_order, grads, opened, inner, outer, own, taps, tap_count)
-    short_sum = sum_over_dp(jnp.sum(pieces.astype(F32), 0)[: tap_count * 3], F32)
-    return mixed[None], grads[None], short_sum.reshape(tap_count, 3, channels), filter_sum
+    short_sum = sum_over_dp(jnp.sum(pieces.astype(F32), 0)[: 3 * RIM], F32)
+    short_sum = short_sum.reshape(3, RIM, channels)[:, :tap_count].transpose(1, 0, 2)
+    return mixed[None], grads[None], short_sum, filter_sum
 
 
 def solution(mesh):

time: 171 us -> 170 us (level)
  starting transfers between devices: 35 us -> 40.2 us
  waiting for transfers between devices: 69.8 us -> 64.7 us
    ppermute x7, starting transfers between devices: 16 us -> 22 us  [on_device(): lax.ppermute(sent, 'ctx', [(j, (j + s) % n) for j in range(n)])]
    all_to_all x1, waiting for transfers between devices: 13.7 us -> 9.83 us  [on_device(): returned = lax.all_to_all(out, 'ctx', 0, 0, tiled=True)]
    ppermute x7, waiting for transfers between devices: 23.3 us -> 20.4 us  [on_device(): lax.ppermute(sent, 'ctx', [(j, (j + s) % n) for j in range(n)])]
  transfers between devices with their start and end apart: 17 -> 17, of which waited for: 7 -> 7; matrix products, arithmetic and copies ran while one was open for 5% -> 4% of each run, Pallas kernels for 14% -> 14%
where the time goes in v5:
time: 170 us; the launch traced here: 169 us
  waiting for transfers between devices  64.7 us (38%)
  Pallas kernels  52.1 us (31%)
  starting transfers between devices  40.2 us (24%)
  other arithmetic  9.31 us (5%)
    ppermute x4, waiting for transfers between devices, sum_over_dp(): lax.ppermute(sent, 'dp', [(j, j ^ hop) for j in range(lax.axis_size('dp'))])  27.9 us
    ppermute x7, starting transfers between devices, on_device(): lax.ppermute(sent, 'ctx', [(j, (j + s) % n) for j in range(n)])  22 us
    ppermute x7, waiting for transfers between devices, on_device(): lax.ppermute(sent, 'ctx', [(j, (j + s) % n) for j in range(n)])  20.4 us
    pallas_call x1, Pallas kernels, long_conv(): pl.pallas_call(functools.partial(long_kernel, min(256, freqs), n), in_spe...  11.7 us
    all_to_all x1, waiting for transfers between devices, on_device(): returned = lax.all_to_all(out, 'ctx', 0, 0, tiled=True)  9.83 us
    pallas_call x1, Pallas kernels, finish(): pl.pallas_call(functools.partial(finish_kernel, tap_count), in_specs=[ANY...  8.48 us
    pallas_call x1, Pallas kernels, tap_grads(): pl.pallas_call(functools.partial(tap_kernel, tap_count), in_specs=[ANYWHE...  8.32 us
    pallas_call x1, Pallas kernels, featurize(): pl.pallas_call(functools.partial(featurize_kernel, tap_count, pieces), in...  7.96 us
  transfers between devices with their start and end apart: 17, of which 7 were waited for; matrix products, arithmetic and copies ran while one was open for 4% of the time, Pallas kernels for 14%

profile of v5, /device:TPU:0, one launch (start us, length us, event | category | flops | bytes accessed | tf_op | source)
XLA Modules:
  0.0 169.2 jit_solution(15391913501336824483)
XLA Ops:
  0.6 1.3 fusion.3
  3.7 3.0 %collective-permute-start = (bf16[3,8,4096]{2,1,0:T(8,128)(2,1)S(1)}, bf16[3,8,4096]{2,1,0:T(8,128)(2,1)S(1)}, u32[]{:S(2)}, u32[]{:S(2)}) collective-permute-start(bf16[3,8,4096]{2,1,0:T(8,128)(2,1)S(1)} %get-tuple-element.53), channel_id=1, source_target_pairs={{0,1},{1,0},{2,3},{3,2},{4,5},{5,4},{6,7},{7,6},{8,9},{9,8},{10,11... | collective-permute-start | bytes 589832 | tf_op jit(solution)/shard_map/ppermute | solution.py:640
  7.4 1.2 and_select_fusion
  8.6 6.5 %collective-permute-done = bf16[3,8,4096]{2,1,0:T(8,128)(2,1)S(1)} collective-permute-done((bf16[3,8,4096]{2,1,0:T(8,128)(2,1)S(1)}, bf16[3,8,4096]{2,1,0:T(8,128)(2,1)S(1)}, u32[]{:S(2)}, u32[]{:S(2)}) %collective-permute-start) | collective-permute-done | bytes 196640 | tf_op jit(solution)/shard_map/ppermute | solution.py:640
  15.9 8.0 %shard_map.120 = (bf16[2,2,2,32,512]{4,3,2,1,0:T(8,128)(2,1)}, bf16[2,2,2,32,512]{4,3,2,1,0:T(8,128)(2,1)}, bf16[2,2,2,32,512]{4,3,2,1,0:T(8,128)(2,1)}, bf16[2,...) custom-call(s32[8]{0:T(128)} %get-tuple-element.58.where_ref, ...), custom_call_target="tpu_custom_call" | custom-call | tf_op jit(solution)/shard_map/pallas_call | solution.py:117
  23.8 2.6 %collective-permute-start.2 = (bf16[2,2,2,32,512]{4,3,2,1,0:T(8,128)(2,1)}, bf16[2,2,2,32,512]{4,3,2,1,0:T(8,128)(2,1)S(1)}, u32[]{:S(2)}, u32[]{:S(2)}) collective-permute-start(bf16[2,2,2,32,512]{4,3,2,1,0:T(8,128)(2,1)} %get-tuple-element.30), channel_id=1, source_target_pairs={{0,2},{1,3},{2,4},{3,5},{4,6},{5,7},{6,0},{7,1},{8,10},{9,11},{10,... | collective-permute-start | bytes 786440 | tf_op jit(solution)/shard_map/ppermute | solution.py:652
  26.4 2.7 %collective-permute-start.3 = (bf16[2,2,2,32,512]{4,3,2,1,0:T(8,128)(2,1)}, bf16[2,2,2,32,512]{4,3,2,1,0:T(8,128)(2,1)S(1)}, u32[]{:S(2)}, u32[]{:S(2)}) collective-permute-start(bf16[2,2,2,32,512]{4,3,2,1,0:T(8,128)(2,1)} %get-tuple-element.31), channel_id=1, source_target_pairs={{0,4},{1,5},{2,6},{3,7},{4,0},{5,1},{6,2},{7,3},{8,12},{9,13},{10,... | collective-permute-start | bytes 786440 | tf_op jit(solution)/shard_map/ppermute | solution.py:652
  29.2 1.1 collective-permute-start.4
  30.4 2.7 %collective-permute-start.5 = (bf16[2,2,2,32,512]{4,3,2,1,0:T(8,128)(2,1)}, bf16[2,2,2,32,512]{4,3,2,1,0:T(8,128)(2,1)}, u32[]{:S(2)}, u32[]{:S(2)}) collective-permute-start(bf16[2,2,2,32,512]{4,3,2,1,0:T(8,128)(2,1)} %get-tuple-element.33), channel_id=1, source_target_pairs={{0,5},{1,6},{2,7},{3,0},{4,1},{5,2},{6,3},{7,4},{8,13},{9,14},{10,... | collective-permute-start | bytes 786440 | tf_op jit(solution)/shard_map/ppermute | solution.py:652
  33.0 1.3 collective-permute-start.6
  34.4 1.6 collective-permute-done.2.refs_0_
  36.0 1.7 %collective-permute-start.7 = (bf16[2,2,2,32,512]{4,3,2,1,0:T(8,128)(2,1)}, bf16[2,2,2,32,512]{4,3,2,1,0:T(8,128)(2,1)}, u32[]{:S(2)}, u32[]{:S(2)}) collective-permute-start(bf16[2,2,2,32,512]{4,3,2,1,0:T(8,128)(2,1)} %get-tuple-element.35), channel_id=1, source_target_pairs={{0,1},{1,2},{2,3},{3,4},{4,5},{5,6},{6,7},{7,0},{8,9},{9,10},{10,1... | collective-permute-start | bytes 786440 | tf_op jit(solution)/shard_map/ppermute | solution.py:652
  37.7 18.7 %collective-permute-done.3.refs_1_ = bf16[2,2,2,32,512]{4,3,2,1,0:T(8,128)(2,1)S(1)} collective-permute-done((bf16[2,2,2,32,512]{4,3,2,1,0:T(8,128)(2,1)}, bf16[2,2,2,32,512]{4,3,2,1,0:T(8,128)(2,1)S(1)}, u32[]{:S(2)}, u32[]{:S(2)}) %collective-permute-start.3) | collective-permute-done | bytes 262176 | tf_op jit(solution)/shard_map/ppermute | solution.py:652
  56.4 10.0 %collective-permute-start.8 = (bf16[2,2,2,32,512]{4,3,2,1,0:T(8,128)(2,1)}, bf16[2,2,2,32,512]{4,3,2,1,0:T(8,128)(2,1)}, u32[]{:S(2)}, u32[]{:S(2)}) collective-permute-start(bf16[2,2,2,32,512]{4,3,2,1,0:T(8,128)(2,1)} %get-tuple-element.36), channel_id=1, source_target_pairs={{0,7},{1,0},{2,1},{3,2},{4,3},{5,4},{6,5},{7,6},{8,15},{9,8},{10,9... | collective-permute-start | bytes 786440 | tf_op jit(solution)/shard_map/ppermute | solution.py:652
  67.1 6.6 %shard_map.121.filt_hbm = f32[1,4,512,512]{3,2,1,0:T(8,128)} custom-call(f32[1024,512]{1,0:T(8,128)} %h_ref, bf16[2,1024,512]{2,1,0:T(8,128)(2,1)} %constant.58.clone.table_ref.table_hbm), custom_call_target="tpu_custom_call" | custom-call | tf_op jit(solution)/shard_map/pallas_call | solution.py:198
  74.5 11.7 %shard_map.122 = (bf16[8,2,2,2,32,512]{5,4,3,2,1,0:T(8,128)(2,1)}, bf16[1,2,1024,512]{3,2,1,0:T(8,128)(2,1)}) custom-call(s32[16]{0:T(128)} %select_reduce_fusion.from_ref, s32[16]{0:T(128)} %order_ref.1, f32[1,4,512,512]{3,2,1,0:T(8,128)} %shard_map.121.filt_hbm, bf16[2,1024,512]{2,1,0:T(8,128)(2,1)} %constant.58.clone.table_ref.table_hbm, ...), custom_call_target="tpu_custom_call" | custom-call | tf_op jit(solution)/shard_map/pallas_call | solution.py:319
  86.1 4.6 %all-to-all-start = ((bf16[8,2,2,2,32,512]{5,4,3,2,1,0:T(8,128)(2,1)}), bf16[8,2,2,2,32,512]{5,4,3,2,1,0:T(8,128)(2,1)}, u32[]{:S(2)}, u32[]{:S(2)}) async-start(bf16[8,2,2,2,32,512]{5,4,3,2,1,0:T(8,128)(2,1)} %get-tuple-element.38), calls=%async_computation | async-start | bytes 4194304 | tf_op jit(solution)/shard_map/all_to_all | solution.py:661
  90.7 4.6 %shard_map.123 = bf16[1024,512]{1,0:T(8,128)(2,1)} custom-call(bf16[1,2,1024,512]{3,2,1,0:T(8,128)(2,1)} %get-tuple-element.39.cross_ref, bf16[2,512,1024]{2,1,0:T(8,128)(2,1)} %constant.59.clone.back_hbm.back_ref), custom_call_target="tpu_custom_call" | custom-call | tf_op jit(solution)/shard_map/pallas_call | solution.py:360
  95.3 2.9 %collective-permute-done.9 = bf16[1024,512]{1,0:T(8,128)(2,1)S(1)} collective-permute-done((bf16[1024,512]{1,0:T(8,128)(2,1)}, bf16[1024,512]{1,0:T(8,128)(2,1)S(1)}, u32[]{:S(2)}, u32[]{:S(2)}) %collective-permute-start.9) | collective-permute-done | bytes 1048608 | tf_op jit(solution)/shard_map/ppermute | solution.py:618
  98.2 1.5 add_convert_fusion
  99.7 1.4 collective-permute-start.10
  101.1 23.9 %collective-permute-done.10 = bf16[1024,512]{1,0:T(8,128)(2,1)S(1)} collective-permute-done((bf16[1024,512]{1,0:T(8,128)(2,1)S(1)}, bf16[1024,512]{1,0:T(8,128)(2,1)S(1)}, u32[]{:S(2)}, u32[]{:S(2)}) %collective-permute-start.10) | collective-permute-done | bytes 1048608 | tf_op jit(solution)/shard_map/ppermute | solution.py:618
  125.0 1.6 convert_add_fusion
  126.6 9.8 %all-to-all-done.recv_hbm = bf16[8,2,2,2,32,512]{5,4,3,2,1,0:T(8,128)(2,1)} async-done(((bf16[8,2,2,2,32,512]{5,4,3,2,1,0:T(8,128)(2,1)}), bf16[8,2,2,2,32,512]{5,4,3,2,1,0:T(8,128)(2,1)}, u32[]{:S(2)}, u32[]{:S(2)}) %all-to-all-start) | async-done | bytes 2097184 | tf_op jit(solution)/shard_map/all_to_all | solution.py:661
  136.4 8.3 %shard_map.125 = (bf16[8,32,512]{2,1,0:T(8,128)(2,1)}, bf16[3,16,4096]{2,1,0:T(8,128)(2,1)}) custom-call(bf16[8,2,2,2,32,512]{5,4,3,2,1,0:T(8,128)(2,1)} %all-to-all-done.recv_hbm, bf16[3,128,4096]{2,1,0:T(8,128)(2,1)} %get-tuple-element.41.qkv_hbm, bf16[3,128,4096]{2,1,0:T(8,128)(2,1)} %bitcast.11, bf16[128,4096]{1,0:T(8,128)(2,1)} %bitcast.13, ...), custom_call_target="tpu_custom_call" | custom-call | tf_op jit(solution)/shard_map/pallas_call | solution.py:435
  144.8 3.4 %all-to-all-start.1 = ((bf16[8,32,512]{2,1,0:T(8,128)(2,1)}), bf16[8,32,512]{2,1,0:T(8,128)(2,1)S(1)}, u32[]{:S(2)}, u32[]{:S(2)}) async-start(bf16[8,32,512]{2,1,0:T(8,128)(2,1)} %get-tuple-element.44), calls=%async_computation.1 | async-start | bytes 524288 | tf_op jit(solution)/shard_map/all_to_all | solution.py:665
  149.3 2.1 %collective-permute-start.11 = (bf16[3,8,4096]{2,1,0:T(8,128)(2,1)S(1)}, bf16[3,8,4096]{2,1,0:T(8,128)(2,1)S(1)}, u32[]{:S(2)}, u32[]{:S(2)}) collective-permute-start(bf16[3,8,4096]{2,1,0:T(8,128)(2,1)S(1)} %get-tuple-element.57), channel_id=1, source_target_pairs={{0,1},{1,0},{2,3},{3,2},{4,5},{5,4},{6,7},{7,6},{8,9},{9,8},{10,11... | collective-permute-start | bytes 589832 | tf_op jit(solution)/shard_map/ppermute | solution.py:640
  151.3 1.3 collective-permute-start.12
  152.7 8.5 %shard_map.124 = (bf16[128,4096]{1,0:T(8,128)(2,1)}, bf16[3,128,4096]{2,1,0:T(8,128)(2,1)}, f32[3,16,4096]{2,1,0:T(8,128)}) custom-call(bf16[8,2,2,2,32,512]{5,4,3,2,1,0:T(8,128)(2,1)} %all-to-all-done.recv_hbm, bf16[3,128,4096]{2,1,0:T(8,128)(2,1)} %get-tuple-element.41.qkv_hbm, bf16[128,4096]{1,0:T(8,128)(2,1)} %bitcast.14, f32[3,7,4096]{2,1,0:T(8,128)} %bitcast.16), custom_call_target="tpu_custom_call" | custom-call | tf_op jit(solution)/shard_map/pallas_call | solution.py:522
  161.3 1.2 collective-permute-done.13
  162.6 1.6 collective-permute-start.14
  164.1 4.4 %shard_map.126 = bf16[3,128,4096]{2,1,0:T(8,128)(2,1)} custom-call(s32[16]{0:T(128)} %order_ref.1, bf16[3,128,4096]{2,1,0:T(8,128)(2,1)} %get-tuple-element.43.old_hbm, f32[3,16,4096]{2,1,0:T(8,128)} %get-tuple-element.47.open_ref, bf16[3,8,4096]{2,1,0:T(8,128)(2,1)} %copy-done.4, ...), custom_call_target="tpu_custom_call", output_to_operand_aliasing={{}: (1, {})} | custom-call | tf_op jit(solution)/shard_map/pallas_call | solution.py:596
  (38 shorter events, 5.9 us)
Async XLA Ops:
  3.7 11.4 %collective-permute-start = (bf16[3,8,4096]{2,1,0:T(8,128)(2,1)S(1)}, bf16[3,8,4096]{2,1,0:T(8,128)(2,1)S(1)}, u32[]{:S(2)}, u32[]{:S(2)}) collective-permute-start(bf16[3,8,4096]{2,1,0:T(8,128)(2,1)S(1)} %get-tuple-element.53), channel_id=1, source_target_pairs={{0,1},{1,0},{2,3},{3,2},{4,5},{5,4},{6,7},{7,6},{8,9},{9,8},{10,11... | collective-permute-start | bytes 589832 | tf_op jit(solution)/shard_map/ppermute | solution.py:640
  6.7 8.4 %collective-permute-start.1 = (bf16[3,8,4096]{2,1,0:T(8,128)(2,1)S(1)}, bf16[3,8,4096]{2,1,0:T(8,128)(2,1)S(1)}, u32[]{:S(2)}, u32[]{:S(2)}) collective-permute-start(bf16[3,8,4096]{2,1,0:T(8,128)(2,1)S(1)} %get-tuple-element.52), channel_id=1, source_target_pairs={{1,2},{2,1},{3,4},{4,3},{5,6},{6,5},{9,10},{10,9},{11,12},{12,11},... | collective-permute-start | bytes 589832 | tf_op jit(solution)/shard_map/ppermute | solution.py:641
  15.9 50.5 %copy-start.5 = (s32[16]{0:T(128)S(1)}, s32[16]{0:T(128)}, u32[]{:S(2)}) copy-start(s32[16]{0:T(128)} %order_ref.1) | copy-start | bytes 196
  23.8 12.1 %collective-permute-start.2 = (bf16[2,2,2,32,512]{4,3,2,1,0:T(8,128)(2,1)}, bf16[2,2,2,32,512]{4,3,2,1,0:T(8,128)(2,1)S(1)}, u32[]{:S(2)}, u32[]{:S(2)}) collective-permute-start(bf16[2,2,2,32,512]{4,3,2,1,0:T(8,128)(2,1)} %get-tuple-element.30), channel_id=1, source_target_pairs={{0,2},{1,3},{2,4},{3,5},{4,6},{5,7},{6,0},{7,1},{8,10},{9,11},{10,... | collective-permute-start | bytes 786440 | tf_op jit(solution)/shard_map/ppermute | solution.py:652
  26.4 30.0 %collective-permute-start.3 = (bf16[2,2,2,32,512]{4,3,2,1,0:T(8,128)(2,1)}, bf16[2,2,2,32,512]{4,3,2,1,0:T(8,128)(2,1)S(1)}, u32[]{:S(2)}, u32[]{:S(2)}) collective-permute-start(bf16[2,2,2,32,512]{4,3,2,1,0:T(8,128)(2,1)} %get-tuple-element.31), channel_id=1, source_target_pairs={{0,4},{1,5},{2,6},{3,7},{4,0},{5,1},{6,2},{7,3},{8,12},{9,13},{10,... | collective-permute-start | bytes 786440 | tf_op jit(solution)/shard_map/ppermute | solution.py:652
  29.2 44.5 %collective-permute-start.4 = (bf16[2,2,2,32,512]{4,3,2,1,0:T(8,128)(2,1)}, bf16[2,2,2,32,512]{4,3,2,1,0:T(8,128)(2,1)S(1)}, u32[]{:S(2)}, u32[]{:S(2)}) collective-permute-start(bf16[2,2,2,32,512]{4,3,2,1,0:T(8,128)(2,1)} %get-tuple-element.32), channel_id=1, source_target_pairs={{0,3},{1,4},{2,5},{3,6},{4,7},{5,0},{6,1},{7,2},{8,11},{9,12},{10,... | collective-permute-start | bytes 786440 | tf_op jit(solution)/shard_map/ppermute | solution.py:652
  30.4 43.4 %collective-permute-start.5 = (bf16[2,2,2,32,512]{4,3,2,1,0:T(8,128)(2,1)}, bf16[2,2,2,32,512]{4,3,2,1,0:T(8,128)(2,1)}, u32[]{:S(2)}, u32[]{:S(2)}) collective-permute-start(bf16[2,2,2,32,512]{4,3,2,1,0:T(8,128)(2,1)} %get-tuple-element.33), channel_id=1, source_target_pairs={{0,5},{1,6},{2,7},{3,0},{4,1},{5,2},{6,3},{7,4},{8,13},{9,14},{10,... | collective-permute-start | bytes 786440 | tf_op jit(solution)/shard_map/ppermute | solution.py:652
  33.0 40.7 %collective-permute-start.6 = (bf16[2,2,2,32,512]{4,3,2,1,0:T(8,128)(2,1)}, bf16[2,2,2,32,512]{4,3,2,1,0:T(8,128)(2,1)}, u32[]{:S(2)}, u32[]{:S(2)}) collective-permute-start(bf16[2,2,2,32,512]{4,3,2,1,0:T(8,128)(2,1)} %get-tuple-element.34), channel_id=1, source_target_pairs={{0,6},{1,7},{2,0},{3,1},{4,2},{5,3},{6,4},{7,5},{8,14},{9,15},{10,... | collective-permute-start | bytes 786440 | tf_op jit(solution)/shard_map/ppermute | solution.py:652
  36.0 37.7 %copy-start.1 = (bf16[2,2,2,32,512]{4,3,2,1,0:T(8,128)(2,1)}, bf16[2,2,2,32,512]{4,3,2,1,0:T(8,128)(2,1)S(1)}, u32[]{:S(2)}) copy-start(bf16[2,2,2,32,512]{4,3,2,1,0:T(8,128)(2,1)S(1)} %collective-permute-done.2.refs_0_) | copy-start | bytes 786436
  36.0 37.8 %collective-permute-start.7 = (bf16[2,2,2,32,512]{4,3,2,1,0:T(8,128)(2,1)}, bf16[2,2,2,32,512]{4,3,2,1,0:T(8,128)(2,1)}, u32[]{:S(2)}, u32[]{:S(2)}) collective-permute-start(bf16[2,2,2,32,512]{4,3,2,1,0:T(8,128)(2,1)} %get-tuple-element.35), channel_id=1, source_target_pairs={{0,1},{1,2},{2,3},{3,4},{4,5},{5,6},{6,7},{7,0},{8,9},{9,10},{10,1... | collective-permute-start | bytes 786440 | tf_op jit(solution)/shard_map/ppermute | solution.py:652
  56.4 17.3 %copy-start.2 = (bf16[2,2,2,32,512]{4,3,2,1,0:T(8,128)(2,1)}, bf16[2,2,2,32,512]{4,3,2,1,0:T(8,128)(2,1)S(1)}, u32[]{:S(2)}) copy-start(bf16[2,2,2,32,512]{4,3,2,1,0:T(8,128)(2,1)S(1)} %collective-permute-done.3.refs_1_) | copy-start | bytes 786436
  56.4 17.4 %collective-permute-start.8 = (bf16[2,2,2,32,512]{4,3,2,1,0:T(8,128)(2,1)}, bf16[2,2,2,32,512]{4,3,2,1,0:T(8,128)(2,1)}, u32[]{:S(2)}, u32[]{:S(2)}) collective-permute-start(bf16[2,2,2,32,512]{4,3,2,1,0:T(8,128)(2,1)} %get-tuple-element.36), channel_id=1, source_target_pairs={{0,7},{1,0},{2,1},{3,2},{4,3},{5,4},{6,5},{7,6},{8,15},{9,8},{10,9... | collective-permute-start | bytes 786440 | tf_op jit(solution)/shard_map/ppermute | solution.py:652
  73.7 0.7 copy-start.3
  86.1 50.3 %all-to-all-start = ((bf16[8,2,2,2,32,512]{5,4,3,2,1,0:T(8,128)(2,1)}), bf16[8,2,2,2,32,512]{5,4,3,2,1,0:T(8,128)(2,1)}, u32[]{:S(2)}, u32[]{:S(2)}) async-start(bf16[8,2,2,2,32,512]{5,4,3,2,1,0:T(8,128)(2,1)} %get-tuple-element.38), calls=%async_computation | async-start | bytes 4194304 | tf_op jit(solution)/shard_map/all_to_all | solution.py:661
  95.3 2.9 %collective-permute-start.9 = (bf16[1024,512]{1,0:T(8,128)(2,1)}, bf16[1024,512]{1,0:T(8,128)(2,1)S(1)}, u32[]{:S(2)}, u32[]{:S(2)}) collective-permute-start(bf16[1024,512]{1,0:T(8,128)(2,1)} %shard_map.123), channel_id=1, source_target_pairs={{0,8},{8,0},{16,24},{24,16},{1,9},{9,1},{17,25},{25,17},{2,10},{10... | collective-permute-start | bytes 3145736 | tf_op jit(solution)/shard_map/ppermute | solution.py:618
  99.7 25.3 %collective-permute-start.10 = (bf16[1024,512]{1,0:T(8,128)(2,1)S(1)}, bf16[1024,512]{1,0:T(8,128)(2,1)S(1)}, u32[]{:S(2)}, u32[]{:S(2)}) collective-permute-start(bf16[1024,512]{1,0:T(8,128)(2,1)S(1)} %add_convert_fusion), channel_id=1, source_target_pairs={{0,16},{8,24},{16,0},{24,8},{1,17},{9,25},{17,1},{25,9},{2,18},{10... | collective-permute-start | bytes 3145736 | tf_op jit(solution)/shard_map/ppermute | solution.py:618
  144.8 16.4 %all-to-all-start.1 = ((bf16[8,32,512]{2,1,0:T(8,128)(2,1)}), bf16[8,32,512]{2,1,0:T(8,128)(2,1)S(1)}, u32[]{:S(2)}, u32[]{:S(2)}) async-start(bf16[8,32,512]{2,1,0:T(8,128)(2,1)} %get-tuple-element.44), calls=%async_computation.1 | async-start | bytes 524288 | tf_op jit(solution)/shard_map/all_to_all | solution.py:665
  149.2 11.9 %copy-start = (bf16[3,8,4096]{2,1,0:T(8,128)(2,1)}, bf16[3,8,4096]{2,1,0:T(8,128)(2,1)S(1)}, u32[]{:S(2)}) copy-start(bf16[3,8,4096]{2,1,0:T(8,128)(2,1)S(1)} %get-tuple-element.56.own_ref) | copy-start | bytes 589828
  149.3 11.9 %collective-permute-start.11 = (bf16[3,8,4096]{2,1,0:T(8,128)(2,1)S(1)}, bf16[3,8,4096]{2,1,0:T(8,128)(2,1)S(1)}, u32[]{:S(2)}, u32[]{:S(2)}) collective-permute-start(bf16[3,8,4096]{2,1,0:T(8,128)(2,1)S(1)} %get-tuple-element.57), channel_id=1, source_target_pairs={{0,1},{1,0},{2,3},{3,2},{4,5},{5,4},{6,7},{7,6},{8,9},{9,8},{10,11... | collective-permute-start | bytes 589832 | tf_op jit(solution)/shard_map/ppermute | solution.py:640
  151.3 9.9 %collective-permute-start.12 = (bf16[3,8,4096]{2,1,0:T(8,128)(2,1)S(1)}, bf16[3,8,4096]{2,1,0:T(8,128)(2,1)}, u32[]{:S(2)}, u32[]{:S(2)}) collective-permute-start(bf16[3,8,4096]{2,1,0:T(8,128)(2,1)S(1)} %get-tuple-element.56.own_ref), channel_id=1, source_target_pairs={{1,2},{2,1},{3,4},{4,3},{5,6},{6,5},{9,10},{10,9},{11,12},{12,11},... | collective-permute-start | bytes 589832 | tf_op jit(solution)/shard_map/ppermute | solution.py:641
  161.2 3.0 %copy-start.4 = (bf16[3,8,4096]{2,1,0:T(8,128)(2,1)}, bf16[3,8,4096]{2,1,0:T(8,128)(2,1)S(1)}, u32[]{:S(2)}) copy-start(bf16[3,8,4096]{2,1,0:T(8,128)(2,1)S(1)} %collective-permute-done.11.inner_ref) | copy-start | bytes 589828
  161.3 1.3 collective-permute-start.13
  162.6 6.0 %collective-permute-start.14 = (f32[24,512]{1,0:T(8,128)S(1)}, f32[24,512]{1,0:T(8,128)S(1)}, u32[]{:S(2)}, u32[]{:S(2)}) collective-permute-start(f32[24,512]{1,0:T(8,128)S(1)} %slice_add_fusion), channel_id=1, source_target_pairs={{0,16},{8,24},{16,0},{24,8},{1,17},{9,25},{17,1},{25,9},{2,18},{10... | collective-permute-start | bytes 147464 | tf_op jit(solution)/shard_map/ppermute | solution.py:618

commit v6 on v5

--- a/solution.py
+++ b/solution.py
@@ -173,32 +173,56 @@
     return tuple(out)
 
 
-def filter_kernel(h_ref, table_ref, out_ref, turn_ref):
-    segments, _, half, width = out_ref.shape
+def filter_kernel(tile, h_hbm, table_ref, out_hbm, out_buf, turn_ref, seq_ref, load_sem, store_sem):
+    segments, _, half, width = out_buf.shape
     lanes = turn_ref.shape[-1]
     size = 2 * half
-    for part in range(width // lanes):
-        cols = slice(part * lanes, (part + 1) * lanes)
-        turn_ref[part] = h_ref[:, cols]
-        first = first_row((half, lanes))
+    steps = half // tile
+    parts = [slice(part * lanes, (part + 1) * lanes) for part in range(width // lanes)]
+    loads = [pltpu.make_async_copy(h_hbm.at[:, cols], turn_ref.at[i], load_sem.at[i]) for i, cols in enumerate(parts)]
+
+    def store(step):
+        at = slice(step * tile, (step + 1) * tile)
+        return pltpu.make_async_copy(out_buf.at[:, :, at], out_hbm.at[:, :, at], store_sem.at[step])
+
+    for copy in loads:
+        copy.start()
+    for i, cols in enumerate(parts):
+        loads[i].wait()
+        for e in range(2):
+            seq_ref[e, :, cols] = turn_ref[i, pl.ds(e, segments * half, stride=2)].astype(BF)
+    for step in range(steps):
+        at = slice(step * tile, (step + 1) * tile)
+        up = slice(half + step * tile, half + (step + 1) * tile)
+        first = first_row((tile, width)) if step == 0 else None
         for s in range(segments):
-            parts = []
-            for e in range(2):
-                time = turn_ref[part, pl.ds(s * size + e, half, stride=2)]
-                made = dot(table_ref[e], time.astype(BF)) * (1.0 / size)
-                parts.append((made[:half], made[half:]))
-            for i, value in enumerate(unite(*parts, first)):
-                out_ref[s, i, :, cols] = value
+            span = slice(s * half, (s + 1) * half)
+            made = [(dot(table_ref[e, at], seq_ref[e, span]), dot(table_ref[e, up], seq_ref[e, span])) for e in range(2)]
+            for k, value in enumerate(unite(*made, first)):
+                out_buf[s, k, at] = value * (1.0 / size)
+        store(step).start()
+    for step in range(steps):
+        store(step).wait()
 
 
 def filter_spectrum(h, table):
     size = table.shape[1]
     rows, width = h.shape
     lanes = min(128, width)
+    shape = (rows // size, 4, size // 2, width)
+    tile = min(128, size // 2)
     return pl.pallas_call(
-        filter_kernel,
-        out_shape=jax.ShapeDtypeStruct((rows // size, 4, size // 2, width), F32),
-        scratch_shapes=[pltpu.VMEM((width // lanes, rows, lanes), F32)],
+        functools.partial(filter_kernel, tile),
+        in_specs=[ANYWHERE, VECTOR],
+        out_specs=ANYWHERE,
+        out_shape=jax.ShapeDtypeStruct(shape, F32),
+        scratch_shapes=[
+            pltpu.VMEM(shape, F32),
+            pltpu.VMEM((width // lanes, rows, lanes), F32),
+            pltpu.VMEM((2, rows // 2, width), BF),
+            pltpu.SemaphoreType.DMA((width // lanes,)),
+            pltpu.SemaphoreType.DMA((size // 2 // tile,)),
+        ],
         compiler_params=PARAMS,
     )(h, table)
 

time: 170 us -> 170 us (level)
  no operation moved by 1% of the time
where the time goes in v6:
time: 170 us; the launch traced here: 169 us
  waiting for transfers between devices  65.6 us (39%)
  Pallas kernels  51.1 us (30%)
  starting transfers between devices  40.1 us (24%)
  other arithmetic  9.31 us (5%)
    ppermute x4, waiting for transfers between devices, sum_over_dp(): lax.ppermute(sent, 'dp', [(j, j ^ hop) for j in range(lax.axis_size('dp'))])  27.9 us
    ppermute x7, starting transfers between devices, on_device(): lax.ppermute(sent, 'ctx', [(j, (j + s) % n) for j in range(n)])  22 us
    ppermute x7, waiting for transfers between devices, on_device(): lax.ppermute(sent, 'ctx', [(j, (j + s) % n) for j in range(n)])  20.4 us
    pallas_call x1, Pallas kernels, long_conv(): pl.pallas_call(functools.partial(long_kernel, min(256, freqs), n), in_spe...  11.7 us
    all_to_all x1, waiting for transfers between devices, on_device(): returned = lax.all_to_all(out, 'ctx', 0, 0, tiled=True)  10.8 us
    pallas_call x1, Pallas kernels, finish(): pl.pallas_call(functools.partial(finish_kernel, tap_count), in_specs=[ANY...  8.48 us
    pallas_call x1, Pallas kernels, tap_grads(): pl.pallas_call(functools.partial(tap_kernel, tap_count), in_specs=[ANYWHE...  8.32 us
    pallas_call x1, Pallas kernels, featurize(): pl.pallas_call(functools.partial(featurize_kernel, tap_count, pieces), in...  7.96 us
  transfers between devices with their start and end apart: 17, of which 7 were waited for; matrix products, arithmetic and copies ran while one was open for 4% of the time, Pallas kernels for 14%

profile of v6, /device:TPU:0, one launch (start us, length us, event | category | flops | bytes accessed | tf_op | source)
XLA Modules:
  0.0 169.1 jit_solution(707709836326663408)
XLA Ops:
  0.6 1.3 fusion.3
  3.7 3.0 %collective-permute-start = (bf16[3,8,4096]{2,1,0:T(8,128)(2,1)S(1)}, bf16[3,8,4096]{2,1,0:T(8,128)(2,1)S(1)}, u32[]{:S(2)}, u32[]{:S(2)}) collective-permute-start(bf16[3,8,4096]{2,1,0:T(8,128)(2,1)S(1)} %get-tuple-element.53), channel_id=1, source_target_pairs={{0,1},{1,0},{2,3},{3,2},{4,5},{5,4},{6,7},{7,6},{8,9},{9,8},{10,11... | collective-permute-start | bytes 589832 | tf_op jit(solution)/shard_map/ppermute | solution.py:664
  7.4 1.2 and_select_fusion
  8.6 6.5 %collective-permute-done = bf16[3,8,4096]{2,1,0:T(8,128)(2,1)S(1)} collective-permute-done((bf16[3,8,4096]{2,1,0:T(8,128)(2,1)S(1)}, bf16[3,8,4096]{2,1,0:T(8,128)(2,1)S(1)}, u32[]{:S(2)}, u32[]{:S(2)}) %collective-permute-start) | collective-permute-done | bytes 196640 | tf_op jit(solution)/shard_map/ppermute | solution.py:664
  15.9 8.0 %shard_map.120 = (bf16[2,2,2,32,512]{4,3,2,1,0:T(8,128)(2,1)}, bf16[2,2,2,32,512]{4,3,2,1,0:T(8,128)(2,1)}, bf16[2,2,2,32,512]{4,3,2,1,0:T(8,128)(2,1)}, bf16[2,...) custom-call(s32[8]{0:T(128)} %get-tuple-element.58.where_ref, ...), custom_call_target="tpu_custom_call" | custom-call | tf_op jit(solution)/shard_map/pallas_call | solution.py:117
  23.8 2.6 %collective-permute-start.2 = (bf16[2,2,2,32,512]{4,3,2,1,0:T(8,128)(2,1)}, bf16[2,2,2,32,512]{4,3,2,1,0:T(8,128)(2,1)S(1)}, u32[]{:S(2)}, u32[]{:S(2)}) collective-permute-start(bf16[2,2,2,32,512]{4,3,2,1,0:T(8,128)(2,1)} %get-tuple-element.30), channel_id=1, source_target_pairs={{0,2},{1,3},{2,4},{3,5},{4,6},{5,7},{6,0},{7,1},{8,10},{9,11},{10,... | collective-permute-start | bytes 786440 | tf_op jit(solution)/shard_map/ppermute | solution.py:676
  26.4 2.7 %collective-permute-start.3 = (bf16[2,2,2,32,512]{4,3,2,1,0:T(8,128)(2,1)}, bf16[2,2,2,32,512]{4,3,2,1,0:T(8,128)(2,1)S(1)}, u32[]{:S(2)}, u32[]{:S(2)}) collective-permute-start(bf16[2,2,2,32,512]{4,3,2,1,0:T(8,128)(2,1)} %get-tuple-element.31), channel_id=1, source_target_pairs={{0,4},{1,5},{2,6},{3,7},{4,0},{5,1},{6,2},{7,3},{8,12},{9,13},{10,... | collective-permute-start | bytes 786440 | tf_op jit(solution)/shard_map/ppermute | solution.py:676
  29.2 1.1 collective-permute-start.4
  30.4 2.7 %collective-permute-start.5 = (bf16[2,2,2,32,512]{4,3,2,1,0:T(8,128)(2,1)}, bf16[2,2,2,32,512]{4,3,2,1,0:T(8,128)(2,1)}, u32[]{:S(2)}, u32[]{:S(2)}) collective-permute-start(bf16[2,2,2,32,512]{4,3,2,1,0:T(8,128)(2,1)} %get-tuple-element.33), channel_id=1, source_target_pairs={{0,5},{1,6},{2,7},{3,0},{4,1},{5,2},{6,3},{7,4},{8,13},{9,14},{10,... | collective-permute-start | bytes 786440 | tf_op jit(solution)/shard_map/ppermute | solution.py:676
  33.0 1.3 collective-permute-start.6
  34.4 1.6 collective-permute-done.2.refs_0_
  36.0 1.7 %collective-permute-start.7 = (bf16[2,2,2,32,512]{4,3,2,1,0:T(8,128)(2,1)}, bf16[2,2,2,32,512]{4,3,2,1,0:T(8,128)(2,1)}, u32[]{:S(2)}, u32[]{:S(2)}) collective-permute-start(bf16[2,2,2,32,512]{4,3,2,1,0:T(8,128)(2,1)} %get-tuple-element.35), channel_id=1, source_target_pairs={{0,1},{1,2},{2,3},{3,4},{4,5},{5,6},{6,7},{7,0},{8,9},{9,10},{10,1... | collective-permute-start | bytes 786440 | tf_op jit(solution)/shard_map/ppermute | solution.py:676
  37.7 18.7 %collective-permute-done.3.refs_1_ = bf16[2,2,2,32,512]{4,3,2,1,0:T(8,128)(2,1)S(1)} collective-permute-done((bf16[2,2,2,32,512]{4,3,2,1,0:T(8,128)(2,1)}, bf16[2,2,2,32,512]{4,3,2,1,0:T(8,128)(2,1)S(1)}, u32[]{:S(2)}, u32[]{:S(2)}) %collective-permute-start.3) | collective-permute-done | bytes 262176 | tf_op jit(solution)/shard_map/ppermute | solution.py:676
  56.4 10.0 %collective-permute-start.8 = (bf16[2,2,2,32,512]{4,3,2,1,0:T(8,128)(2,1)}, bf16[2,2,2,32,512]{4,3,2,1,0:T(8,128)(2,1)}, u32[]{:S(2)}, u32[]{:S(2)}) collective-permute-start(bf16[2,2,2,32,512]{4,3,2,1,0:T(8,128)(2,1)} %get-tuple-element.36), channel_id=1, source_target_pairs={{0,7},{1,0},{2,1},{3,2},{4,3},{5,4},{6,5},{7,6},{8,15},{9,8},{10,9... | collective-permute-start | bytes 786440 | tf_op jit(solution)/shard_map/ppermute | solution.py:676
  67.1 5.6 %shard_map.121.filt_hbm = f32[1,4,512,512]{3,2,1,0:T(8,128)} custom-call(f32[1024,512]{1,0:T(8,128)} %h_hbm, bf16[2,1024,512]{2,1,0:T(8,128)(2,1)} %constant.58.clone.table_ref.table_hbm), custom_call_target="tpu_custom_call" | custom-call | tf_op jit(solution)/shard_map/pallas_call | solution.py:214
  73.5 11.7 %shard_map.122 = (bf16[8,2,2,2,32,512]{5,4,3,2,1,0:T(8,128)(2,1)}, bf16[1,2,1024,512]{3,2,1,0:T(8,128)(2,1)}) custom-call(s32[16]{0:T(128)} %select_reduce_fusion.from_ref, s32[16]{0:T(128)} %order_ref.1, f32[1,4,512,512]{3,2,1,0:T(8,128)} %shard_map.121.filt_hbm, bf16[2,1024,512]{2,1,0:T(8,128)(2,1)} %constant.58.clone.table_ref.table_hbm, ...), custom_call_target="tpu_custom_call" | custom-call | tf_op jit(solution)/shard_map/pallas_call | solution.py:343
  85.2 4.6 %all-to-all-start = ((bf16[8,2,2,2,32,512]{5,4,3,2,1,0:T(8,128)(2,1)}), bf16[8,2,2,2,32,512]{5,4,3,2,1,0:T(8,128)(2,1)}, u32[]{:S(2)}, u32[]{:S(2)}) async-start(bf16[8,2,2,2,32,512]{5,4,3,2,1,0:T(8,128)(2,1)} %get-tuple-element.38), calls=%async_computation | async-start | bytes 4194304 | tf_op jit(solution)/shard_map/all_to_all | solution.py:685
  89.7 4.6 %shard_map.123 = bf16[1024,512]{1,0:T(8,128)(2,1)} custom-call(bf16[1,2,1024,512]{3,2,1,0:T(8,128)(2,1)} %get-tuple-element.39.cross_ref, bf16[2,512,1024]{2,1,0:T(8,128)(2,1)} %constant.59.clone.back_hbm.back_ref), custom_call_target="tpu_custom_call" | custom-call | tf_op jit(solution)/shard_map/pallas_call | solution.py:384
  94.3 2.9 %collective-permute-done.9 = bf16[1024,512]{1,0:T(8,128)(2,1)S(1)} collective-permute-done((bf16[1024,512]{1,0:T(8,128)(2,1)}, bf16[1024,512]{1,0:T(8,128)(2,1)S(1)}, u32[]{:S(2)}, u32[]{:S(2)}) %collective-permute-start.9) | collective-permute-done | bytes 1048608 | tf_op jit(solution)/shard_map/ppermute | solution.py:642
  97.2 1.5 add_convert_fusion
  98.7 1.4 collective-permute-start.10
  100.1 23.9 %collective-permute-done.10 = bf16[1024,512]{1,0:T(8,128)(2,1)S(1)} collective-permute-done((bf16[1024,512]{1,0:T(8,128)(2,1)S(1)}, bf16[1024,512]{1,0:T(8,128)(2,1)S(1)}, u32[]{:S(2)}, u32[]{:S(2)}) %collective-permute-start.10) | collective-permute-done | bytes 1048608 | tf_op jit(solution)/shard_map/ppermute | solution.py:642
  124.0 1.6 convert_add_fusion
  125.6 10.8 %all-to-all-done.recv_hbm = bf16[8,2,2,2,32,512]{5,4,3,2,1,0:T(8,128)(2,1)} async-done(((bf16[8,2,2,2,32,512]{5,4,3,2,1,0:T(8,128)(2,1)}), bf16[8,2,2,2,32,512]{5,4,3,2,1,0:T(8,128)(2,1)}, u32[]{:S(2)}, u32[]{:S(2)}) %all-to-all-start) | async-done | bytes 2097184 | tf_op jit(solution)/shard_map/all_to_all | solution.py:685
  136.4 8.3 %shard_map.125 = (bf16[8,32,512]{2,1,0:T(8,128)(2,1)}, bf16[3,16,4096]{2,1,0:T(8,128)(2,1)}) custom-call(bf16[8,2,2,2,32,512]{5,4,3,2,1,0:T(8,128)(2,1)} %all-to-all-done.recv_hbm, bf16[3,128,4096]{2,1,0:T(8,128)(2,1)} %get-tuple-element.41.qkv_hbm, bf16[3,128,4096]{2,1,0:T(8,128)(2,1)} %bitcast.11, bf16[128,4096]{1,0:T(8,128)(2,1)} %bitcast.13, ...), custom_call_target="tpu_custom_call" | custom-call | tf_op jit(solution)/shard_map/pallas_call | solution.py:459
  144.7 3.4 %all-to-all-start.1 = ((bf16[8,32,512]{2,1,0:T(8,128)(2,1)}), bf16[8,32,512]{2,1,0:T(8,128)(2,1)S(1)}, u32[]{:S(2)}, u32[]{:S(2)}) async-start(bf16[8,32,512]{2,1,0:T(8,128)(2,1)} %get-tuple-element.44), calls=%async_computation.1 | async-start | bytes 524288 | tf_op jit(solution)/shard_map/all_to_all | solution.py:689
  149.2 2.1 %collective-permute-start.11 = (bf16[3,8,4096]{2,1,0:T(8,128)(2,1)S(1)}, bf16[3,8,4096]{2,1,0:T(8,128)(2,1)S(1)}, u32[]{:S(2)}, u32[]{:S(2)}) collective-permute-start(bf16[3,8,4096]{2,1,0:T(8,128)(2,1)S(1)} %get-tuple-element.57), channel_id=1, source_target_pairs={{0,1},{1,0},{2,3},{3,2},{4,5},{5,4},{6,7},{7,6},{8,9},{9,8},{10,11... | collective-permute-start | bytes 589832 | tf_op jit(solution)/shard_map/ppermute | solution.py:664
  151.3 1.3 collective-permute-start.12
  152.6 8.5 %shard_map.124 = (bf16[128,4096]{1,0:T(8,128)(2,1)}, bf16[3,128,4096]{2,1,0:T(8,128)(2,1)}, f32[3,16,4096]{2,1,0:T(8,128)}) custom-call(bf16[8,2,2,2,32,512]{5,4,3,2,1,0:T(8,128)(2,1)} %all-to-all-done.recv_hbm, bf16[3,128,4096]{2,1,0:T(8,128)(2,1)} %get-tuple-element.41.qkv_hbm, bf16[128,4096]{1,0:T(8,128)(2,1)} %bitcast.14, f32[3,7,4096]{2,1,0:T(8,128)} %bitcast.16), custom_call_target="tpu_custom_call" | custom-call | tf_op jit(solution)/shard_map/pallas_call | solution.py:546
  161.3 1.2 collective-permute-done.13
  162.5 1.6 collective-permute-start.14
  164.1 4.4 %shard_map.126 = bf16[3,128,4096]{2,1,0:T(8,128)(2,1)} custom-call(s32[16]{0:T(128)} %order_ref.1, bf16[3,128,4096]{2,1,0:T(8,128)(2,1)} %get-tuple-element.43.old_hbm, f32[3,16,4096]{2,1,0:T(8,128)} %get-tuple-element.47.open_ref, bf16[3,8,4096]{2,1,0:T(8,128)(2,1)} %copy-done.4, ...), custom_call_target="tpu_custom_call", output_to_operand_aliasing={{}: (1, {})} | custom-call | tf_op jit(solution)/shard_map/pallas_call | solution.py:620
  (38 shorter events, 5.9 us)
Async XLA Ops:
  3.7 11.4 %collective-permute-start = (bf16[3,8,4096]{2,1,0:T(8,128)(2,1)S(1)}, bf16[3,8,4096]{2,1,0:T(8,128)(2,1)S(1)}, u32[]{:S(2)}, u32[]{:S(2)}) collective-permute-start(bf16[3,8,4096]{2,1,0:T(8,128)(2,1)S(1)} %get-tuple-element.53), channel_id=1, source_target_pairs={{0,1},{1,0},{2,3},{3,2},{4,5},{5,4},{6,7},{7,6},{8,9},{9,8},{10,11... | collective-permute-start | bytes 589832 | tf_op jit(solution)/shard_map/ppermute | solution.py:664
  6.7 8.4 %collective-permute-start.1 = (bf16[3,8,4096]{2,1,0:T(8,128)(2,1)S(1)}, bf16[3,8,4096]{2,1,0:T(8,128)(2,1)S(1)}, u32[]{:S(2)}, u32[]{:S(2)}) collective-permute-start(bf16[3,8,4096]{2,1,0:T(8,128)(2,1)S(1)} %get-tuple-element.52), channel_id=1, source_target_pairs={{1,2},{2,1},{3,4},{4,3},{5,6},{6,5},{9,10},{10,9},{11,12},{12,11},... | collective-permute-start | bytes 589832 | tf_op jit(solution)/shard_map/ppermute | solution.py:665
  15.9 50.5 %copy-start.5 = (s32[16]{0:T(128)S(1)}, s32[16]{0:T(128)}, u32[]{:S(2)}) copy-start(s32[16]{0:T(128)} %order_ref.1) | copy-start | bytes 196
  23.8 12.1 %collective-permute-start.2 = (bf16[2,2,2,32,512]{4,3,2,1,0:T(8,128)(2,1)}, bf16[2,2,2,32,512]{4,3,2,1,0:T(8,128)(2,1)S(1)}, u32[]{:S(2)}, u32[]{:S(2)}) collective-permute-start(bf16[2,2,2,32,512]{4,3,2,1,0:T(8,128)(2,1)} %get-tuple-element.30), channel_id=1, source_target_pairs={{0,2},{1,3},{2,4},{3,5},{4,6},{5,7},{6,0},{7,1},{8,10},{9,11},{10,... | collective-permute-start | bytes 786440 | tf_op jit(solution)/shard_map/ppermute | solution.py:676
  26.4 30.0 %collective-permute-start.3 = (bf16[2,2,2,32,512]{4,3,2,1,0:T(8,128)(2,1)}, bf16[2,2,2,32,512]{4,3,2,1,0:T(8,128)(2,1)S(1)}, u32[]{:S(2)}, u32[]{:S(2)}) collective-permute-start(bf16[2,2,2,32,512]{4,3,2,1,0:T(8,128)(2,1)} %get-tuple-element.31), channel_id=1, source_target_pairs={{0,4},{1,5},{2,6},{3,7},{4,0},{5,1},{6,2},{7,3},{8,12},{9,13},{10,... | collective-permute-start | bytes 786440 | tf_op jit(solution)/shard_map/ppermute | solution.py:676
  29.2 43.5 %collective-permute-start.4 = (bf16[2,2,2,32,512]{4,3,2,1,0:T(8,128)(2,1)}, bf16[2,2,2,32,512]{4,3,2,1,0:T(8,128)(2,1)S(1)}, u32[]{:S(2)}, u32[]{:S(2)}) collective-permute-start(bf16[2,2,2,32,512]{4,3,2,1,0:T(8,128)(2,1)} %get-tuple-element.32), channel_id=1, source_target_pairs={{0,3},{1,4},{2,5},{3,6},{4,7},{5,0},{6,1},{7,2},{8,11},{9,12},{10,... | collective-permute-start | bytes 786440 | tf_op jit(solution)/shard_map/ppermute | solution.py:676
  30.4 42.4 %collective-permute-start.5 = (bf16[2,2,2,32,512]{4,3,2,1,0:T(8,128)(2,1)}, bf16[2,2,2,32,512]{4,3,2,1,0:T(8,128)(2,1)}, u32[]{:S(2)}, u32[]{:S(2)}) collective-permute-start(bf16[2,2,2,32,512]{4,3,2,1,0:T(8,128)(2,1)} %get-tuple-element.33), channel_id=1, source_target_pairs={{0,5},{1,6},{2,7},{3,0},{4,1},{5,2},{6,3},{7,4},{8,13},{9,14},{10,... | collective-permute-start | bytes 786440 | tf_op jit(solution)/shard_map/ppermute | solution.py:676
  33.0 39.7 %collective-permute-start.6 = (bf16[2,2,2,32,512]{4,3,2,1,0:T(8,128)(2,1)}, bf16[2,2,2,32,512]{4,3,2,1,0:T(8,128)(2,1)}, u32[]{:S(2)}, u32[]{:S(2)}) collective-permute-start(bf16[2,2,2,32,512]{4,3,2,1,0:T(8,128)(2,1)} %get-tuple-element.34), channel_id=1, source_target_pairs={{0,6},{1,7},{2,0},{3,1},{4,2},{5,3},{6,4},{7,5},{8,14},{9,15},{10,... | collective-permute-start | bytes 786440 | tf_op jit(solution)/shard_map/ppermute | solution.py:676
  36.0 36.7 %copy-start.1 = (bf16[2,2,2,32,512]{4,3,2,1,0:T(8,128)(2,1)}, bf16[2,2,2,32,512]{4,3,2,1,0:T(8,128)(2,1)S(1)}, u32[]{:S(2)}) copy-start(bf16[2,2,2,32,512]{4,3,2,1,0:T(8,128)(2,1)S(1)} %collective-permute-done.2.refs_0_) | copy-start | bytes 786436
  36.0 36.8 %collective-permute-start.7 = (bf16[2,2,2,32,512]{4,3,2,1,0:T(8,128)(2,1)}, bf16[2,2,2,32,512]{4,3,2,1,0:T(8,128)(2,1)}, u32[]{:S(2)}, u32[]{:S(2)}) collective-permute-start(bf16[2,2,2,32,512]{4,3,2,1,0:T(8,128)(2,1)} %get-tuple-element.35), channel_id=1, source_target_pairs={{0,1},{1,2},{2,3},{3,4},{4,5},{5,6},{6,7},{7,0},{8,9},{9,10},{10,1... | collective-permute-start | bytes 786440 | tf_op jit(solution)/shard_map/ppermute | solution.py:676
  56.4 16.3 %copy-start.2 = (bf16[2,2,2,32,512]{4,3,2,1,0:T(8,128)(2,1)}, bf16[2,2,2,32,512]{4,3,2,1,0:T(8,128)(2,1)S(1)}, u32[]{:S(2)}) copy-start(bf16[2,2,2,32,512]{4,3,2,1,0:T(8,128)(2,1)S(1)} %collective-permute-done.3.refs_1_) | copy-start | bytes 786436
  56.4 16.4 %collective-permute-start.8 = (bf16[2,2,2,32,512]{4,3,2,1,0:T(8,128)(2,1)}, bf16[2,2,2,32,512]{4,3,2,1,0:T(8,128)(2,1)}, u32[]{:S(2)}, u32[]{:S(2)}) collective-permute-start(bf16[2,2,2,32,512]{4,3,2,1,0:T(8,128)(2,1)} %get-tuple-element.36), channel_id=1, source_target_pairs={{0,7},{1,0},{2,1},{3,2},{4,3},{5,4},{6,5},{7,6},{8,15},{9,8},{10,9... | collective-permute-start | bytes 786440 | tf_op jit(solution)/shard_map/ppermute | solution.py:676
  72.8 0.7 copy-start.3
  85.2 51.2 %all-to-all-start = ((bf16[8,2,2,2,32,512]{5,4,3,2,1,0:T(8,128)(2,1)}), bf16[8,2,2,2,32,512]{5,4,3,2,1,0:T(8,128)(2,1)}, u32[]{:S(2)}, u32[]{:S(2)}) async-start(bf16[8,2,2,2,32,512]{5,4,3,2,1,0:T(8,128)(2,1)} %get-tuple-element.38), calls=%async_computation | async-start | bytes 4194304 | tf_op jit(solution)/shard_map/all_to_all | solution.py:685
  94.3 2.9 %collective-permute-start.9 = (bf16[1024,512]{1,0:T(8,128)(2,1)}, bf16[1024,512]{1,0:T(8,128)(2,1)S(1)}, u32[]{:S(2)}, u32[]{:S(2)}) collective-permute-start(bf16[1024,512]{1,0:T(8,128)(2,1)} %shard_map.123), channel_id=1, source_target_pairs={{0,8},{8,0},{16,24},{24,16},{1,9},{9,1},{17,25},{25,17},{2,10},{10... | collective-permute-start | bytes 3145736 | tf_op jit(solution)/shard_map/ppermute | solution.py:642
  98.7 25.3 %collective-permute-start.10 = (bf16[1024,512]{1,0:T(8,128)(2,1)S(1)}, bf16[1024,512]{1,0:T(8,128)(2,1)S(1)}, u32[]{:S(2)}, u32[]{:S(2)}) collective-permute-start(bf16[1024,512]{1,0:T(8,128)(2,1)S(1)} %add_convert_fusion), channel_id=1, source_target_pairs={{0,16},{8,24},{16,0},{24,8},{1,17},{9,25},{17,1},{25,9},{2,18},{10... | collective-permute-start | bytes 3145736 | tf_op jit(solution)/shard_map/ppermute | solution.py:642
  144.7 16.4 %all-to-all-start.1 = ((bf16[8,32,512]{2,1,0:T(8,128)(2,1)}), bf16[8,32,512]{2,1,0:T(8,128)(2,1)S(1)}, u32[]{:S(2)}, u32[]{:S(2)}) async-start(bf16[8,32,512]{2,1,0:T(8,128)(2,1)} %get-tuple-element.44), calls=%async_computation.1 | async-start | bytes 524288 | tf_op jit(solution)/shard_map/all_to_all | solution.py:689
  149.2 11.9 %copy-start = (bf16[3,8,4096]{2,1,0:T(8,128)(2,1)}, bf16[3,8,4096]{2,1,0:T(8,128)(2,1)S(1)}, u32[]{:S(2)}) copy-start(bf16[3,8,4096]{2,1,0:T(8,128)(2,1)S(1)} %get-tuple-element.56.own_ref) | copy-start | bytes 589828
  149.2 11.9 %collective-permute-start.11 = (bf16[3,8,4096]{2,1,0:T(8,128)(2,1)S(1)}, bf16[3,8,4096]{2,1,0:T(8,128)(2,1)S(1)}, u32[]{:S(2)}, u32[]{:S(2)}) collective-permute-start(bf16[3,8,4096]{2,1,0:T(8,128)(2,1)S(1)} %get-tuple-element.57), channel_id=1, source_target_pairs={{0,1},{1,0},{2,3},{3,2},{4,5},{5,4},{6,7},{7,6},{8,9},{9,8},{10,11... | collective-permute-start | bytes 589832 | tf_op jit(solution)/shard_map/ppermute | solution.py:664
  151.3 9.9 %collective-permute-start.12 = (bf16[3,8,4096]{2,1,0:T(8,128)(2,1)S(1)}, bf16[3,8,4096]{2,1,0:T(8,128)(2,1)}, u32[]{:S(2)}, u32[]{:S(2)}) collective-permute-start(bf16[3,8,4096]{2,1,0:T(8,128)(2,1)S(1)} %get-tuple-element.56.own_ref), channel_id=1, source_target_pairs={{1,2},{2,1},{3,4},{4,3},{5,6},{6,5},{9,10},{10,9},{11,12},{12,11},... | collective-permute-start | bytes 589832 | tf_op jit(solution)/shard_map/ppermute | solution.py:665
  161.1 3.0 %copy-start.4 = (bf16[3,8,4096]{2,1,0:T(8,128)(2,1)}, bf16[3,8,4096]{2,1,0:T(8,128)(2,1)S(1)}, u32[]{:S(2)}) copy-start(bf16[3,8,4096]{2,1,0:T(8,128)(2,1)S(1)} %collective-permute-done.11.inner_ref) | copy-start | bytes 589828
  161.2 1.3 collective-permute-start.13
  162.5 6.0 %collective-permute-start.14 = (f32[24,512]{1,0:T(8,128)S(1)}, f32[24,512]{1,0:T(8,128)S(1)}, u32[]{:S(2)}, u32[]{:S(2)}) collective-permute-start(f32[24,512]{1,0:T(8,128)S(1)} %slice_add_fusion), channel_id=1, source_target_pairs={{0,16},{8,24},{16,0},{24,8},{1,17},{9,25},{17,1},{25,9},{2,18},{10... | collective-permute-start | bytes 147464 | tf_op jit(solution)/shard_map/ppermute | solution.py:642
